TPU v7x, 32 devices: a whole 2x2x4 slice. The times are simulated.
32 devices in a mesh: head: 4 (over y, x), blk: 8 (over z, core).
Axes of the slice: x: 2, y: 2, z: 4, core: 2. Of those that a mesh axis runs over, the one named last changes fastest.
Arguments:
- stream: bfloat16 [2, 32, 128, 512], P(None, ('head', 'blk')), may hold values from -6 to 6
- accumulator: bfloat16 [2, 32, 128, 512], P(None, ('head', 'blk')), may hold values from -12 to 12
- upstream: bfloat16 [2, 32, 128, 512], P(None, ('head', 'blk')), may hold values from -6 to 6
- segment_ids: int32 [2, 32, 128], P(None, ('head', 'blk')), may hold values from 0 to 3, as said below
- w_query: bfloat16 [512, 512], P(('head', 'blk')), may hold values from -0.5 to 0.5
- w_key: bfloat16 [512, 512], P(('head', 'blk')), may hold values from -0.25 to 0.25
- w_value: bfloat16 [512, 512], P(('head', 'blk')), may hold values from -0.25 to 0.25
- w_out: bfloat16 [512, 512], P(('head', 'blk')), may hold values from -1 to 1
- w_up: bfloat16 [512, 2048], P(('head', 'blk')), may hold values from -0.25 to 0.25
- b_up: bfloat16 [2048], P(('head', 'blk')), may hold values from -1.796875 to 1.796875
- w_down: bfloat16 [2048, 512], P(('head', 'blk')), may hold values from -0.125 to 0.125
- b_down: bfloat16 [512], P(('head', 'blk')), may hold values from -1.796875 to 1.796875
- gain_attn: bfloat16 [512], P(('head', 'blk')), may hold values from 0.5 to 1.5
- bias_attn: bfloat16 [512], P(('head', 'blk')), may hold values from -1.796875 to 1.796875
- gain_ffn: bfloat16 [512], P(('head', 'blk')), may hold values from 0.5 to 1.5
- bias_ffn: bfloat16 [512], P(('head', 'blk')), may hold values from -1.796875 to 1.796875
- gain_final: bfloat16 [512], P(('head', 'blk')), may hold values from 0.5 to 1.5
- bias_final: bfloat16 [512], P(('head', 'blk')), may hold values from -1.796875 to 1.796875
Outputs:
- layer_out: bfloat16 [2, 32, 128, 512], P(None, ('head', 'blk'))
- grad_stream: float32 [2, 32, 128, 512], P(None, ('head', 'blk'))
- grad_accum: float32 [2, 32, 128, 512], P(None, ('head', 'blk'))
- grad_w_query: float32 [512, 512], P(('head', 'blk'))
- grad_w_key: float32 [512, 512], P(('head', 'blk'))
- grad_w_value: float32 [512, 512], P(('head', 'blk'))
- grad_w_out: float32 [512, 512], P(('head', 'blk'))
- grad_w_up: float32 [512, 2048], P(('head', 'blk'))
- grad_b_up: float32 [2048], P(('head', 'blk'))
- grad_w_down: float32 [2048, 512], P(('head', 'blk'))
- grad_b_down: float32 [512], P(('head', 'blk'))
- grad_gain_attn: float32 [512], P(('head', 'blk'))
- grad_bias_attn: float32 [512], P(('head', 'blk'))
- grad_gain_ffn: float32 [512], P(('head', 'blk'))
- grad_bias_ffn: float32 [512], P(('head', 'blk'))
- grad_gain_final: float32 [512], P(('head', 'blk'))
- grad_bias_final: float32 [512], P(('head', 'blk'))
Inputs may be any that keep to these rules, and one draw needn't show every extreme that they name: `segment_ids`: entry [m, d, c] belongs to position c * 32 + d of sequence m. Along a sequence's positions the numbers start at 0 and never fall, rising by one at each new document; every sequence holds exactly (3546) // 1100 + 1 documents; each document is a run of consecutive positions, the first one of at least 825, each but the last of at most 1650.
All inputs are finite; a program needn't handle non-finite values.
Results may differ from a plain program's by a relative error of at most 0.015.
The roundings to bfloat16 on the way count: a program that leaves them out, or rounds other values in their place, can miss the bound.
Values may be sent and summed in bfloat16 or wider, within the bound.
A program may use at most 256 MiB of HBM per device.

v0:
```python
import math

import jax
import jax.numpy as jnp
from jax import lax
from jax.sharding import PartitionSpec as P

DH = 64


EPSILON = 1e-05


def norm_forward(inputs, norm_gain, norm_bias):
    average = jnp.mean(inputs, axis=-1, keepdims=True)
    centered = inputs - average
    inv_std = lax.rsqrt(jnp.mean(centered * centered, axis=-1, keepdims=True) + EPSILON)
    normed = centered * inv_std
    return (normed * norm_gain + norm_bias, normed, inv_std)


def norm_backward(gradient, normed, inv_std, norm_gain):
    scaled = gradient * norm_gain
    projected = (
        scaled
        - jnp.mean(scaled, axis=-1, keepdims=True)
        - normed * jnp.mean(scaled * normed, axis=-1, keepdims=True)
    )
    return (inv_std * projected, jnp.sum(gradient * normed, axis=0), jnp.sum(gradient, axis=0))


def smooth_gate(pre_act):
    return jax.nn.gelu(pre_act, approximate=False)


def split_rows(length):
    block_len = math.gcd(length, 512)
    return (length // block_len, block_len)


def block_scores(queries, query_seg, key_rows, key_seg, scaling):
    scores = (
        jnp.einsum("sgd,kgd->sgk", queries, key_rows, preferred_element_type=jnp.float32) * scaling
    )
    allowed = query_seg[:, None, None] == key_seg[None, None, :]
    return (scores, allowed)


def block_grads(
    queries, query_seg, grad_rows, log_total, row_delta, key_rows, value_rows, key_seg, scaling
):
    scores, allowed = block_scores(queries, query_seg, key_rows, key_seg, scaling)
    attn_prob = jnp.where(allowed, jnp.exp(scores - log_total[:, :, None]), 0.0)
    prob_grad = jnp.einsum(
        "sgd,kgd->sgk", grad_rows, value_rows, preferred_element_type=jnp.float32
    )
    score_grad = (attn_prob * (prob_grad - row_delta[:, :, None]) * scaling).astype(jnp.bfloat16)
    return (attn_prob.astype(jnp.bfloat16), score_grad)


def key_blocks(key_rows, value_rows, key_seg, groups):
    block_num, block_len = split_rows(key_rows.shape[0])
    return (
        key_rows.reshape(block_num, block_len, groups, -1),
        value_rows.reshape(block_num, block_len, groups, -1),
        key_seg.reshape(block_num, block_len),
    )


def attend_fold(queries, query_seg, scaling, carried, portion):
    key_rows, value_rows, key_seg = portion

    def step(running, blocks):
        key_part, value_part, seg_part = blocks
        old_max, old_total, weighted = running
        scores, allowed = block_scores(queries, query_seg, key_part, seg_part, scaling)
        row_max = jnp.maximum(old_max, jnp.max(jnp.where(allowed, scores, -1e30), axis=2))
        exp_scores = jnp.where(allowed, jnp.exp(scores - row_max[:, :, None]), 0.0)
        rescale = jnp.exp(old_max - row_max)
        new_total = old_total * rescale + jnp.sum(exp_scores, axis=2)
        weighted = weighted * rescale[:, :, None] + jnp.einsum(
            "sgk,kgd->sgd",
            exp_scores.astype(jnp.bfloat16),
            value_part,
            preferred_element_type=jnp.float32,
        )
        return ((row_max, new_total, weighted), None)

    running, unused = lax.scan(
        step, carried, key_blocks(key_rows, value_rows, key_seg, queries.shape[1])
    )
    return running


def local(
    stream,
    accumulator,
    upstream,
    segment_ids,
    w_query,
    w_key,
    w_value,
    w_out,
    w_up,
    b_up,
    w_down,
    b_down,
    gain_attn,
    bias_attn,
    gain_ffn,
    bias_ffn,
    gain_final,
    bias_final,
):
    heads_axis = lax.axis_size("head")
    micro = stream.shape[0]
    tokens = stream.shape[2]
    width = stream.shape[3]
    group_width = width // heads_axis
    groups = group_width // DH
    scaling = DH ** (-0.5)
    f32 = jnp.float32
    bf16 = jnp.bfloat16
    out_list = []
    stream_grads = []
    accum_grads = []
    grad_totals = None
    for micro_step in range(micro):
        (
            q_weight,
            k_weight,
            v_weight,
            o_weight,
            up_weight,
            up_bias,
            down_weight,
            down_bias,
            gain_one,
            shift_one,
            gain_two,
            shift_two,
            gain_three,
            shift_three,
        ) = (
            lax.all_gather(w_query, ("head", "blk"), axis=0, tiled=True),
            lax.all_gather(w_key, ("head", "blk"), axis=0, tiled=True),
            lax.all_gather(w_value, ("head", "blk"), axis=0, tiled=True),
            lax.all_gather(w_out, ("head", "blk"), axis=0, tiled=True),
            lax.all_gather(w_up, ("head", "blk"), axis=0, tiled=True),
            lax.all_gather(b_up, ("head", "blk"), axis=0, tiled=True),
            lax.all_gather(w_down, ("head", "blk"), axis=0, tiled=True),
            lax.all_gather(b_down, ("head", "blk"), axis=0, tiled=True),
            lax.all_gather(gain_attn, ("head", "blk"), axis=0, tiled=True),
            lax.all_gather(bias_attn, ("head", "blk"), axis=0, tiled=True),
            lax.all_gather(gain_ffn, ("head", "blk"), axis=0, tiled=True),
            lax.all_gather(bias_ffn, ("head", "blk"), axis=0, tiled=True),
            lax.all_gather(gain_final, ("head", "blk"), axis=0, tiled=True),
            lax.all_gather(bias_final, ("head", "blk"), axis=0, tiled=True),
        )
        inputs = stream[micro_step, 0]
        input_wide = inputs.astype(f32)
        carried = accumulator[micro_step, 0].astype(f32)
        segs = segment_ids[micro_step, 0]
        projections = jnp.stack(
            [
                jnp.dot(inputs, q_weight, preferred_element_type=f32),
                jnp.dot(inputs, k_weight, preferred_element_type=f32),
                jnp.dot(inputs, v_weight, preferred_element_type=f32),
            ]
        ).astype(bf16)
        projections = projections.reshape(3, tokens, heads_axis, group_width)
        seg_wide = jnp.broadcast_to(segs[None, :, None, None], (1, tokens, heads_axis, 1))
        regrouped, seg_group = (
            lax.all_to_all(projections, "head", split_axis=2, concat_axis=1, tiled=True),
            lax.all_to_all(seg_wide, "head", split_axis=2, concat_axis=1, tiled=True),
        )
        rows = regrouped.shape[1]
        query_loc = regrouped[0, :, 0]
        key_loc = regrouped[1, :, 0]
        value_loc = regrouped[2, :, 0]
        seg_loc = seg_group[0, :, 0, 0]
        queries3 = query_loc.reshape(rows, groups, DH)
        start_state = (
            jnp.full((rows, groups), -1e30, f32),
            jnp.zeros((rows, groups), f32),
            jnp.zeros((rows, groups, DH), f32),
        )
        row_max, row_total, weighted = attend_fold(
            queries3,
            seg_loc,
            scaling,
            start_state,
            (
                lax.all_gather(key_loc, "blk", axis=0, tiled=True),
                lax.all_gather(value_loc, "blk", axis=0, tiled=True),
                lax.all_gather(seg_loc, "blk", axis=0, tiled=True),
            ),
        )
        attn_out = weighted / row_total[:, :, None]
        log_total = row_max + jnp.log(row_total)
        attn_send = attn_out.astype(bf16).reshape(rows, 1, group_width)
        mixed = lax.all_to_all(attn_send, "head", split_axis=0, concat_axis=1, tiled=True).reshape(
            tokens, width
        )
        branch = jnp.dot(mixed, o_weight, preferred_element_type=f32)
        first, normed_one, inv_one = norm_forward(
            input_wide + branch, gain_one.astype(f32), shift_one.astype(f32)
        )
        first_low = first.astype(bf16)
        hidden_pre = jnp.dot(first_low, up_weight, preferred_element_type=f32) + up_bias.astype(f32)
        hidden_act, gate_pull = jax.vjp(smooth_gate, hidden_pre)
        hidden = hidden_act.astype(bf16)
        feed = jnp.dot(hidden, down_weight, preferred_element_type=f32) + down_bias.astype(f32)
        second, normed_two, inv_two = norm_forward(
            first + feed, gain_two.astype(f32), shift_two.astype(f32)
        )
        final, normed_three, inv_three = norm_forward(
            carried + branch + feed, gain_three.astype(f32), shift_three.astype(f32)
        )
        out_list.append((second + final).astype(bf16))
        cotangent = upstream[micro_step, 0].astype(f32)
        accum_grad, gain3_grad, shift3_grad = norm_backward(
            cotangent, normed_three, inv_three, gain_three.astype(f32)
        )
        second_grad, gain2_grad, shift2_grad = norm_backward(
            cotangent, normed_two, inv_two, gain_two.astype(f32)
        )
        feed_grad = second_grad + accum_grad
        feed_low = feed_grad.astype(bf16)
        down_grad = jnp.dot(hidden.T, feed_low, preferred_element_type=f32)
        (hidden_grad,) = gate_pull(jnp.dot(feed_low, down_weight.T, preferred_element_type=f32))
        hidden_low = hidden_grad.astype(bf16)
        up_grad = jnp.dot(first_low.T, hidden_low, preferred_element_type=f32)
        first_grad = second_grad + jnp.dot(hidden_low, up_weight.T, preferred_element_type=f32)
        resid_grad, gain1_grad, shift1_grad = norm_backward(
            first_grad, normed_one, inv_one, gain_one.astype(f32)
        )
        branch_low = (resid_grad + accum_grad).astype(bf16)
        out_wgrad = jnp.dot(mixed.T, branch_low, preferred_element_type=f32)
        mixed_grad = jnp.dot(branch_low, o_weight.T, preferred_element_type=f32).astype(bf16)
        mixed_grad = mixed_grad.reshape(tokens, heads_axis, group_width)
        grad_group = lax.all_to_all(mixed_grad, "head", split_axis=1, concat_axis=0, tiled=True)
        grad_loc = grad_group[:, 0]
        grad3 = grad_loc.reshape(rows, groups, DH)
        row_delta = jnp.sum(grad3.astype(f32) * attn_out, axis=2)
        whole_keys, whole_values, whole_seg = (
            lax.all_gather(key_loc, "blk", axis=0, tiled=True),
            lax.all_gather(value_loc, "blk", axis=0, tiled=True),
            lax.all_gather(seg_loc, "blk", axis=0, tiled=True),
        )

        def backward_step(running, blocks):
            key_part, value_part, seg_part = blocks
            attn_prob, score_grad = block_grads(
                queries3,
                seg_loc,
                grad3,
                log_total,
                row_delta,
                key_part,
                value_part,
                seg_part,
                scaling,
            )
            running = running + jnp.einsum(
                "sgk,kgd->sgd", score_grad, key_part, preferred_element_type=f32
            )
            key_term = jnp.einsum("sgk,sgd->kgd", score_grad, queries3, preferred_element_type=f32)
            value_term = jnp.einsum("sgk,sgd->kgd", attn_prob, grad3, preferred_element_type=f32)
            return (running, (key_term, value_term))

        query_grad, (key_terms, value_terms) = lax.scan(
            backward_step,
            jnp.zeros((rows, groups, DH), f32),
            key_blocks(whole_keys, whole_values, whole_seg, groups),
        )
        key_grad, value_grad = (
            lax.psum_scatter(
                key_terms.reshape(-1, group_width), "blk", scatter_dimension=0, tiled=True
            ),
            lax.psum_scatter(
                value_terms.reshape(-1, group_width), "blk", scatter_dimension=0, tiled=True
            ),
        )
        grad_stack = jnp.stack(
            [query_grad.reshape(rows, group_width), key_grad, value_grad]
        ).astype(bf16)
        grad_stack = grad_stack.reshape(3, rows, 1, group_width)
        returned = lax.all_to_all(
            grad_stack, "head", split_axis=1, concat_axis=2, tiled=True
        ).reshape(3, tokens, width)
        query_wgrad = jnp.dot(inputs.T, returned[0], preferred_element_type=f32)
        key_wgrad = jnp.dot(inputs.T, returned[1], preferred_element_type=f32)
        value_wgrad = jnp.dot(inputs.T, returned[2], preferred_element_type=f32)
        input_grad = (
            resid_grad
            + jnp.dot(returned[0], q_weight.T, preferred_element_type=f32)
            + jnp.dot(returned[1], k_weight.T, preferred_element_type=f32)
            + jnp.dot(returned[2], v_weight.T, preferred_element_type=f32)
        )
        stream_grads.append(input_grad)
        accum_grads.append(accum_grad)
        step_grads = (
            query_wgrad,
            key_wgrad,
            value_wgrad,
            out_wgrad,
            up_grad,
            jnp.sum(hidden_grad, axis=0),
            down_grad,
            jnp.sum(feed_grad, axis=0),
            gain1_grad,
            shift1_grad,
            gain2_grad,
            shift2_grad,
            gain3_grad,
            shift3_grad,
        )
        if grad_totals is None:
            grad_totals = step_grads
        else:
            grad_totals = tuple((older + newer for older, newer in zip(grad_totals, step_grads)))
    summed = lax.psum_scatter(grad_totals, ("head", "blk"), scatter_dimension=0, tiled=True)
    layer_out = jnp.stack(out_list)[:, None]
    grad_stream = jnp.stack(stream_grads)[:, None]
    grad_accum = jnp.stack(accum_grads)[:, None]
    return (
        layer_out,
        grad_stream,
        grad_accum,
        summed[0],
        summed[1],
        summed[2],
        summed[3],
        summed[4],
        summed[5],
        summed[6],
        summed[7],
        summed[8],
        summed[9],
        summed[10],
        summed[11],
        summed[12],
        summed[13],
    )


def solution(mesh):
    return jax.shard_map(
        local,
        mesh=mesh,
        in_specs=(
            P(None, ("head", "blk"), None, None),
            P(None, ("head", "blk"), None, None),
            P(None, ("head", "blk"), None, None),
            P(None, ("head", "blk"), None),
            P(("head", "blk"), None),
            P(("head", "blk"), None),
            P(("head", "blk"), None),
            P(("head", "blk"), None),
            P(("head", "blk"), None),
            P(("head", "blk")),
            P(("head", "blk"), None),
            P(("head", "blk")),
            P(("head", "blk")),
            P(("head", "blk")),
            P(("head", "blk")),
            P(("head", "blk")),
            P(("head", "blk")),
            P(("head", "blk")),
        ),
        out_specs=(
            P(None, ("head", "blk"), None, None),
            P(None, ("head", "blk"), None, None),
            P(None, ("head", "blk"), None, None),
            P(("head", "blk"), None),
            P(("head", "blk"), None),
            P(("head", "blk"), None),
            P(("head", "blk"), None),
            P(("head", "blk"), None),
            P(("head", "blk")),
            P(("head", "blk"), None),
            P(("head", "blk")),
            P(("head", "blk")),
            P(("head", "blk")),
            P(("head", "blk")),
            P(("head", "blk")),
            P(("head", "blk")),
            P(("head", "blk")),
        ),
        check_vma=False,
    )
```

profile of v0, /device:TPU:0, one launch (start us, length us, event | category | flops | bytes accessed | tf_op | source)
XLA Modules:
  0.0 1655.9 jit_solution(10126575302264865134)
XLA Ops:
  7.2 45.6 %all_gather.81 = bf16[512,512]{1,0:T(8,128)(2,1)S(1)} all-gather(bf16[16,512]{1,0:T(8,128)(2,1)} %param.30), channel_id=1, replica_groups=mesh['head'=4,'blk'=8] {'head','blk'}, dimensions={0}, use_global_device_ids=true | all-gather | bytes 540672 | tf_op jit(solution)/shard_map/all_gather | solution.py:145
  53.8 39.1 %all_gather.82 = bf16[512,512]{1,0:T(8,128)(2,1)S(1)} all-gather(bf16[16,512]{1,0:T(8,128)(2,1)} %param.31), channel_id=1, replica_groups=mesh['head'=4,'blk'=8] {'head','blk'}, dimensions={0}, use_global_device_ids=true | all-gather | bytes 540672 | tf_op jit(solution)/shard_map/all_gather | solution.py:146
  93.8 40.1 %all_gather.83 = bf16[512,512]{1,0:T(8,128)(2,1)S(1)} all-gather(bf16[16,512]{1,0:T(8,128)(2,1)S(1)} %copy-done.75), channel_id=1, replica_groups=mesh['head'=4,'blk'=8] {'head','blk'}, dimensions={0}, use_global_device_ids=true | all-gather | bytes 540672 | tf_op jit(solution)/shard_map/all_gather | solution.py:147
  134.5 10.3 all_to_all.156
  147.6 9.0 all_to_all.157
  171.0 12.7 all-gather.1
  183.7 12.7 all-gather
  202.8 37.4 %while.61 = (s32[]{:T(128)}, f32[512,2]{0,1:T(2,128)S(1)}, f32[512,2]{0,1:T(2,128)S(1)}, f32[512,2,64]{0,2,1:T(8,128)}, s32[1,512,1,1]{1,3,2,0:T(1,128)S(1)}, /*...) while((s32[]{:T(128)}, f32[512,2]{0,1:T(2,128)S(1)}, ...), condition=%wide.region_13.14_spmd.clone, body=%wide.region_10.13_spmd.clone.sunk | while | flops 140448768 | bytes 8332413 | solution.py:89
  253.7 31.3 %while.60 = (s32[]{:T(128)}, f32[512,2]{0,1:T(2,128)S(1)}, f32[512,2]{0,1:T(2,128)S(1)}, f32[512,2,64]{0,2,1:T(8,128)S(1)}, s32[1,512,1,1]{1,3,2,0:T(1,128)S(1)}...) while((s32[]{:T(128)}, f32[512,2]{0,1:T(2,128)S(1)}, ...), condition=%wide.region_3.4_spmd.clone, body=%wide.region_0.3_spmd.clone.sunk | while | flops 140448768 | bytes 8332413 | solution.py:89
  290.8 40.8 %all_gather.86 = bf16[512,512]{1,0:T(8,128)(2,1)S(1)} all-gather(bf16[16,512]{1,0:T(8,128)(2,1)S(1)} %copy-done.76), channel_id=1, replica_groups=mesh['head'=4,'blk'=8] {'head','blk'}, dimensions={0}, use_global_device_ids=true | all-gather | bytes 540672 | tf_op jit(solution)/shard_map/all_gather | solution.py:148
  333.6 38.2 %all-reduce.16 = (bf16[512]{0:T(512)(128)(2,1)S(1)}, bf16[512]{0:T(512)(128)(2,1)S(1)}, bf16[2048]{0:T(1024)(128)(2,1)S(1)}, bf16[512]{0:T(512)(128)(2,1)S(1)}, ...) all-reduce(bf16[512]{0:T(512)(128)(2,1)S(1)} %dynamic-update-slice., ...), channel_id=1, replica_groups=mesh['head'=4,'blk'=8] {'head','blk'}, use_global_device_ids=true, to_apply=%add.7 | all-reduce | flops 5632 | bytes 22528
  412.8 156.7 %while.62 = (s32[]{:T(128)}, f32[512,2,64]{0,2,1:T(8,128)}, f32[8,512,2,64]{1,0,3,2:T(8,128)}, f32[8,512,2,64]{1,0,3,2:T(8,128)}, bf16[8,512,2,64]{1,3,2,0:T(8,1...) while((s32[]{:T(128)}, f32[512,2,64]{0,2,1:T(8,128)}, ...), condition=%wide.region_28.29_spmd.clone, body=%wide.region_27.28_spmd.clone.sunk | while | flops 340131840 | bytes 15288187 | solution.py:272
  589.0 162.3 %while.63 = (s32[]{:T(128)}, f32[512,2,64]{0,2,1:T(8,128)}, f32[8,512,2,64]{1,0,3,2:T(8,128)}, f32[8,512,2,64]{1,0,3,2:T(8,128)}, bf16[8,512,2,64]{1,3,2,0:T(8,1...) while((s32[]{:T(128)}, f32[512,2,64]{0,2,1:T(8,128)}, ...), condition=%wide.region_39.40_spmd.clone, body=%wide.region_38.39_spmd.clone.sunk | while | flops 340131840 | bytes 14599927 | solution.py:272
  602.8 6.4 dynamic_update_slice.24
  614.0 6.4 dynamic_update_slice.23
  769.8 19.7 %reduce-scatter.23.cloned.1.call-done = f32[512,128]{0,1:T(8,128)} async-done(((f32[4096,128]{0,1:T(8,128)}), f32[512,128]{0,1:T(8,128)}) %reduce-scatter.23.cloned.1.call-update) | async-done | bytes 262160 | tf_op jit(solution)/shard_map/reduce_scatter | solution.py:281
  790.4 35.6 %reduce-scatter.21.cloned.1.call-done = f32[512,128]{0,1:T(8,128)} async-done(((f32[4096,128]{0,1:T(8,128)}), f32[512,128]{0,1:T(8,128)}) %reduce-scatter.21.cloned.1.call-update) | async-done | bytes 262160 | tf_op jit(solution)/shard_map/reduce_scatter | solution.py:278
  858.9 37.8 %all-reduce.15 = (f32[2048]{0:T(1024)S(1)}, f32[512]{0:T(512)S(1)}, f32[512]{0:T(512)S(1)}, f32[512]{0:T(512)S(1)}, f32[512]{0:T(512)S(1)}, /*index=5*/f32[512]{0:T(512)S(1)}, f32[512]{0:T(512)S(1)}) all-reduce(f32[2048]{0:T(1024)S(1)} %add.357, f32[512]{0:T(512)S(1)} %add.359, ...), channel_id=11, replica_groups=mesh['head'=4,'blk'=8] {'head','blk'}, use_global_device_ids=true, to_apply=%region_49.50.clone | all-reduce | flops 5120 | bytes 40960
  906.3 56.4 %reduce-scatter.25.cloned.1.call-done = f32[16,512]{1,0:T(8,128)} async-done(((f32[512,512]{1,0:T(8,128)}), f32[16,512]{1,0:T(8,128)}) %reduce-scatter.25.cloned.1.call-update) | async-done | bytes 32784 | tf_op jit(solution)/shard_map/reduce_scatter | solution.py:323
  962.7 133.8 %reduce-scatter.35.cloned.1.call-done = f32[16,512]{1,0:T(8,128)} async-done(((f32[512,512]{1,0:T(8,128)}), f32[16,512]{1,0:T(8,128)}) %reduce-scatter.35.cloned.1.call-update) | async-done | bytes 32784
  1096.5 134.0 %reduce-scatter.33.cloned.1.call-done = f32[16,512]{1,0:T(8,128)} async-done(((f32[512,512]{1,0:T(8,128)}), f32[16,512]{1,0:T(8,128)}) %reduce-scatter.33.cloned.1.call-update) | async-done | bytes 32784
  1230.5 134.2 %reduce-scatter.31.cloned.1.call-done = f32[16,512]{1,0:T(8,128)} async-done(((f32[512,512]{1,0:T(8,128)}), f32[16,512]{1,0:T(8,128)}) %reduce-scatter.31.cloned.1.call-update) | async-done | bytes 32784
  1364.8 141.5 %reduce-scatter.29.cloned.1.call-done = f32[64,512]{1,0:T(8,128)} async-done(((f32[2048,512]{1,0:T(8,128)}), f32[64,512]{1,0:T(8,128)}) %reduce-scatter.29.cloned.1.call-update) | async-done | bytes 131088 | tf_op jit(solution)/shard_map/reduce_scatter | solution.py:323
  1506.3 142.3 %reduce-scatter.27.cloned.1.call-done = f32[16,2048]{1,0:T(8,128)} async-done(((f32[512,2048]{1,0:T(8,128)}), f32[16,2048]{1,0:T(8,128)}) %reduce-scatter.27.cloned.1.call-update) | async-done | bytes 131088 | tf_op jit(solution)/shard_map/reduce_scatter | solution.py:323
  (945 shorter events, 541.2 us)
Async XLA Ops:
  7.2 189.7 %all-gather.17.cloned.1.call-start = ((), (), s32[]{:S(2)}) async-start(), calls=%async_computation.24 | async-start | bytes 1179648 | tf_op jit(solution)/shard_map/all_gather | solution.py:194
  145.6 54.2 %all-gather.19.cloned.1.call-start = ((), (), s32[]{:S(2)}) async-start(), calls=%async_computation.25 | async-start | bytes 1179648 | tf_op jit(solution)/shard_map/all_gather | solution.py:195
  146.5 101.2 %all-gather.9.cloned.1.call-start = ((), (), s32[]{:S(2)}) async-start(), calls=%async_computation.20 | async-start | bytes 1179648 | tf_op jit(solution)/shard_map/all_gather | solution.py:194
  157.4 93.2 %all-gather.11.cloned.1.call-start = ((), (), s32[]{:S(2)}) async-start(), calls=%async_computation.21 | async-start | bytes 1179648 | tf_op jit(solution)/shard_map/all_gather | solution.py:195
  158.2 215.3 %all-gather.13.cloned.1.call-start = ((), (), s32[]{:S(2)}) async-start(), calls=%async_computation.22 | async-start | bytes 2162688 | tf_op jit(solution)/shard_map/all_gather | solution.py:149
  159.4 7.8 all-to-all-start.3
  162.6 220.6 %all-gather.15.cloned.1.call-start = ((), (), s32[]{:S(2)}) async-start(), calls=%async_computation.23 | async-start | bytes 2162688 | tf_op jit(solution)/shard_map/all_gather | solution.py:151
  167.7 16.0 all-to-all-start
  243.2 43.4 %all-to-all-start.5 = ((bf16[4,2,8192]{2,1,0:T(2,128)(2,1)}), bf16[4,2,8192]{2,1,0:T(2,128)(2,1)S(1)}, u32[]{:S(2)}, u32[]{:S(2)}) async-start(bf16[4,2,8192]{2,1,0:T(2,128)(2,1)} %reshape.612), calls=%async_computation.5 | async-start | bytes 262144 | tf_op jit(solution)/shard_map/all_to_all | solution.py:202
  286.6 85.6 %all-to-all-start.2 = ((bf16[4,2,8192]{2,1,0:T(2,128)(2,1)}), bf16[4,2,8192]{2,1,0:T(2,128)(2,1)S(1)}, u32[]{:S(2)}, u32[]{:S(2)}) async-start(bf16[4,2,8192]{2,1,0:T(2,128)(2,1)} %reshape.614), calls=%async_computation.2 | async-start | bytes 262144 | tf_op jit(solution)/shard_map/all_to_all | solution.py:202
  399.5 9.8 all-to-all-start.6
  404.3 358.9 %reduce-scatter.19.cloned.1.call-start = ((), (), s32[]{:S(2)}) async-start(), calls=%async_computation.27 | async-start | bytes 2359296 | tf_op jit(solution)/shard_map/reduce_scatter | solution.py:281
  576.9 8.3 all-to-all-start.8
  580.2 184.0 %reduce-scatter.17.cloned.1.call-start = ((), (), s32[]{:S(2)}) async-start(), calls=%async_computation.26 | async-start | bytes 2359296 | tf_op jit(solution)/shard_map/reduce_scatter | solution.py:278
  585.5 204.0 %reduce-scatter.23.cloned.1.call-start = ((), (), s32[]{:S(2)}) async-start(), calls=%async_computation.29 | async-start | bytes 2359296 | tf_op jit(solution)/shard_map/reduce_scatter | solution.py:281
  755.9 70.2 %reduce-scatter.21.cloned.1.call-start = ((), (), s32[]{:S(2)}) async-start(), calls=%async_computation.28 | async-start | bytes 2359296 | tf_op jit(solution)/shard_map/reduce_scatter | solution.py:278
  760.5 202.2 %reduce-scatter.25.cloned.1.call-start = ((), (), s32[]{:S(2)}) async-start(), calls=%async_computation.30 | async-start | bytes 1081344 | tf_op jit(solution)/shard_map/reduce_scatter | solution.py:323
  766.3 61.9 %all-to-all-start.7 = ((bf16[3,512,1,128]{3,0,2,1:T(4,128)(2,1)}), bf16[3,512,1,128]{3,0,2,1:T(4,128)(2,1)S(1)}, u32[]{:S(2)}, u32[]{:S(2)}) async-start(bf16[3,512,1,128]{3,0,2,1:T(4,128)(2,1)} %copy.318), calls=%async_computation.9 | async-start | bytes 1048576 | tf_op jit(solution)/shard_map/all_to_all | solution.py:289
  828.2 10.3 all-to-all-start.9
  831.8 264.7 %reduce-scatter.35.cloned.1.call-start = ((), (), s32[]{:S(2)}) async-start(), calls=%async_computation.35 | async-start | bytes 1081344
  840.6 389.9 %reduce-scatter.33.cloned.1.call-start = ((), (), s32[]{:S(2)}) async-start(), calls=%async_computation.34 | async-start | bytes 1081344
  842.9 521.9 %reduce-scatter.31.cloned.1.call-start = ((), (), s32[]{:S(2)}) async-start(), calls=%async_computation.33 | async-start | bytes 1081344
  845.2 661.1 %reduce-scatter.29.cloned.1.call-start = ((), (), s32[]{:S(2)}) async-start(), calls=%async_computation.32 | async-start | bytes 4325376 | tf_op jit(solution)/shard_map/reduce_scatter | solution.py:323
  849.0 799.6 %reduce-scatter.27.cloned.1.call-start = ((), (), s32[]{:S(2)}) async-start(), calls=%async_computation.31 | async-start | bytes 4325376 | tf_op jit(solution)/shard_map/reduce_scatter | solution.py:323
  (190 other events, 2869.5 us)
Sparse Core Ops, SparseCore 0:
  145.8 18.5 all-gather.16
  166.6 22.0 all-gather.18
  190.8 21.5 all-gather.8
  213.9 21.9 all-gather.10
  238.7 55.9 all-gather.12
  297.5 55.3 all-gather.14
  574.4 33.2 reduce-scatter.18
  610.0 34.3 reduce-scatter.16
  756.0 33.4 reduce-scatter.22
  791.6 34.4 reduce-scatter.20
  828.9 133.7 reduce-scatter.24
  965.5 130.9 reduce-scatter.34
  1099.3 131.1 reduce-scatter.32
  1233.3 131.4 reduce-scatter.30
  1367.5 138.7 reduce-scatter.28
  1509.0 139.5 reduce-scatter.26
where the time goes:
time: 1670 us; the launch traced here: 1660 us
  waiting for transfers between devices  816 us (49%)
  blocking collectives  286 us (17%)
  local copies, waits for them, and re-layouts  283 us (17%)
  matrix products  187 us (11%)
  other arithmetic  34.5 us (2%)
  starting transfers between devices  31.8 us (2%)
    unnamed x19, waiting for transfers between devices  403 us
    reduce_scatter x3, waiting for transfers between devices, local(): lax.psum_scatter(grad_totals, ('head', 'blk'), scatter_dimension=0, tiled...  340 us
    dynamic_update_slice x64, local copies, waits for them, and re-layouts, local(): lax.scan(backward_step, jnp.zeros((rows, groups, DH), f32), key_blocks(wh...  213 us
    unnamed x2, blocking collectives  76 us
    dot_general x32, matrix products, block_scores(): jnp.einsum('sgd,kgd->sgk', queries, key_rows, preferred_element_type=jnp....  51.1 us
    unnamed x253, local copies, waits for them, and re-layouts  46.6 us
    all_gather x1, blocking collectives, local(): lax.all_gather(w_query, ('head', 'blk'), axis=0, tiled=True)  45.6 us
    all_gather x1, blocking collectives, local(): lax.all_gather(w_out, ('head', 'blk'), axis=0, tiled=True)  40.8 us
  transfers between devices with their start and end apart: 24, of which 12 were waited for; matrix products, arithmetic and copies ran while one was open for 19% of the time, Pallas kernels for 0%

commit v1 on v0

--- a/solution.py
+++ b/solution.py
@@ -1,11 +1,17 @@
+import functools
 import math
 
 import jax
 import jax.numpy as jnp
 from jax import lax
+from jax.experimental import pallas as pl
+from jax.experimental.pallas import tpu as pltpu
 from jax.sharding import PartitionSpec as P
 
 DH = 64
+f32, bf16 = jnp.float32, jnp.bfloat16
+MESH = pl.DeviceIdType.MESH
+FAR = -1e30
 
 
 EPSILON = 1e-05
@@ -345,9 +351,936 @@
     )
 
 
+def dot_t(a, b):
+    return lax.dot_general(a, b, (((1,), (1,)), ((), ())), preferred_element_type=f32)
+
+def dot_n(a, b):
+    return lax.dot_general(a, b, (((1,), (0,)), ((), ())), preferred_element_type=f32)
+
+def dot_0(a, b):
+    return lax.dot_general(a, b, (((0,), (0,)), ((), ())), preferred_element_type=f32)
+
+def lanes(shape):
+    return lax.broadcasted_iota(jnp.int32, shape, len(shape) - 1)
+
+def query_marks(seg_row):
+    wide = jnp.broadcast_to(seg_row, (128, seg_row.shape[1])).T
+    return (wide == lanes(wide.shape)).astype(f32).astype(bf16)
+
+def half_lanes(tile, half):
+    wide = tile.astype(f32)
+    if half:
+        wide = pltpu.roll(wide, 64, 1)
+    return jnp.where(lanes(wide.shape) < 64, wide, 0.0).astype(bf16)
+
+def attn_fwd_kernel(bounds, q_ref, kv_ref, seg_q_ref, seg_k_ref, o_ref, of_ref, lse_ref, kv2_ref, vo_ref):
+    chunks, keys = seg_k_ref.shape
+    log_scale = math.log2(math.e) * DH ** (-0.5)
+
+    def prepare(t, c):
+        rows = pl.ds(pl.multiple_of(t * keys, keys), keys)
+        kv = kv_ref[rows, :]
+        wide = jnp.broadcast_to(seg_k_ref[pl.ds(t, 1), :], (128, keys)).T
+        kv2_ref[rows, 0:128] = kv
+        kv2_ref[rows, 128:256] = jnp.where(wide == lanes(wide.shape), 0.0, FAR).astype(bf16)
+        vo_ref[rows, :] = jnp.where(lanes(kv.shape) < 64, 1.0, kv.astype(f32)).astype(bf16)
+        return c
+
+    lax.fori_loop(0, chunks, prepare, 0)
+
+    def tile(j, c):
+        q_tile = q_ref[j]
+        rows = q_tile.shape[0]
+        outs = []
+        for half in range(2):
+            i = half * (chunks // 2) + j
+            left = half_lanes(q_tile, half)
+            left = jnp.concatenate([left, query_marks(seg_q_ref[pl.ds(i, 1), :])], axis=1)
+            low, high = bounds[0, i], bounds[1, i]
+            first = lax.fori_loop(0, chunks, lambda t, n: n + jnp.where(bounds[1, t] < low, 1, 0), 0)
+            last = lax.fori_loop(0, chunks, lambda t, n: n + jnp.where(bounds[0, t] <= high, 1, 0), 0)
+
+            def step(t, carry):
+                top, acc = carry
+                at = pl.ds(pl.multiple_of(t * keys, keys), keys)
+                s = dot_t(left, kv2_ref[at, :])
+                new = jnp.maximum(top, jnp.max(s, axis=1, keepdims=True))
+                p = jnp.exp2((s - new) * log_scale)
+                acc = acc * jnp.exp2((top - new) * log_scale) + dot_n(p.astype(bf16), vo_ref[at, :])
+                return new, acc
+
+            top, acc = lax.fori_loop(
+                first, last, step, (jnp.full((rows, 1), FAR, f32), jnp.zeros((rows, 128), f32))
+            )
+            total = pltpu.roll(acc, 64, 1)
+            outs.append(acc / total)
+            lse = jnp.broadcast_to(top * log_scale, acc.shape) + jnp.log2(acc)
+            lse_ref[pl.ds(i, 1), :] = lse.T[0:1, :]
+        o = jnp.where(lanes(outs[0].shape) < 64, pltpu.roll(outs[0], 64, 1), outs[1])
+        of_ref[j] = o
+        o_ref[j] = o.astype(bf16)
+        return c
+
+    lax.fori_loop(0, chunks // 2, tile, 0)
+
+def attn_fwd(bounds, q, kv, seg_q, seg_k):
+    chunks, keys = seg_k.shape
+    vm = pl.BlockSpec(memory_space=pltpu.VMEM)
+    return pl.pallas_call(
+        attn_fwd_kernel,
+        out_shape=(
+            jax.ShapeDtypeStruct(q.shape, bf16),
+            jax.ShapeDtypeStruct(q.shape, f32),
+            jax.ShapeDtypeStruct(seg_q.shape, f32),
+            jax.ShapeDtypeStruct((chunks * keys, 256), bf16),
+        ),
+        in_specs=[pl.BlockSpec(memory_space=pltpu.SMEM), vm, vm, vm, vm],
+        out_specs=(vm, vm, vm, vm),
+        scratch_shapes=[pltpu.VMEM((chunks * keys, 128), bf16)],
+        compiler_params=pltpu.CompilerParams(vmem_limit_bytes=56 << 20),
+        name="attn_fwd",
+    )(bounds, q, kv, seg_q, seg_k)
+
+def attn_bwd_kernel(bounds, q_ref, do_ref, of_ref, lse_ref, kv2_ref, seg_q_ref, dq_ref, dkv_ref):
+    chunks = seg_q_ref.shape[0]
+    keys = kv2_ref.shape[0] // chunks
+    log_scale = math.log2(math.e) * DH ** (-0.5)
+    dkv_ref[...] = jnp.zeros_like(dkv_ref)
+
+    def tile(j, c):
+        q_tile, do_tile = q_ref[j], do_ref[j]
+        rows = q_tile.shape[0]
+        prod = do_tile.astype(f32) * of_ref[j]
+        prod = prod.T
+        dqs = []
+        for half in range(2):
+            i = half * (chunks // 2) + j
+            left = half_lanes(q_tile, half)
+            grad = do_tile.astype(f32)
+            if not half:
+                grad = pltpu.roll(grad, 64, 1)
+            grad = jnp.where(lanes(grad.shape) < 64, 0.0, grad).astype(bf16)
+            delta = jnp.sum(prod[64 * half:64 * half + 64], axis=0, keepdims=True)
+            lse = lse_ref[pl.ds(i, 1), :]
+            both = jnp.concatenate([left, grad], axis=0)
+            marks = query_marks(seg_q_ref[pl.ds(i, 1), :])
+            right = jnp.concatenate([both, jnp.concatenate([marks, jnp.zeros_like(marks)], axis=0)], axis=1)
+            low, high = bounds[0, i], bounds[1, i]
+            first = lax.fori_loop(0, chunks, lambda t, n: n + jnp.where(bounds[1, t] < low, 1, 0), 0)
+            last = lax.fori_loop(0, chunks, lambda t, n: n + jnp.where(bounds[0, t] <= high, 1, 0), 0)
+
+            def step(t, dq):
+                at = pl.ds(pl.multiple_of(t * keys, keys), keys)
+                kv2 = kv2_ref[at, :]
+                sdp = dot_t(kv2, right)
+                p = jnp.exp2(sdp[:, :rows] * log_scale - lse)
+                ds = (p * (sdp[:, rows:] - delta)).astype(bf16)
+                dkv_ref[at, :] += dot_n(jnp.concatenate([ds, p.astype(bf16)], axis=1), both)
+                return dq + dot_0(ds, kv2[:, 0:128])
+
+            dqs.append(lax.fori_loop(first, last, step, jnp.zeros((rows, 128), f32)))
+        dq = jnp.where(lanes(dqs[0].shape) < 64, dqs[0], pltpu.roll(dqs[1], 64, 1))
+        dq_ref[j] = (dq * DH ** (-0.5)).astype(bf16)
+        return c
+
+    lax.fori_loop(0, chunks // 2, tile, 0)
+    dkv = dkv_ref[...]
+    dkv_ref[...] = jnp.where(lanes(dkv.shape) < 64, dkv * DH ** (-0.5), dkv)
+
+def attn_bwd(bounds, q, do, of, lse, kv2, seg_q):
+    vm = pl.BlockSpec(memory_space=pltpu.VMEM)
+    return pl.pallas_call(
+        attn_bwd_kernel,
+        out_shape=(
+            jax.ShapeDtypeStruct(q.shape, bf16),
+            jax.ShapeDtypeStruct((kv2.shape[0], 128), f32),
+        ),
+        in_specs=[pl.BlockSpec(memory_space=pltpu.SMEM), vm, vm, vm, vm, vm, vm],
+        out_specs=(vm, vm),
+        compiler_params=pltpu.CompilerParams(vmem_limit_bytes=56 << 20),
+        name="attn_bwd",
+    )(bounds, q, do, of, lse, kv2, seg_q)
+
+
+class Spot:
+    def __init__(self, nb):
+        self.nb, self.nz = nb, nb // 2
+        self.h, b = lax.axis_index("head"), lax.axis_index("blk")
+        self.z, self.c = b // 2, lax.rem(b, 2)
+        self.near = (self.h + 1 - 2 * lax.rem(self.h, 2), lax.rem(self.h + 2, 4))
+        self.diag = 3 - self.h
+        self.me = self.h * nb + b
+
+    def index(self, h, z, c):
+        return h * self.nb + z * 2 + c
+
+    def ahead(self, k):
+        return lax.rem(self.z + k, self.nz)
+
+
+def remote(src, dst, send, recv, h, b):
+    return pltpu.make_async_remote_copy(
+        src_ref=src,
+        dst_ref=dst,
+        send_sem=send,
+        recv_sem=recv,
+        device_id={"head": h, "blk": b},
+        device_id_type=MESH,
+    )
+
+
+def each(count, body, start=0):
+    def run(i, c):
+        body(i)
+        return c
+
+    lax.fori_loop(start, count, run, 0)
+
+
+def greet_all(n, nb, me):
+    barrier = pltpu.get_barrier_semaphore()
+
+    def signal(i):
+        t = lax.rem(me + i, n)
+        pl.semaphore_signal(
+            barrier, inc=1, device_id={"head": t // nb, "blk": lax.rem(t, nb)}, device_id_type=MESH
+        )
+
+    each(n, signal, 1)
+    pl.semaphore_wait(barrier, n - 1)
+
+
+class Gather:
+    def __init__(self, spot, shard, full, send, recv, local):
+        self.s, self.shard, self.full, self.local = spot, shard, full, local
+        self.send, self.recv = send, recv
+        self.half = shard.shape[-1] // 2
+
+    def copy(self, src, dst, k, h, z, c, recv_k=None):
+        recv_k = k if recv_k is None else recv_k
+        return remote(src, dst, self.send.at[k], self.recv.at[recv_k], h, z * 2 + c)
+
+    def to_z(self, z):
+        s = self.s
+        return self.copy(self.shard, self.full.at[s.me], z, s.h, z, s.c, s.z)
+
+    def from_z(self, z):
+        s = self.s
+        slot = self.full.at[s.index(s.h, z, s.c)]
+        return self.copy(slot, slot, z, s.h, z, s.c)
+
+    def near(self, w, z, own=False):
+        s = self.s
+        slot = self.full.at[s.index(s.h, z, s.c)]
+        return self.copy(self.shard if own else slot, slot, (1 + w) * s.nz + z, s.near[w], s.z, s.c)
+
+    def from_near(self, w, z):
+        s = self.s
+        slot = self.full.at[s.index(s.near[w], z, s.c)]
+        return self.copy(slot, slot, (1 + w) * s.nz + z, s.near[w], s.z, s.c)
+
+    def lanes(self, slot, w):
+        return slot.at[:, pl.ds(w * self.half, self.half)]
+
+    def onward(self, w, z):
+        s = self.s
+        slot = self.lanes(self.full.at[s.index(s.near[w], z, s.c)], w)
+        return self.copy(slot, slot, (3 + w) * s.nz + z, s.near[1 - w], s.z, s.c)
+
+    def from_onward(self, w, z):
+        s = self.s
+        slot = self.lanes(self.full.at[s.index(s.diag, z, s.c)], w)
+        return self.copy(slot, slot, (3 + w) * s.nz + z, s.near[1 - w], s.z, s.c)
+
+    def twin(self, h, z, own=False):
+        s = self.s
+        slot = self.full.at[s.index(h, z, s.c)]
+        return self.copy(self.shard if own else slot, slot, 5 * s.nz + h * s.nz + z, s.h, s.z, 1 - s.c)
+
+    def from_twin(self, h, z):
+        s = self.s
+        slot = self.full.at[s.index(h, z, 1 - s.c)]
+        return self.copy(slot, slot, 5 * s.nz + h * s.nz + z, s.h, s.z, 1 - s.c)
+
+    def begin(self):
+        s = self.s
+        self.own = pltpu.make_async_copy(self.shard, self.full.at[s.me], self.local)
+        self.own.start()
+        each(s.nz, lambda k: self.to_z(s.ahead(k)).start(), 1)
+        self.near(0, s.z, True).start()
+        self.near(1, s.z, True).start()
+        self.twin(s.h, s.z, True).start()
+
+    def spread(self):
+        s = self.s
+
+        def go(k):
+            z = s.ahead(k)
+            self.from_z(z).wait_recv()
+            self.near(0, z).start()
+            self.near(1, z).start()
+            self.twin(s.h, z).start()
+
+        each(s.nz, go, 1)
+
+    def cross(self):
+        s = self.s
+
+        def go(k):
+            z = s.ahead(k)
+            for w in range(2):
+                self.from_near(w, z).wait_recv()
+                self.onward(w, z).start()
+                self.twin(s.near[w], z).start()
+
+        each(s.nz, go)
+
+    def last(self):
+        s = self.s
+
+        def go(k):
+            z = s.ahead(k)
+            for w in range(2):
+                self.from_onward(w, z).wait_recv()
+            self.twin(s.diag, z).start()
+
+        each(s.nz, go)
+
+    def arrive(self):
+        s = self.s
+        each(4, lambda h: each(s.nz, lambda z: self.from_twin(h, z).wait_recv()))
+        self.own.wait()
+
+    def sent(self):
+        s = self.s
+        each(s.nz, lambda k: self.to_z(s.ahead(k)).wait_send(), 1)
+
+        def go(z):
+            for w in range(2):
+                self.near(w, z).wait_send()
+                self.onward(w, z).wait_send()
+            each(4, lambda h: self.twin(h, z).wait_send())
+
+        each(s.nz, go)
+
+
+class Scatter:
+    def __init__(self, spot, part, twin, diag, near, line, send, recv):
+        self.s, self.part, self.t, self.d, self.n, self.l = spot, part, twin, diag, near, line
+        self.send, self.recv = send, recv
+        self.half = part.shape[-1] // 2
+
+    def copy(self, src, dst, k, h, z, c, recv_k=None):
+        recv_k = k if recv_k is None else recv_k
+        return remote(src, dst, self.send.at[k], self.recv.at[recv_k], h, z * 2 + c)
+
+    def mine(self, h, z):
+        return self.s.index(h, z, self.s.c)
+
+    def lanes(self, w):
+        return pl.ds(w * self.half, self.half)
+
+    def to_twin(self, h, z):
+        s = self.s
+        src = self.part.at[s.index(h, z, 1 - s.c)]
+        return self.copy(src, self.t.at[h, z], h * s.nz + z, s.h, s.z, 1 - s.c)
+
+    def to_diag(self, w, z):
+        s = self.s
+        src = self.part.at[self.mine(s.diag, z), :, self.lanes(w)]
+        return self.copy(src, self.d.at[w, z], (4 + w) * s.nz + z, s.near[w], s.z, s.c)
+
+    def to_near(self, w, z):
+        s = self.s
+        src = self.part.at[self.mine(s.near[w], z)]
+        return self.copy(src, self.n.at[w, z], (6 + w) * s.nz + z, s.near[w], s.z, s.c)
+
+    def to_line(self, z):
+        s = self.s
+        src = self.part.at[self.mine(s.h, z)]
+        return self.copy(src, self.l.at[s.z], 8 * s.nz + z, s.h, z, s.c, 8 * s.nz + s.z)
+
+    def from_line(self, z):
+        s = self.s
+        src = self.part.at[self.mine(s.h, z)]
+        return self.copy(src, self.l.at[z], 8 * s.nz + z, s.h, z, s.c)
+
+    def begin(self):
+        each(4, lambda h: each(self.s.nz, lambda z: self.to_twin(h, z).start()))
+
+    def pair(self, h, z):
+        self.to_twin(h, z).wait_recv()
+        return self.part[self.mine(h, z)].astype(f32) + self.t[h, z].astype(f32)
+
+    def keep(self, h, z, value):
+        self.part[self.mine(h, z)] = value.astype(self.part.dtype)
+
+    def first(self):
+        s = self.s
+
+        def go(k):
+            z = s.ahead(k)
+            self.keep(s.diag, z, self.pair(s.diag, z))
+            for w in range(2):
+                self.to_diag(w, z).start()
+
+        each(s.nz + 1, go, 1)
+
+    def second(self):
+        s = self.s
+
+        def go(k):
+            z = s.ahead(k)
+            for w in range(2):
+                value = self.pair(s.near[w], z)
+                self.to_diag(1 - w, z).wait_recv()
+                other = self.d[1 - w, z].astype(f32)
+                if w == 0:
+                    value = jnp.concatenate([value[:, : self.half], value[:, self.half :] + other], axis=1)
+                else:
+                    value = jnp.concatenate([value[:, : self.half] + other, value[:, self.half :]], axis=1)
+                self.keep(s.near[w], z, value)
+                self.to_near(w, z).start()
+
+        each(s.nz + 1, go, 1)
+
+    def joined(self, z):
+        value = self.pair(self.s.h, z)
+        for w in range(2):
+            self.to_near(w, z).wait_recv()
+            value = value + self.n[w, z].astype(f32)
+        return value
+
+    def third(self):
+        s = self.s
+
+        def go(k):
+            z = s.ahead(k)
+            self.keep(s.h, z, self.joined(z))
+            self.to_line(z).start()
+
+        each(s.nz, go, 1)
+
+    def total(self):
+        s = self.s
+        value = self.joined(s.z)
+
+        def go(k, value):
+            z = s.ahead(k)
+            self.from_line(z).wait_recv()
+            return value + self.l[z].astype(f32)
+
+        return lax.fori_loop(1, s.nz, go, value)
+
+    def sent(self):
+        s = self.s
+
+        def go(z):
+            each(4, lambda h: self.to_twin(h, z).wait_send())
+            for w in range(2):
+                self.to_diag(w, z).wait_send()
+                self.to_near(w, z).wait_send()
+
+        each(s.nz, go)
+        each(s.nz, lambda k: self.to_line(s.ahead(k)).wait_send(), 1)
+
+
+class Exchange:
+    def __init__(self, spot, src, dst, send, recv, local):
+        self.s, self.src, self.dst, self.send, self.recv, self.local = spot, src, dst, send, recv, local
+        self.g = spot.me // 2
+
+    def copy(self, i, back=False):
+        s = self.s
+        to = lax.rem(self.g + i, 16)
+        t = to * 2 + s.c
+        src = self.src(to)
+        dst = self.dst(lax.rem(self.g + 16 - i, 16)) if back else self.dst(self.g)
+        return remote(src, dst, self.send.at[i], self.recv.at[i], t // s.nb, lax.rem(t, s.nb))
+
+    def own(self):
+        return pltpu.make_async_copy(self.src(self.g), self.dst(self.g), self.local)
+
+    def begin(self):
+        self.own().start()
+        each(16, lambda i: self.copy(i).start(), 1)
+
+    def arrive(self, i):
+        self.copy(i, True).wait_recv()
+
+    def end(self):
+        each(16, self.arrive, 1)
+        self.sent()
+
+    def sent(self):
+        self.own().wait()
+        each(16, lambda i: self.copy(i).wait_send(), 1)
+
+
+def weave(left, right):
+    kind = left.dtype
+    left, right = left.astype(f32), right.astype(f32)
+    low = lanes(left.shape) < 64
+    first = jnp.where(low, left, pltpu.roll(right, 64, 1)).astype(kind)
+    second = jnp.where(low, pltpu.roll(left, 64, 1), right).astype(kind)
+    return first, second
+
+
+def any_specs(count):
+    return [pl.BlockSpec(memory_space=pl.ANY)] * count
+
+
+def vmem_specs(count):
+    return [pl.BlockSpec(memory_space=pltpu.VMEM)] * count
+
+
+def project_kernel(
+    n, nb, x_ref, wq_ref, wk_ref, wv_ref, wo_ref, wu_ref, wd_ref, vec_ref,
+    q_out, kv_out, wa_out, wb_out, wd_out, vec_out,
+    sa, sb, wa, kv_send, q_send, ag_send, ag_recv, ag_local, ex_send, ex_recv, ex_local,
+    tw_send, tw_recv, out_sem,
+):
+    s = Spot(nb)
+    greet_all(n, nb, s.me)
+    for t in range(4):
+        tile = slice(128 * t, 128 * t + 128)
+        first, second = weave(wk_ref[:, tile], wv_ref[:, tile])
+        sa[:, 256 * t:256 * t + 128] = first
+        sa[:, 256 * t + 128:256 * t + 256] = second
+    sa[:, 1024:1536] = wq_ref[...]
+    sb[:, 0:512] = wo_ref[...]
+    sb[:, 512:2560] = wu_ref[...]
+    jobs = [
+        Gather(s, shard, full, ag_send.at[k], ag_recv.at[k], ag_local.at[k])
+        for k, (shard, full) in enumerate(((sa, wa), (sb, wb_out), (wd_ref, wd_out), (vec_ref, vec_out)))
+    ]
+    jobs[0].begin()
+    jobs[0].spread()
+    jobs[0].cross()
+    jobs[0].last()
+    for job in jobs[1:]:
+        job.begin()
+    jobs[0].arrive()
+    keep = pltpu.make_async_copy(wa, wa_out, out_sem)
+    keep.start()
+    qkv = dot_n(x_ref[...], wa[...].reshape(512, 1536)).astype(bf16)
+    for m in range(2):
+        rows = slice(128 * m, 128 * m + 128)
+        for h in range(8):
+            kv_send[8 * m + h] = qkv[rows, 128 * h:128 * h + 128].reshape(8, 16, 128)
+        for t in range(4):
+            tile = qkv[rows, 1024 + 128 * t:1152 + 128 * t]
+            first, second = weave(tile[0:64], tile[64:128])
+            q_send[8 * m + 2 * t] = first.reshape(4, 16, 128)
+            q_send[8 * m + 2 * t + 1] = second.reshape(4, 16, 128)
+    kv_ex = Exchange(
+        s, lambda p: kv_send.at[p], lambda g: kv_out.at[:, g, s.c], ex_send.at[0], ex_recv.at[0], ex_local.at[0]
+    )
+    q_ex = Exchange(s, lambda p: q_send.at[p], lambda g: q_out.at[:, g], ex_send.at[1], ex_recv.at[1], ex_local.at[1])
+    kv_ex.begin()
+    q_ex.begin()
+    for job in jobs[1:]:
+        job.spread()
+    for job in jobs[1:]:
+        job.cross()
+
+    def twin(g, c):
+        slot = kv_out.at[:, g, c]
+        return remote(slot, slot, tw_send.at[g], tw_recv.at[g], s.h, s.z * 2 + 1 - s.c)
+
+    kv_ex.own().wait()
+    twin(kv_ex.g, s.c).start()
+
+    def forward(i):
+        kv_ex.arrive(i)
+        twin(lax.rem(kv_ex.g + 16 - i, 16), s.c).start()
+
+    each(16, forward, 1)
+    for job in jobs[1:]:
+        job.last()
+    for job in jobs[1:]:
+        job.arrive()
+    each(16, lambda g: twin(g, 1 - s.c).wait_recv())
+    each(16, lambda g: twin(g, s.c).wait_send())
+    each(16, lambda i: kv_ex.copy(i).wait_send(), 1)
+    q_ex.end()
+    for job in jobs:
+        job.sent()
+    keep.wait()
+
+
+def project(n, nb, x, wq, wk, wv, wo, wu, wd, vec):
+    dma = pltpu.SemaphoreType.DMA
+    nz = nb // 2
+    return pl.pallas_call(
+        functools.partial(project_kernel, n, nb),
+        out_shape=(
+            jax.ShapeDtypeStruct((4, 16, 16, 128), bf16),
+            jax.ShapeDtypeStruct((8, 16, 2, 16, 128), bf16),
+            jax.ShapeDtypeStruct((n, 16, 1536), bf16),
+            jax.ShapeDtypeStruct((n, 16, 2560), bf16),
+            jax.ShapeDtypeStruct((n, 64, 512), bf16),
+            jax.ShapeDtypeStruct((n, 8, 256), f32),
+        ),
+        in_specs=vmem_specs(8),
+        out_specs=any_specs(6),
+        scratch_shapes=[
+            pltpu.VMEM((16, 1536), bf16),
+            pltpu.VMEM((16, 2560), bf16),
+            pltpu.VMEM((n, 16, 1536), bf16),
+            pltpu.VMEM((16, 8, 16, 128), bf16),
+            pltpu.VMEM((16, 4, 16, 128), bf16),
+            dma((4, 9 * nz)),
+            dma((4, 9 * nz)),
+            dma((4,)),
+            dma((2, 16)),
+            dma((2, 16)),
+            dma((2,)),
+            dma((16,)),
+            dma((16,)),
+            dma,
+        ],
+        compiler_params=pltpu.CompilerParams(
+            collective_id=1, has_side_effects=True, vmem_limit_bytes=40 << 20
+        ),
+        name="project",
+    )(x, wq, wk, wv, wo, wu, wd, vec)
+
+
+def row_norm(v):
+    mean = jnp.mean(v, axis=-1, keepdims=True)
+    mid = v - mean
+    inv = lax.rsqrt(jnp.mean(mid * mid, axis=-1, keepdims=True) + EPSILON)
+    return mid * inv, inv
+
+
+def row_norm_back(grad, normed, inv, gain):
+    part = grad * gain
+    return inv * (
+        part
+        - jnp.mean(part, axis=-1, keepdims=True)
+        - normed * jnp.mean(part * normed, axis=-1, keepdims=True)
+    )
+
+
+def column_sum(v):
+    return jnp.sum(v, axis=0, keepdims=True)
+
+
+def middle_kernel(
+    n, nb, o_ref, x_ref, y_ref, g_ref, wb_hbm, wd_hbm, par_ref, bup_ref,
+    do_out, out_ref, dacc_ref, dz1_ref, x1_ref, dur_ref, h_ref, dfr_ref, omix_ref, dar_ref, pg_ref, bg_ref,
+    wb, wd, o_recv, do_send, slope, ex_send, ex_recv, ex_local, in_sem,
+):
+    s = Spot(nb)
+    load_b = pltpu.make_async_copy(wb_hbm, wb, in_sem.at[0])
+    load_d = pltpu.make_async_copy(wd_hbm, wd, in_sem.at[1])
+    load_b.start()
+    load_d.start()
+    greet_all(n, nb, s.me)
+    o_ex = Exchange(
+        s, lambda p: o_ref.at[:, p], lambda g: o_recv.at[g], ex_send.at[0], ex_recv.at[0], ex_local.at[0]
+    )
+    o_ex.begin()
+    load_b.wait()
+    load_d.wait()
+    o_ex.end()
+    for m in range(2):
+        for t in range(4):
+            first, second = weave(
+                o_recv[8 * m + 2 * t].reshape(64, 128), o_recv[8 * m + 2 * t + 1].reshape(64, 128)
+            )
+            omix_ref[128 * m:128 * m + 64, 128 * t:128 * t + 128] = first
+            omix_ref[128 * m + 64:128 * m + 128, 128 * t:128 * t + 128] = second
+    gain1, bias1 = par_ref[1:2], par_ref[2:3]
+    gain2, bias2 = par_ref[3:4], par_ref[4:5]
+    gain3, bias3 = par_ref[5:6], par_ref[6:7]
+    w_out = wb[:, :, 0:512].reshape(512, 512)
+    a = dot_n(omix_ref[...], w_out)
+    n1, r1 = row_norm(x_ref[...].astype(f32) + a)
+    x1 = n1 * gain1 + bias1
+    x1r = x1.astype(bf16)
+    x1_ref[...] = x1r
+    feed = jnp.zeros_like(x1)
+    for t in range(4):
+        cols = slice(512 * t, 512 * t + 512)
+        u = dot_n(x1r, wb[:, :, 512 + 512 * t:1024 + 512 * t].reshape(512, 512)) + bup_ref[:, cols]
+        phi = 0.5 * (1.0 + lax.erf(u * (0.5**0.5)))
+        hid = (u * phi).astype(bf16)
+        slope[:, cols] = phi + u * jnp.exp(-0.5 * u * u) * ((2.0 * math.pi) ** -0.5)
+        h_ref[:, cols] = hid
+        feed = feed + dot_n(hid, wd[8 * t:8 * t + 8].reshape(512, 512))
+    feed = feed + par_ref[0:1]
+    n2, r2 = row_norm(x1 + feed)
+    n3, r3 = row_norm(y_ref[...].astype(f32) + a + feed)
+    out_ref[...] = (n2 * gain2 + bias2 + (n3 * gain3 + bias3)).astype(bf16)
+    g = g_ref[...].astype(f32)
+    dacc = row_norm_back(g, n3, r3, gain3)
+    dacc_ref[...] = dacc
+    dz2 = row_norm_back(g, n2, r2, gain2)
+    df = dz2 + dacc
+    dfr = df.astype(bf16)
+    dfr_ref[...] = dfr
+    dx1 = dz2
+    for t in range(4):
+        cols = slice(512 * t, 512 * t + 512)
+        du = dot_t(dfr, wd[8 * t:8 * t + 8].reshape(512, 512)) * slope[:, cols]
+        bg_ref[:, cols] = column_sum(du)
+        dur = du.astype(bf16)
+        dur_ref[:, cols] = dur
+        dx1 = dx1 + dot_t(dur, wb[:, :, 512 + 512 * t:1024 + 512 * t].reshape(512, 512))
+    dz1 = row_norm_back(dx1, n1, r1, gain1)
+    dz1_ref[...] = dz1
+    dar = (dz1 + dacc).astype(bf16)
+    dar_ref[...] = dar
+    do = dot_t(dar, w_out).astype(bf16)
+    for m in range(2):
+        for t in range(4):
+            tile = do[128 * m:128 * m + 128, 128 * t:128 * t + 128]
+            first, second = weave(tile[0:64], tile[64:128])
+            do_send[8 * m + 2 * t] = first.reshape(4, 16, 128)
+            do_send[8 * m + 2 * t + 1] = second.reshape(4, 16, 128)
+    do_ex = Exchange(
+        s, lambda p: do_send.at[p], lambda g: do_out.at[:, g], ex_send.at[1], ex_recv.at[1], ex_local.at[1]
+    )
+    do_ex.begin()
+    pg_ref[0:1] = column_sum(df)
+    pg_ref[1:2] = column_sum(dx1 * n1)
+    pg_ref[2:3] = column_sum(dx1)
+    pg_ref[3:4] = column_sum(g * n2)
+    pg_ref[4:5] = column_sum(g)
+    pg_ref[5:6] = column_sum(g * n3)
+    pg_ref[6:7] = column_sum(g)
+    pg_ref[7:8] = jnp.zeros((1, 512), f32)
+    do_ex.end()
+
+
+def middle(n, nb, o, x, y, g, wb, wd, par, bup):
+    dma = pltpu.SemaphoreType.DMA
+    rows = x.shape[0]
+
+    def wide(width, kind):
+        return jax.ShapeDtypeStruct((rows, width), kind)
+
+    return pl.pallas_call(
+        functools.partial(middle_kernel, n, nb),
+        out_shape=(
+            jax.ShapeDtypeStruct((4, 16, 16, 128), bf16),
+            wide(512, bf16), wide(512, f32), wide(512, f32), wide(512, bf16), wide(2048, bf16),
+            wide(2048, bf16), wide(512, bf16), wide(512, bf16), wide(512, bf16),
+            jax.ShapeDtypeStruct((8, 512), f32),
+            jax.ShapeDtypeStruct((1, 2048), f32),
+        ),
+        in_specs=vmem_specs(4) + any_specs(2) + vmem_specs(2),
+        out_specs=any_specs(1) + vmem_specs(11),
+        scratch_shapes=[
+            pltpu.VMEM(wb.shape, bf16),
+            pltpu.VMEM(wd.shape, bf16),
+            pltpu.VMEM((16, 4, 16, 128), bf16),
+            pltpu.VMEM((16, 4, 16, 128), bf16),
+            pltpu.VMEM((rows, 2048), f32),
+            dma((2, 16)),
+            dma((2, 16)),
+            dma((2,)),
+            dma((2,)),
+        ],
+        compiler_params=pltpu.CompilerParams(
+            collective_id=2, has_side_effects=True, vmem_limit_bytes=50 << 20
+        ),
+        name="middle",
+    )(o, x, y, g, wb, wd, par, bup)
+
+
+def finish_kernel(
+    n, nb, dq_ref, dkv_ref, x_ref, dz1_ref, x1_ref, dur_ref, h_ref, dfr_ref, omix_ref, dar_ref, gv_ref, wa_ref,
+    gx_ref, gq_ref, gk_ref, gv_out, go_ref, gu_ref, gd_ref, gvec_ref,
+    pa, ta, da, na, la, pb, tb, db, nb_, lb, pd, td, dd, nd, ld, pv, tv, dv, nv, lv,
+    twin_buf, dkv_send, dkv_recv, dq_recv, dqkv, rs_send, rs_recv, ex_send, ex_recv, ex_local, tw_send, tw_recv,
+):
+    s = Spot(nb)
+    greet_all(n, nb, s.me)
+    swap = remote(dkv_ref.at[:, :, 1 - s.c], twin_buf, tw_send, tw_recv, s.h, s.z * 2 + 1 - s.c)
+    swap.start()
+    jobs = [
+        Scatter(s, *bufs, rs_send.at[k], rs_recv.at[k])
+        for k, bufs in enumerate(
+            ((pb, tb, db, nb_, lb), (pd, td, dd, nd, ld), (pv, tv, dv, nv, lv), (pa, ta, da, na, la))
+        )
+    ]
+    pv[...] = gv_ref[...]
+    jobs[2].begin()
+    pb[:, :, 0:512] = dot_0(omix_ref[...], dar_ref[...]).astype(bf16).reshape(n, 16, 512)
+    for t in range(4):
+        cols = slice(512 * t, 512 * t + 512)
+        pb[:, :, 512 + 512 * t:1024 + 512 * t] = (
+            dot_0(x1_ref[...], dur_ref[:, cols]).astype(bf16).reshape(n, 16, 512)
+        )
+    jobs[0].begin()
+    for t in range(4):
+        cols = slice(512 * t, 512 * t + 512)
+        pd[8 * t:8 * t + 8] = dot_0(h_ref[:, cols], dfr_ref[...]).astype(bf16).reshape(8, 64, 512)
+    jobs[1].begin()
+    swap.wait()
+
+    def add(g):
+        dkv_send[g] = (dkv_ref[:, g, s.c] + twin_buf[:, g]).astype(bf16)
+
+    each(16, add)
+    kv_ex = Exchange(
+        s, lambda p: dkv_send.at[p], lambda g: dkv_recv.at[g], ex_send.at[0], ex_recv.at[0], ex_local.at[0]
+    )
+    q_ex = Exchange(s, lambda p: dq_ref.at[:, p], lambda g: dq_recv.at[g], ex_send.at[1], ex_recv.at[1], ex_local.at[1])
+    kv_ex.begin()
+    q_ex.begin()
+    for job in jobs[:3]:
+        job.first()
+    for job in jobs[:3]:
+        job.second()
+    for job in jobs[:3]:
+        job.third()
+    kv_ex.end()
+    q_ex.end()
+    for m in range(2):
+        rows = slice(128 * m, 128 * m + 128)
+        for h in range(8):
+            dqkv[rows, 128 * h:128 * h + 128] = dkv_recv[8 * m + h].reshape(128, 128)
+        for t in range(4):
+            first, second = weave(
+                dq_recv[8 * m + 2 * t].reshape(64, 128), dq_recv[8 * m + 2 * t + 1].reshape(64, 128)
+            )
+            dqkv[128 * m:128 * m + 64, 1024 + 128 * t:1152 + 128 * t] = first
+            dqkv[128 * m + 64:128 * m + 128, 1024 + 128 * t:1152 + 128 * t] = second
+    for t in range(3):
+        cols = slice(512 * t, 512 * t + 512)
+        pa[:, :, cols] = dot_0(x_ref[...], dqkv[:, cols]).astype(bf16).reshape(n, 16, 512)
+    jobs[3].begin()
+    gx_ref[...] = dz1_ref[...] + dot_t(dqkv[...], wa_ref[...].reshape(512, 1536))
+    total = jobs[0].total()
+    go_ref[...] = total[:, 0:512]
+    gu_ref[...] = total[:, 512:2560]
+    gd_ref[...] = jobs[1].total()
+    gvec_ref[...] = jobs[2].total()
+    jobs[3].first()
+    jobs[3].second()
+    jobs[3].third()
+    total = jobs[3].total()
+    gq_ref[...] = total[:, 1024:1536]
+    for t in range(4):
+        first, second = weave(total[:, 256 * t:256 * t + 128], total[:, 256 * t + 128:256 * t + 256])
+        gk_ref[:, 128 * t:128 * t + 128] = first
+        gv_out[:, 128 * t:128 * t + 128] = second
+    for job in jobs:
+        job.sent()
+
+
+def finish(n, nb, dq, dkv, x, dz1, x1, dur, hid, dfr, omix, dar, gvec, wa):
+    dma = pltpu.SemaphoreType.DMA
+    nz = nb // 2
+    rows = x.shape[0]
+
+    def buffers(depth, width, kind):
+        return [
+            pltpu.VMEM((n, depth, width), kind),
+            pltpu.VMEM((4, nz, depth, width), kind),
+            pltpu.VMEM((2, nz, depth, width // 2), kind),
+            pltpu.VMEM((2, nz, depth, width), kind),
+            pltpu.VMEM((nz, depth, width), kind),
+        ]
+
+    def wide(height, width):
+        return jax.ShapeDtypeStruct((height, width), f32)
+
+    return pl.pallas_call(
+        functools.partial(finish_kernel, n, nb),
+        out_shape=(
+            wide(rows, 512), wide(16, 512), wide(16, 512), wide(16, 512), wide(16, 512), wide(16, 2048),
+            wide(64, 512), wide(8, 256),
+        ),
+        in_specs=vmem_specs(12),
+        out_specs=vmem_specs(8),
+        scratch_shapes=[
+            *buffers(16, 1536, bf16),
+            *buffers(16, 2560, bf16),
+            *buffers(64, 512, bf16),
+            *buffers(8, 256, f32),
+            pltpu.VMEM((8, 16, 16, 128), f32),
+            pltpu.VMEM((16, 8, 16, 128), bf16),
+            pltpu.VMEM((16, 8, 16, 128), bf16),
+            pltpu.VMEM((16, 4, 16, 128), bf16),
+            pltpu.VMEM((rows, 1536), bf16),
+            dma((4, 9 * nz)),
+            dma((4, 9 * nz)),
+            dma((2, 16)),
+            dma((2, 16)),
+            dma((2,)),
+            dma,
+            dma,
+        ],
+        compiler_params=pltpu.CompilerParams(
+            collective_id=3, has_side_effects=True, vmem_limit_bytes=58 << 20
+        ),
+        name="finish",
+    )(dq, dkv, x, dz1, x1, dur, hid, dfr, omix, dar, gvec, wa)
+
+
+def by_pairs(
+    stream, accumulator, upstream, segment_ids, w_query, w_key, w_value, w_out, w_up, b_up, w_down, b_down,
+    gain_attn, bias_attn, gain_ffn, bias_ffn, gain_final, bias_final,
+):
+    nb = lax.axis_size("blk")
+    n = 4 * nb
+    x = stream.reshape(256, 512)
+    y = accumulator.reshape(256, 512)
+    g = upstream.reshape(256, 512)
+    small = (b_down, gain_attn, bias_attn, gain_ffn, bias_ffn, gain_final, bias_final)
+    row = jnp.concatenate([b_up.astype(f32), *(v.astype(f32) for v in small), jnp.zeros((80,), f32)])
+    seg_row = segment_ids.astype(f32).reshape(256)
+    vec = jnp.concatenate([row[None], seg_row[None], jnp.zeros((6, 256), f32)], axis=0)
+    q, kv, wa, wb, wd, vecs = project(n, nb, x, w_query, w_key, w_value, w_out, w_up, w_down, vec)
+    bup = vecs[:, 0, 0:64].reshape(1, 2048)
+    par = jnp.pad(vecs[:, 0, 64:176].reshape(n, 7, 16).transpose(1, 0, 2).reshape(7, 512), ((0, 1), (0, 0)))
+    me = lax.axis_index("head") * nb + lax.axis_index("blk")
+    pair = me // 2
+    seg = vecs[:, 1].reshape(n, 2, 8, 16).astype(jnp.int32)
+    seg = lax.dynamic_index_in_dim(seg, pair // 8, 1, False)
+    seg_k = seg.transpose(1, 0, 2).reshape(8, 16 * n)
+    seg_q = lax.dynamic_index_in_dim(seg.reshape(n // 2, 2, 8, 16), lax.rem(me, 2), 1, False)
+    seg_q = seg_q.transpose(1, 0, 2).reshape(8, 8 * n)
+    bounds = jnp.stack([seg_k[:, 0], seg_k[:, -1]])
+    o, of, lse, kv2 = attn_fwd(bounds, q.reshape(4, 256, 128), kv.reshape(4096, 128), seg_q, seg_k)
+    do, out, dacc, dz1, x1, dur, hid, dfr, omix, dar, pg, bg = middle(
+        n, nb, o.reshape(4, 16, 16, 128), x, y, g, wb, wd, par, bup
+    )
+    gvec = jnp.concatenate(
+        [bg.reshape(n, 64), pg[0:7].reshape(7, n, 16).transpose(1, 0, 2).reshape(n, 112), jnp.zeros((n, 80), f32)], axis=1
+    )
+    gvec = jnp.pad(gvec[:, None], ((0, 0), (0, 7), (0, 0)))
+    dq, dkv = attn_bwd(bounds, q.reshape(4, 256, 128), do.reshape(4, 256, 128), of, lse, kv2, seg_q)
+    gx, gq, gk, gv, go, gu, gd, gs = finish(
+        n, nb, dq.reshape(4, 16, 16, 128), dkv.reshape(8, 16, 2, 16, 128), x, dz1, x1, dur, hid, dfr, omix, dar, gvec, wa
+    )
+    gs = gs[0]
+    smalls = [gs[64 + 16 * k:80 + 16 * k] for k in range(7)]
+    return (
+        out.reshape(stream.shape), gx.reshape(stream.shape), dacc.reshape(stream.shape),
+        gq, gk, gv, go, gu, gs[0:64], gd, *smalls,
+    )
+
+
+def pairs_fit(mesh, shape):
+    return mesh.shape["head"] == 4 and mesh.shape["blk"] == 8 and shape == (2, 32, 128, 512)
+
+
 def solution(mesh):
+    def step(*args):
+        return run(by_pairs if pairs_fit(mesh, args[0].shape) else local, mesh)(*args)
+
+    return step
+
+
+def run(body, mesh):
     return jax.shard_map(
-        local,
+        body,
         mesh=mesh,
         in_specs=(
             P(None, ("head", "blk"), None, None),

time: 1670 us -> 229 us (0.14)
  waiting for transfers between devices: 816 us -> 0 us
  blocking collectives: 286 us -> 0 us
  local copies, waits for them, and re-layouts: 283 us -> 35.4 us
  Pallas kernels: 0 us -> 188 us
  matrix products: 187 us -> 0 us
  other arithmetic: 34.5 us -> 2.12 us
  starting transfers between devices: 31.8 us -> 0 us
    unnamed x19 -> x0, waiting for transfers between devices: 403 us -> none
    reduce_scatter x7 -> x0, waiting for transfers between devices: 396 us -> none  [the longest x3 340 us: local(): lax.psum_scatter(grad_totals, ('head', 'blk'), scatter_dimension=0, tiled...]
    dynamic_update_slice x64 -> x0, local copies, waits for them, and re-layouts: 213 us -> none  [local(): lax.scan(backward_step, jnp.zeros((rows, groups, DH), f32), key_blocks(wh...]
    all_gather x6 -> x0, blocking collectives: 191 us -> none  [the longest x1 45.6 us: local(): lax.all_gather(w_query, ('head', 'blk'), axis=0, tiled=True)]
    pallas_call x0 -> x5, Pallas kernels: none -> 188 us  [the longest x1 59.7 us: finish(): pl.pallas_call(functools.partial(finish_kernel, n, nb), out_shape=(wide(r...]
    dot_general x148 -> x0, matrix products: 187 us -> none  [the longest x32 51.1 us: block_scores(): jnp.einsum('sgd,kgd->sgk', queries, key_rows, preferred_element_type=jnp....]
    unnamed x2 -> x0, blocking collectives: 76 us -> none
    all_to_all x8 -> x0, starting transfers between devices: 30.3 us -> none  [the longest x2 8.64 us: local(): lax.all_to_all(attn_send, 'head', split_axis=0, concat_axis=1, tiled=True)]
  transfers between devices with their start and end apart: 24 -> 0, of which waited for: 12 -> 0; matrix products, arithmetic and copies ran while one was open for 19% -> 0% of each run, Pallas kernels for 0% -> 0%
where the time goes in v1:
time: 229 us; the launch traced here: 227 us
  Pallas kernels  188 us (82%)
  local copies, waits for them, and re-layouts  35.4 us (15%)
    pallas_call x1, Pallas kernels, finish(): pl.pallas_call(functools.partial(finish_kernel, n, nb), out_shape=(wide(r...  59.7 us
    pallas_call x1, Pallas kernels, project(): pl.pallas_call(functools.partial(project_kernel, n, nb), out_shape=(jax.S...  54.5 us
    pallas_call x1, Pallas kernels, middle(): pl.pallas_call(functools.partial(middle_kernel, n, nb), out_shape=(jax.Sh...  29.4 us
    unnamed x67, local copies, waits for them, and re-layouts  23.7 us
    pallas_call x1, Pallas kernels, attn_bwd(): pl.pallas_call(attn_bwd_kernel, out_shape=(jax.ShapeDtypeStruct(q.shape,...  23.1 us
    pallas_call x1, Pallas kernels, attn_fwd(): pl.pallas_call(attn_fwd_kernel, out_shape=(jax.ShapeDtypeStruct(q.shape,...  21.5 us
    concatenate x1, local copies, waits for them, and re-layouts, by_pairs(): jnp.concatenate([b_up.astype(f32), *(v.astype(f32) for v in small), jnp.z...  5.43 us

profile of v1, /device:TPU:0, one launch (start us, length us, event | category | flops | bytes accessed | tf_op | source)
XLA Modules:
  0.0 226.8 jit_solution(1975624208410593867)
XLA Ops:
  0.7 5.4 %concatenate.9 = f32[256]{0:T(256)S(1)} concatenate(bf16[64]{0:T(256)(128)(2,1)} %param.27, bf16[16]{0:T(256)(128)(2,1)} %param.29, bf16[16]{0:T(256)(128)(2,1)} %param.30, bf16[16]{0:T(256)(128)(2,1)} %param.31, bf16[16]{0:T(256)(128)(2,1)} %param.32, bf16[16]{0:T(256)(128)(2,1)} %param.33, bf16[16]{0:T(256)(128)(2,1)} %param.34, bf16[16]{0:T(256)(128)(2,1)} %param.35, ...), dimensions={0} | concatenate | bytes 1696 | tf_op jit(solution)/shard_map/concatenate | solution.py:1236
  7.0 0.9 copy-done.1
  7.9 0.8 copy-done.16
  8.8 0.8 copy-done.17
  9.6 0.7 copy-done.18
  10.3 0.7 copy-done.19
  11.0 0.7 copy-done.20
  12.5 54.5 %project.1 = (bf16[4,16,16,128]{3,2,1,0:T(8,128)(2,1)S(1)}, bf16[8,16,2,16,128]{4,3,2,1,0:T(8,128)(2,1)S(1)}, bf16[32,16,1536]{2,1,0:T(8,128)(2,1)S(1)}, bf16[32...) custom-call(bf16[256,512]{1,0:T(8,128)(2,1)S(1)} %bitcast.56, ...), custom_call_target="tpu_custom_call" | custom-call | tf_op jit(solution)/shard_map/project/pallas_call | solution.py:915
  67.0 1.5 copy-done
  68.5 1.4 copy-done.3
  69.9 1.2 copy-done.4
  71.1 1.0 copy-done.5
  74.9 21.5 %attn_fwd.1 = (bf16[4,256,128]{2,1,0:T(8,128)(2,1)}, f32[4,256,128]{2,1,0:T(8,128)}, f32[8,256]{1,0:T(8,128)}, bf16[4096,256]{1,0:T(8,128)(2,1)}) custom-call(s32[2,8]{1,0:T(2,128)} %pad_add_fusion.bounds, bf16[4,256,128]{2,1,0:T(8,128)(2,1)} %bitcast.59, bf16[4096,128]{1,0:T(8,128)(2,1)} %bitcast.58, s32[8,256]{1,0:T(8,128)} %reshape.107.seg_q_ref, ...), custom_call_target="tpu_custom_call" | custom-call | tf_op jit(solution)/shard_map/attn_fwd/pallas_call | solution.py:429
  97.0 0.9 copy-done.15
  97.9 29.4 %middle.1 = (bf16[4,16,16,128]{3,2,1,0:T(8,128)(2,1)S(1)}, bf16[256,512]{1,0:T(8,128)(2,1)S(1)}, f32[256,512]{1,0:T(8,128)S(1)}, f32[256,512]{1,0:T(8,128)S(1)},...) custom-call(bf16[4,16,16,128]{3,2,1,0:T(8,128)(2,1)S(1)} %bitcast.65, ...), custom_call_target="tpu_custom_call" | custom-call | tf_op jit(solution)/shard_map/middle/pallas_call | solution.py:1065
  127.3 0.8 copy-done.7
  128.8 0.7 copy-done.11
  133.4 0.7 pad.9.gv_ref
  134.1 23.1 %attn_bwd.1 = (bf16[4,256,128]{2,1,0:T(8,128)(2,1)}, f32[4096,128]{1,0:T(8,128)}) custom-call(s32[2,8]{1,0:T(2,128)} %pad_add_fusion.bounds, bf16[4,256,128]{2,1,0:T(8,128)(2,1)} %bitcast.60, bf16[4,256,128]{2,1,0:T(8,128)(2,1)} %bitcast.64, f32[4,256,128]{2,1,0:T(8,128)} %get-tuple-element.57.of_ref, f32[8,256]{1,0:T(8,128)} %get-tuple-element.58.lse_ref, ...), custom_call_target="tpu_custom_call" | custom-call | tf_op jit(solution)/shard_map/attn_bwd/pallas_call | solution.py:492
  157.2 59.7 %finish.1 = (f32[256,512]{1,0:T(8,128)}, f32[16,512]{1,0:T(8,128)}, f32[16,512]{1,0:T(8,128)}, f32[16,512]{1,0:T(8,128)}, f32[16,512]{1,0:T(8,128)}, /*index=5*/...) custom-call(bf16[4,16,16,128]{3,2,1,0:T(8,128)(2,1)} %bitcast.74, f32[8,16,2,16,128]{4,3,2,1,0:T(8,128)} %bitcast.68, ...), custom_call_target="tpu_custom_call" | custom-call | tf_op jit(solution)/shard_map/finish/pallas_call | solution.py:1193
  217.0 1.4 slice_bitcast_fusion
  218.5 1.2 slice_bitcast_fusion.7
  220.3 1.9 copy.82
  222.2 0.8 copy.83
  (85 shorter events, 13.7 us)
Async XLA Ops:
  7.0 0.9 copy-start.1
  7.9 0.8 copy-start.16
  8.8 0.8 copy-start.17
  9.6 0.7 copy-start.18
  10.3 0.7 copy-start.19
  11.0 0.7 copy-start.20
  11.8 0.7 copy-start.21
  12.5 84.5 %copy-start.2 = (bf16[2,1,128,512]{3,2,1,0:T(8,128)(2,1)S(1)}, bf16[2,1,128,512]{3,2,1,0:T(8,128)(2,1)}, u32[]{:S(2)}) copy-start(bf16[2,1,128,512]{3,2,1,0:T(8,128)(2,1)} %param.18) | copy-start | bytes 786436
  12.5 84.5 %copy-start.8 = (bf16[2,1,128,512]{3,2,1,0:T(8,128)(2,1)S(1)}, bf16[2,1,128,512]{3,2,1,0:T(8,128)(2,1)}, u32[]{:S(2)}) copy-start(bf16[2,1,128,512]{3,2,1,0:T(8,128)(2,1)} %param.19) | copy-start | bytes 786436
  12.5 84.5 %copy-start.9 = (bf16[2,1,128,512]{3,2,1,0:T(8,128)(2,1)S(1)}, bf16[2,1,128,512]{3,2,1,0:T(8,128)(2,1)}, u32[]{:S(2)}) copy-start(bf16[2,1,128,512]{3,2,1,0:T(8,128)(2,1)} %param.20) | copy-start | bytes 786436
  67.0 1.5 copy-start
  68.5 1.4 copy-start.3
  69.9 1.2 copy-start.4
  71.1 1.0 copy-start.5
  74.1 0.8 copy-start.24
  96.9 1.0 copy-start.15
  127.3 0.8 copy-start.7
  128.8 0.7 copy-start.11
  217.0 6.0 %copy-start.28 = (f32[16,512]{1,0:T(8,128)S(1)}, f32[16,512]{1,0:T(8,128)}, u32[]{:S(2)}) copy-start(f32[16,512]{1,0:T(8,128)} %get-tuple-element.178) | copy-start | bytes 98308
  217.0 6.7 %copy-start.27 = (f32[16,512]{1,0:T(8,128)S(1)}, f32[16,512]{1,0:T(8,128)}, u32[]{:S(2)}) copy-start(f32[16,512]{1,0:T(8,128)} %get-tuple-element.179) | copy-start | bytes 98308
  217.0 7.3 %copy-start.26 = (f32[16,512]{1,0:T(8,128)S(1)}, f32[16,512]{1,0:T(8,128)}, u32[]{:S(2)}) copy-start(f32[16,512]{1,0:T(8,128)} %get-tuple-element.180) | copy-start | bytes 98308
  217.0 7.9 %copy-start.25 = (f32[16,512]{1,0:T(8,128)S(1)}, f32[16,512]{1,0:T(8,128)}, u32[]{:S(2)}) copy-start(f32[16,512]{1,0:T(8,128)} %get-tuple-element.181) | copy-start | bytes 98308
  217.0 8.5 %copy-start.23 = (f32[16,2048]{1,0:T(8,128)S(1)}, f32[16,2048]{1,0:T(8,128)}, u32[]{:S(2)}) copy-start(f32[16,2048]{1,0:T(8,128)} %get-tuple-element.182) | copy-start | bytes 393220
  217.0 9.1 %copy-start.22 = (f32[64,512]{1,0:T(8,128)S(1)}, f32[64,512]{1,0:T(8,128)}, u32[]{:S(2)}) copy-start(f32[64,512]{1,0:T(8,128)} %get-tuple-element.184) | copy-start | bytes 393220
  (5 other events, 3.5 us)

commit v2 on v1

--- a/solution.py
+++ b/solution.py
@@ -12,6 +12,7 @@
 f32, bf16 = jnp.float32, jnp.bfloat16
 MESH = pl.DeviceIdType.MESH
 FAR = -1e30
+VMEM_BYTES = 60 << 20
 
 
 EPSILON = 1e-05
@@ -373,7 +374,14 @@
         wide = pltpu.roll(wide, 64, 1)
     return jnp.where(lanes(wide.shape) < 64, wide, 0.0).astype(bf16)
 
-def attn_fwd_kernel(bounds, q_ref, kv_ref, seg_q_ref, seg_k_ref, o_ref, of_ref, lse_ref, kv2_ref, vo_ref):
+def attn_fwd_kernel(
+    q_hbm, kv_hbm, seg_q_hbm, seg_k_hbm, o_hbm, of_hbm, lse_hbm, kv2_hbm,
+    q_ref, kv_ref, seg_q_ref, seg_k_ref, bounds, o_ref, of_ref, lse_ref, kv2_ref, vo_ref, in_sem, out_sem,
+):
+    loads = copies(
+        [(seg_q_hbm, seg_q_ref), (seg_k_hbm, seg_k_ref), (seg_k_hbm, bounds), (kv_hbm, kv_ref), (q_hbm, q_ref)], in_sem
+    )
+    wait_all(loads)
     chunks, keys = seg_k_ref.shape
     log_scale = math.log2(math.e) * DH ** (-0.5)
 
@@ -387,6 +395,7 @@
         return c
 
     lax.fori_loop(0, chunks, prepare, 0)
+    stores = copies([(kv2_ref, kv2_hbm)], out_sem)
 
     def tile(j, c):
         q_tile = q_ref[j]
@@ -396,9 +405,9 @@
             i = half * (chunks // 2) + j
             left = half_lanes(q_tile, half)
             left = jnp.concatenate([left, query_marks(seg_q_ref[pl.ds(i, 1), :])], axis=1)
-            low, high = bounds[0, i], bounds[1, i]
-            first = lax.fori_loop(0, chunks, lambda t, n: n + jnp.where(bounds[1, t] < low, 1, 0), 0)
-            last = lax.fori_loop(0, chunks, lambda t, n: n + jnp.where(bounds[0, t] <= high, 1, 0), 0)
+            low, high = bounds[i, 0], bounds[i, keys - 1]
+            first = lax.fori_loop(0, chunks, lambda t, n: n + jnp.where(bounds[t, keys - 1] < low, 1, 0), 0)
+            last = lax.fori_loop(0, chunks, lambda t, n: n + jnp.where(bounds[t, 0] <= high, 1, 0), 0)
 
             def step(t, carry):
                 top, acc = carry
@@ -422,30 +431,49 @@
         return c
 
     lax.fori_loop(0, chunks // 2, tile, 0)
-
-def attn_fwd(bounds, q, kv, seg_q, seg_k):
+    stores += copies([(o_ref, o_hbm), (of_ref, of_hbm), (lse_ref, lse_hbm)], out_sem.at[pl.ds(1, 3)])
+    wait_all(stores)
+
+
+def attn_fwd(q, kv, seg_q, seg_k):
     chunks, keys = seg_k.shape
-    vm = pl.BlockSpec(memory_space=pltpu.VMEM)
+    dma = pltpu.SemaphoreType.DMA
+    shapes = ((q.shape, bf16), (q.shape, f32), (seg_q.shape, f32), ((chunks * keys, 256), bf16))
     return pl.pallas_call(
         attn_fwd_kernel,
-        out_shape=(
-            jax.ShapeDtypeStruct(q.shape, bf16),
-            jax.ShapeDtypeStruct(q.shape, f32),
-            jax.ShapeDtypeStruct(seg_q.shape, f32),
-            jax.ShapeDtypeStruct((chunks * keys, 256), bf16),
-        ),
-        in_specs=[pl.BlockSpec(memory_space=pltpu.SMEM), vm, vm, vm, vm],
-        out_specs=(vm, vm, vm, vm),
-        scratch_shapes=[pltpu.VMEM((chunks * keys, 128), bf16)],
-        compiler_params=pltpu.CompilerParams(vmem_limit_bytes=56 << 20),
+        out_shape=[jax.ShapeDtypeStruct(shape, kind) for shape, kind in shapes],
+        in_specs=any_specs(4),
+        out_specs=any_specs(4),
+        scratch_shapes=[
+            *[pltpu.VMEM(a.shape, a.dtype) for a in (q, kv, seg_q, seg_k)],
+            pltpu.SMEM(seg_k.shape, jnp.int32),
+            *[pltpu.VMEM(shape, kind) for shape, kind in shapes],
+            pltpu.VMEM((chunks * keys, 128), bf16),
+            dma((5,)),
+            dma((4,)),
+        ],
+        compiler_params=pltpu.CompilerParams(vmem_limit_bytes=VMEM_BYTES),
         name="attn_fwd",
-    )(bounds, q, kv, seg_q, seg_k)
-
-def attn_bwd_kernel(bounds, q_ref, do_ref, of_ref, lse_ref, kv2_ref, seg_q_ref, dq_ref, dkv_ref):
-    chunks = seg_q_ref.shape[0]
-    keys = kv2_ref.shape[0] // chunks
+    )(q, kv, seg_q, seg_k)
+
+
+def attn_bwd_kernel(
+    q_hbm, do_hbm, of_hbm, lse_hbm, kv2_hbm, seg_q_hbm, seg_k_hbm, pass1, pass2, dq_hbm, dkv_hbm, out1, out2,
+    q_ref, do_ref, of_ref, lse_ref, kv2_ref, seg_q_ref, bounds, dq_ref, dkv_ref, hold1, hold2, in_sem, out_sem,
+):
+    loads = copies(
+        [
+            (q_hbm, q_ref), (do_hbm, do_ref), (of_hbm, of_ref), (lse_hbm, lse_ref), (kv2_hbm, kv2_ref),
+            (seg_q_hbm, seg_q_ref), (seg_k_hbm, bounds),
+            (pass1, hold1), (pass2, hold2),
+        ],
+        in_sem,
+    )
+    dkv_ref[...] = jnp.zeros_like(dkv_ref)
+    wait_all(loads)
+    stores = copies([(hold1, out1), (hold2, out2)], out_sem)
+    chunks, keys = bounds.shape
     log_scale = math.log2(math.e) * DH ** (-0.5)
-    dkv_ref[...] = jnp.zeros_like(dkv_ref)
 
     def tile(j, c):
         q_tile, do_tile = q_ref[j], do_ref[j]
@@ -465,9 +493,9 @@
             both = jnp.concatenate([left, grad], axis=0)
             marks = query_marks(seg_q_ref[pl.ds(i, 1), :])
             right = jnp.concatenate([both, jnp.concatenate([marks, jnp.zeros_like(marks)], axis=0)], axis=1)
-            low, high = bounds[0, i], bounds[1, i]
-            first = lax.fori_loop(0, chunks, lambda t, n: n + jnp.where(bounds[1, t] < low, 1, 0), 0)
-            last = lax.fori_loop(0, chunks, lambda t, n: n + jnp.where(bounds[0, t] <= high, 1, 0), 0)
+            low, high = bounds[i, 0], bounds[i, keys - 1]
+            first = lax.fori_loop(0, chunks, lambda t, n: n + jnp.where(bounds[t, keys - 1] < low, 1, 0), 0)
+            last = lax.fori_loop(0, chunks, lambda t, n: n + jnp.where(bounds[t, 0] <= high, 1, 0), 0)
 
             def step(t, dq):
                 at = pl.ds(pl.multiple_of(t * keys, keys), keys)
@@ -486,20 +514,30 @@
     lax.fori_loop(0, chunks // 2, tile, 0)
     dkv = dkv_ref[...]
     dkv_ref[...] = jnp.where(lanes(dkv.shape) < 64, dkv * DH ** (-0.5), dkv)
-
-def attn_bwd(bounds, q, do, of, lse, kv2, seg_q):
-    vm = pl.BlockSpec(memory_space=pltpu.VMEM)
+    stores += copies([(dq_ref, dq_hbm), (dkv_ref, dkv_hbm)], out_sem.at[pl.ds(2, 2)])
+    wait_all(stores)
+
+
+def attn_bwd(q, do, of, lse, kv2, seg_q, seg_k, pass1, pass2):
+    dma = pltpu.SemaphoreType.DMA
+    shapes = ((q.shape, bf16), ((kv2.shape[0], 128), f32))
     return pl.pallas_call(
         attn_bwd_kernel,
-        out_shape=(
-            jax.ShapeDtypeStruct(q.shape, bf16),
-            jax.ShapeDtypeStruct((kv2.shape[0], 128), f32),
-        ),
-        in_specs=[pl.BlockSpec(memory_space=pltpu.SMEM), vm, vm, vm, vm, vm, vm],
-        out_specs=(vm, vm),
-        compiler_params=pltpu.CompilerParams(vmem_limit_bytes=56 << 20),
+        out_shape=[jax.ShapeDtypeStruct(shape, kind) for shape, kind in shapes]
+        + [jax.ShapeDtypeStruct(a.shape, a.dtype) for a in (pass1, pass2)],
+        in_specs=any_specs(9),
+        out_specs=any_specs(4),
+        scratch_shapes=[
+            *[pltpu.VMEM(a.shape, a.dtype) for a in (q, do, of, lse, kv2, seg_q)],
+            pltpu.SMEM(seg_k.shape, jnp.int32),
+            *[pltpu.VMEM(shape, kind) for shape, kind in shapes],
+            *[pltpu.VMEM(a.shape, a.dtype) for a in (pass1, pass2)],
+            dma((9,)),
+            dma((4,)),
+        ],
+        compiler_params=pltpu.CompilerParams(vmem_limit_bytes=VMEM_BYTES),
         name="attn_bwd",
-    )(bounds, q, do, of, lse, kv2, seg_q)
+    )(q, do, of, lse, kv2, seg_q, seg_k, pass1, pass2)
 
 
 class Spot:
@@ -550,11 +588,18 @@
     pl.semaphore_wait(barrier, n - 1)
 
 
+def halves(shape):
+    rows, width = shape
+    if width > 128:
+        return [(slice(None), slice(w * width // 2, (w + 1) * width // 2)) for w in range(2)]
+    return [(slice(w * rows // 2, (w + 1) * rows // 2), slice(None)) for w in range(2)]
+
+
 class Gather:
     def __init__(self, spot, shard, full, send, recv, local):
         self.s, self.shard, self.full, self.local = spot, shard, full, local
         self.send, self.recv = send, recv
-        self.half = shard.shape[-1] // 2
+        self.cut = halves(shard.shape)
 
     def copy(self, src, dst, k, h, z, c, recv_k=None):
         recv_k = k if recv_k is None else recv_k
@@ -580,7 +625,7 @@
         return self.copy(slot, slot, (1 + w) * s.nz + z, s.near[w], s.z, s.c)
 
     def lanes(self, slot, w):
-        return slot.at[:, pl.ds(w * self.half, self.half)]
+        return slot.at[self.cut[w]]
 
     def onward(self, w, z):
         s = self.s
@@ -668,7 +713,8 @@
     def __init__(self, spot, part, twin, diag, near, line, send, recv):
         self.s, self.part, self.t, self.d, self.n, self.l = spot, part, twin, diag, near, line
         self.send, self.recv = send, recv
-        self.half = part.shape[-1] // 2
+        self.cut = halves(part.shape[1:])
+        self.axis = 1 if self.cut[0][0] == slice(None) else 0
 
     def copy(self, src, dst, k, h, z, c, recv_k=None):
         recv_k = k if recv_k is None else recv_k
@@ -677,9 +723,6 @@
     def mine(self, h, z):
         return self.s.index(h, z, self.s.c)
 
-    def lanes(self, w):
-        return pl.ds(w * self.half, self.half)
-
     def to_twin(self, h, z):
         s = self.s
         src = self.part.at[s.index(h, z, 1 - s.c)]
@@ -687,7 +730,7 @@
 
     def to_diag(self, w, z):
         s = self.s
-        src = self.part.at[self.mine(s.diag, z), :, self.lanes(w)]
+        src = self.part.at[self.mine(s.diag, z)].at[self.cut[w]]
         return self.copy(src, self.d.at[w, z], (4 + w) * s.nz + z, s.near[w], s.z, s.c)
 
     def to_near(self, w, z):
@@ -735,10 +778,9 @@
                 value = self.pair(s.near[w], z)
                 self.to_diag(1 - w, z).wait_recv()
                 other = self.d[1 - w, z].astype(f32)
-                if w == 0:
-                    value = jnp.concatenate([value[:, : self.half], value[:, self.half :] + other], axis=1)
-                else:
-                    value = jnp.concatenate([value[:, : self.half] + other, value[:, self.half :]], axis=1)
+                pieces = [value[cut] for cut in self.cut]
+                pieces[1 - w] = pieces[1 - w] + other
+                value = jnp.concatenate(pieces, axis=self.axis)
                 self.keep(s.near[w], z, value)
                 self.to_near(w, z).start()
 
@@ -830,40 +872,87 @@
     return [pl.BlockSpec(memory_space=pl.ANY)] * count
 
 
-def vmem_specs(count):
-    return [pl.BlockSpec(memory_space=pltpu.VMEM)] * count
-
-
-def project_kernel(
-    n, nb, x_ref, wq_ref, wk_ref, wv_ref, wo_ref, wu_ref, wd_ref, vec_ref,
-    q_out, kv_out, wa_out, wb_out, wd_out, vec_out,
-    sa, sb, wa, kv_send, q_send, ag_send, ag_recv, ag_local, ex_send, ex_recv, ex_local,
-    tw_send, tw_recv, out_sem,
-):
+def copies(pairs, sems):
+    jobs = [pltpu.make_async_copy(src, dst, sems.at[k]) for k, (src, dst) in enumerate(pairs)]
+    for job in jobs:
+        job.start()
+    return jobs
+
+
+def wait_all(jobs):
+    for job in jobs:
+        job.wait()
+
+
+def rows_of(shape):
+    return lax.broadcasted_iota(jnp.int32, shape, 0)
+
+
+def spread_row(block, width, each_lane):
+    count = block.shape[0]
+    pick = (rows_of((128, width)) == lax.rem(lanes((128, width)), each_lane)).astype(f32).astype(bf16)
+    wide = dot_n(block.astype(bf16), pick)
+    return column_sum(jnp.where(rows_of((count, width)) == lanes((count, width)) // each_lane, wide, 0.0))
+
+
+def gather_row(row, count, each_lane):
+    width = row.shape[1]
+    wide = jnp.where(rows_of((count, width)) == lanes((count, width)) // each_lane, row, 0.0)
+    pick = (lanes((width, 128)) == lax.rem(rows_of((width, 128)), each_lane)).astype(f32)
+    return lax.dot_general(
+        wide, pick, (((1,), (0,)), ((), ())), precision=lax.Precision.HIGHEST, preferred_element_type=f32
+    )
+
+
+def project_kernel(n, nb, *refs):
+    x_hbm, wq_hbm, wk_hbm, wv_hbm, wo_hbm, wu_hbm, wd_hbm, seg_hbm = refs[:8]
+    smalls = refs[8:16]
+    q_out, kv_out, wa_out, wb_out, wd_out, par_out, bup_out, segk_out, segq_out = refs[16:25]
+    (
+        x, wq, wk, wv, wo, wu, wd, seg, *small, bup_small, vec, vecs, sa, sb, wa, kv_send, q_send, par, bup, segk, segq,
+        in_sem, out_sem, ag_send, ag_recv, ag_local, ex_send, ex_recv, ex_local, tw_send, tw_recv,
+    ) = refs[25:]
     s = Spot(nb)
+    loads = copies(
+        [(wq_hbm, wq), (wk_hbm, wk), (wv_hbm, wv), (seg_hbm, seg), (smalls[0], bup_small)]
+        + [(smalls[k], small[k - 1]) for k in range(1, 8)]
+        + [(wo_hbm, wo), (wu_hbm, wu), (wd_hbm, wd), (x_hbm, x)],
+        in_sem,
+    )
     greet_all(n, nb, s.me)
+    wait_all(loads[:12])
     for t in range(4):
         tile = slice(128 * t, 128 * t + 128)
-        first, second = weave(wk_ref[:, tile], wv_ref[:, tile])
+        first, second = weave(wk[:, tile], wv[:, tile])
         sa[:, 256 * t:256 * t + 128] = first
         sa[:, 256 * t + 128:256 * t + 256] = second
-    sa[:, 1024:1536] = wq_ref[...]
-    sb[:, 0:512] = wo_ref[...]
-    sb[:, 512:2560] = wu_ref[...]
+    sa[:, 1024:1536] = wq[...]
+    vec[...] = jnp.zeros_like(vec)
+    vec[0:1, 0:64] = bup_small[...].astype(f32).reshape(1, 64)
+    for k in range(7):
+        vec[k + 1:k + 2, 0:16] = small[k][...].astype(f32).reshape(1, 16)
+    vec[8:10, :] = seg[...].astype(f32)
     jobs = [
         Gather(s, shard, full, ag_send.at[k], ag_recv.at[k], ag_local.at[k])
-        for k, (shard, full) in enumerate(((sa, wa), (sb, wb_out), (wd_ref, wd_out), (vec_ref, vec_out)))
+        for k, (shard, full) in enumerate(((sa, wa), (vec, vecs), (sb, wb_out), (wd, wd_out)))
     ]
-    jobs[0].begin()
-    jobs[0].spread()
-    jobs[0].cross()
-    jobs[0].last()
-    for job in jobs[1:]:
+    for job in jobs[:2]:
         job.begin()
-    jobs[0].arrive()
-    keep = pltpu.make_async_copy(wa, wa_out, out_sem)
-    keep.start()
-    qkv = dot_n(x_ref[...], wa[...].reshape(512, 1536)).astype(bf16)
+    wait_all(loads[12:])
+    sb[:, 0:512] = wo[...]
+    sb[:, 512:2560] = wu[...]
+    for job in jobs[:2]:
+        job.spread()
+    for job in jobs[:2]:
+        job.cross()
+    for job in jobs[:2]:
+        job.last()
+    for job in jobs[2:]:
+        job.begin()
+    for job in jobs[:2]:
+        job.arrive()
+    outs = copies([(wa, wa_out)], out_sem)
+    qkv = dot_n(x[...], wa[...].reshape(512, 1536)).astype(bf16)
     for m in range(2):
         rows = slice(128 * m, 128 * m + 128)
         for h in range(8):
@@ -879,9 +968,24 @@
     q_ex = Exchange(s, lambda p: q_send.at[p], lambda g: q_out.at[:, g], ex_send.at[1], ex_recv.at[1], ex_local.at[1])
     kv_ex.begin()
     q_ex.begin()
-    for job in jobs[1:]:
+    for job in jobs[2:]:
         job.spread()
-    for job in jobs[1:]:
+    bup[...] = spread_row(vecs[:, 0, :], 2048, 64)
+    for k in range(7):
+        par[k:k + 1, :] = spread_row(vecs[:, k + 1, :], 512, 16)
+    par[7:8, :] = jnp.zeros((1, 512), f32)
+    ids = jnp.where(kv_ex.g < 8, vecs[:, 8, :], vecs[:, 9, :]).astype(bf16)
+    for i in range(8):
+        pick = (rows_of((128, 512)) == 16 * i + lax.rem(lanes((128, 512)), 16)).astype(f32).astype(bf16)
+        wide = dot_n(ids, pick)
+        source = rows_of((n, 512))
+        row = jnp.where(source == lanes((n, 512)) // 16, wide, 0.0)
+        segk[i:i + 1, :] = column_sum(row).astype(jnp.int32)
+        source = rows_of((n, 256))
+        own = (source // 2 == lanes((n, 256)) // 16) & (lax.rem(source, 2) == s.c)
+        segq[i:i + 1, :] = column_sum(jnp.where(own, wide[:, 0:256], 0.0)).astype(jnp.int32)
+    outs += copies([(par, par_out), (bup, bup_out), (segk, segk_out), (segq, segq_out)], out_sem.at[pl.ds(1, 4)])
+    for job in jobs[2:]:
         job.cross()
 
     def twin(g, c):
@@ -896,9 +1000,9 @@
         twin(lax.rem(kv_ex.g + 16 - i, 16), s.c).start()
 
     each(16, forward, 1)
-    for job in jobs[1:]:
+    for job in jobs[2:]:
         job.last()
-    for job in jobs[1:]:
+    for job in jobs[2:]:
         job.arrive()
     each(16, lambda g: twin(g, 1 - s.c).wait_recv())
     each(16, lambda g: twin(g, s.c).wait_send())
@@ -906,10 +1010,10 @@
     q_ex.end()
     for job in jobs:
         job.sent()
-    keep.wait()
-
-
-def project(n, nb, x, wq, wk, wv, wo, wu, wd, vec):
+    wait_all(outs)
+
+
+def project(n, nb, x, wq, wk, wv, wo, wu, wd, seg, smalls):
     dma = pltpu.SemaphoreType.DMA
     nz = nb // 2
     return pl.pallas_call(
@@ -920,16 +1024,37 @@
             jax.ShapeDtypeStruct((n, 16, 1536), bf16),
             jax.ShapeDtypeStruct((n, 16, 2560), bf16),
             jax.ShapeDtypeStruct((n, 64, 512), bf16),
-            jax.ShapeDtypeStruct((n, 8, 256), f32),
+            jax.ShapeDtypeStruct((8, 512), f32),
+            jax.ShapeDtypeStruct((1, 2048), f32),
+            jax.ShapeDtypeStruct((8, 512), jnp.int32),
+            jax.ShapeDtypeStruct((8, 256), jnp.int32),
         ),
-        in_specs=vmem_specs(8),
-        out_specs=any_specs(6),
+        in_specs=any_specs(16),
+        out_specs=any_specs(9),
         scratch_shapes=[
+            pltpu.VMEM(x.shape, bf16),
+            pltpu.VMEM((16, 512), bf16),
+            pltpu.VMEM((16, 512), bf16),
+            pltpu.VMEM((16, 512), bf16),
+            pltpu.VMEM((16, 512), bf16),
+            pltpu.VMEM((16, 2048), bf16),
+            pltpu.VMEM((64, 512), bf16),
+            pltpu.VMEM((2, 128), jnp.int32),
+            *[pltpu.VMEM((16,), bf16)] * 7,
+            pltpu.VMEM((64,), bf16),
+            pltpu.VMEM((16, 128), f32),
+            pltpu.VMEM((n, 16, 128), f32),
             pltpu.VMEM((16, 1536), bf16),
             pltpu.VMEM((16, 2560), bf16),
             pltpu.VMEM((n, 16, 1536), bf16),
             pltpu.VMEM((16, 8, 16, 128), bf16),
             pltpu.VMEM((16, 4, 16, 128), bf16),
+            pltpu.VMEM((8, 512), f32),
+            pltpu.VMEM((1, 2048), f32),
+            pltpu.VMEM((8, 512), jnp.int32),
+            pltpu.VMEM((8, 256), jnp.int32),
+            dma((16,)),
+            dma((5,)),
             dma((4, 9 * nz)),
             dma((4, 9 * nz)),
             dma((4,)),
@@ -938,13 +1063,12 @@
             dma((2,)),
             dma((16,)),
             dma((16,)),
-            dma,
         ],
         compiler_params=pltpu.CompilerParams(
-            collective_id=1, has_side_effects=True, vmem_limit_bytes=40 << 20
+            collective_id=1, has_side_effects=True, vmem_limit_bytes=VMEM_BYTES
         ),
         name="project",
-    )(x, wq, wk, wv, wo, wu, wd, vec)
+    )(x, wq, wk, wv, wo, wu, wd, seg, *smalls)
 
 
 def row_norm(v):
@@ -967,54 +1091,58 @@
     return jnp.sum(v, axis=0, keepdims=True)
 
 
-def middle_kernel(
-    n, nb, o_ref, x_ref, y_ref, g_ref, wb_hbm, wd_hbm, par_ref, bup_ref,
-    do_out, out_ref, dacc_ref, dz1_ref, x1_ref, dur_ref, h_ref, dfr_ref, omix_ref, dar_ref, pg_ref, bg_ref,
-    wb, wd, o_recv, do_send, slope, ex_send, ex_recv, ex_local, in_sem,
-):
+def middle_kernel(n, nb, *refs):
+    o_hbm, x_hbm, y_hbm, g_hbm, wb_hbm, wd_hbm, par_hbm, bup_hbm = refs[:8]
+    outs_hbm = refs[9:20]
+    do_out = refs[8]
+    (
+        o_in, x, y, g_in, wb, wd, par, bup, o_recv, do_send, slope,
+        out, dacc_ref, dz1_ref, x1_ref, dur_ref, hid_ref, dfr_ref, omix, dar_ref, gvec, bias_up,
+        in_sem, out_sem, ex_send, ex_recv, ex_local,
+    ) = refs[20:]
     s = Spot(nb)
-    load_b = pltpu.make_async_copy(wb_hbm, wb, in_sem.at[0])
-    load_d = pltpu.make_async_copy(wd_hbm, wd, in_sem.at[1])
-    load_b.start()
-    load_d.start()
+    loads = copies(
+        [(o_hbm, o_in), (x_hbm, x), (y_hbm, y), (g_hbm, g_in), (par_hbm, par), (bup_hbm, bup), (wb_hbm, wb), (wd_hbm, wd)],
+        in_sem,
+    )
     greet_all(n, nb, s.me)
+    loads[0].wait()
     o_ex = Exchange(
-        s, lambda p: o_ref.at[:, p], lambda g: o_recv.at[g], ex_send.at[0], ex_recv.at[0], ex_local.at[0]
+        s, lambda p: o_in.at[:, p], lambda g: o_recv.at[g], ex_send.at[0], ex_recv.at[0], ex_local.at[0]
     )
     o_ex.begin()
-    load_b.wait()
-    load_d.wait()
+    wait_all(loads[1:])
     o_ex.end()
     for m in range(2):
         for t in range(4):
             first, second = weave(
                 o_recv[8 * m + 2 * t].reshape(64, 128), o_recv[8 * m + 2 * t + 1].reshape(64, 128)
             )
-            omix_ref[128 * m:128 * m + 64, 128 * t:128 * t + 128] = first
-            omix_ref[128 * m + 64:128 * m + 128, 128 * t:128 * t + 128] = second
-    gain1, bias1 = par_ref[1:2], par_ref[2:3]
-    gain2, bias2 = par_ref[3:4], par_ref[4:5]
-    gain3, bias3 = par_ref[5:6], par_ref[6:7]
+            omix[128 * m:128 * m + 64, 128 * t:128 * t + 128] = first
+            omix[128 * m + 64:128 * m + 128, 128 * t:128 * t + 128] = second
+    gain1, bias1 = par[1:2], par[2:3]
+    gain2, bias2 = par[3:4], par[4:5]
+    gain3, bias3 = par[5:6], par[6:7]
     w_out = wb[:, :, 0:512].reshape(512, 512)
-    a = dot_n(omix_ref[...], w_out)
-    n1, r1 = row_norm(x_ref[...].astype(f32) + a)
+    a = dot_n(omix[...], w_out)
+    n1, r1 = row_norm(x[...].astype(f32) + a)
     x1 = n1 * gain1 + bias1
     x1r = x1.astype(bf16)
     x1_ref[...] = x1r
     feed = jnp.zeros_like(x1)
     for t in range(4):
         cols = slice(512 * t, 512 * t + 512)
-        u = dot_n(x1r, wb[:, :, 512 + 512 * t:1024 + 512 * t].reshape(512, 512)) + bup_ref[:, cols]
+        u = dot_n(x1r, wb[:, :, 512 + 512 * t:1024 + 512 * t].reshape(512, 512)) + bup[:, cols]
         phi = 0.5 * (1.0 + lax.erf(u * (0.5**0.5)))
         hid = (u * phi).astype(bf16)
         slope[:, cols] = phi + u * jnp.exp(-0.5 * u * u) * ((2.0 * math.pi) ** -0.5)
-        h_ref[:, cols] = hid
+        hid_ref[:, cols] = hid
         feed = feed + dot_n(hid, wd[8 * t:8 * t + 8].reshape(512, 512))
-    feed = feed + par_ref[0:1]
+    feed = feed + par[0:1]
     n2, r2 = row_norm(x1 + feed)
-    n3, r3 = row_norm(y_ref[...].astype(f32) + a + feed)
-    out_ref[...] = (n2 * gain2 + bias2 + (n3 * gain3 + bias3)).astype(bf16)
-    g = g_ref[...].astype(f32)
+    n3, r3 = row_norm(y[...].astype(f32) + a + feed)
+    out[...] = (n2 * gain2 + bias2 + (n3 * gain3 + bias3)).astype(bf16)
+    g = g_in[...].astype(f32)
     dacc = row_norm_back(g, n3, r3, gain3)
     dacc_ref[...] = dacc
     dz2 = row_norm_back(g, n2, r2, gain2)
@@ -1025,7 +1153,7 @@
     for t in range(4):
         cols = slice(512 * t, 512 * t + 512)
         du = dot_t(dfr, wd[8 * t:8 * t + 8].reshape(512, 512)) * slope[:, cols]
-        bg_ref[:, cols] = column_sum(du)
+        bias_up[:, cols] = column_sum(du)
         dur = du.astype(bf16)
         dur_ref[:, cols] = dur
         dx1 = dx1 + dot_t(dur, wb[:, :, 512 + 512 * t:1024 + 512 * t].reshape(512, 512))
@@ -1044,92 +1172,107 @@
         s, lambda p: do_send.at[p], lambda g: do_out.at[:, g], ex_send.at[1], ex_recv.at[1], ex_local.at[1]
     )
     do_ex.begin()
-    pg_ref[0:1] = column_sum(df)
-    pg_ref[1:2] = column_sum(dx1 * n1)
-    pg_ref[2:3] = column_sum(dx1)
-    pg_ref[3:4] = column_sum(g * n2)
-    pg_ref[4:5] = column_sum(g)
-    pg_ref[5:6] = column_sum(g * n3)
-    pg_ref[6:7] = column_sum(g)
-    pg_ref[7:8] = jnp.zeros((1, 512), f32)
+    stores = copies(
+        zip((out, dacc_ref, dz1_ref, x1_ref, dur_ref, hid_ref, dfr_ref, omix, dar_ref), outs_hbm[:9]), out_sem
+    )
+    sum_g = column_sum(g)
+    sums = (
+        column_sum(df), column_sum(dx1 * n1), column_sum(dx1), column_sum(g * n2), sum_g, column_sum(g * n3), sum_g
+    )
+    gvec[...] = jnp.zeros_like(gvec)
+    gvec[:, 0, :] = gather_row(bias_up[...], n, 64)
+    for k in range(7):
+        gvec[:, k + 1, :] = gather_row(sums[k], n, 16)
+    stores += copies([(gvec, outs_hbm[9])], out_sem.at[pl.ds(9, 1)])
     do_ex.end()
+    wait_all(stores)
 
 
 def middle(n, nb, o, x, y, g, wb, wd, par, bup):
     dma = pltpu.SemaphoreType.DMA
     rows = x.shape[0]
-
-    def wide(width, kind):
-        return jax.ShapeDtypeStruct((rows, width), kind)
-
+    saved = [
+        ((rows, 512), bf16), ((rows, 512), f32), ((rows, 512), f32), ((rows, 512), bf16), ((rows, 2048), bf16),
+        ((rows, 2048), bf16), ((rows, 512), bf16), ((rows, 512), bf16), ((rows, 512), bf16), ((n, 16, 128), f32),
+    ]
     return pl.pallas_call(
         functools.partial(middle_kernel, n, nb),
-        out_shape=(
-            jax.ShapeDtypeStruct((4, 16, 16, 128), bf16),
-            wide(512, bf16), wide(512, f32), wide(512, f32), wide(512, bf16), wide(2048, bf16),
-            wide(2048, bf16), wide(512, bf16), wide(512, bf16), wide(512, bf16),
-            jax.ShapeDtypeStruct((8, 512), f32),
-            jax.ShapeDtypeStruct((1, 2048), f32),
-        ),
-        in_specs=vmem_specs(4) + any_specs(2) + vmem_specs(2),
-        out_specs=any_specs(1) + vmem_specs(11),
+        out_shape=[jax.ShapeDtypeStruct((4, 16, 16, 128), bf16)]
+        + [jax.ShapeDtypeStruct(shape, kind) for shape, kind in saved]
+        + [jax.ShapeDtypeStruct((8, 128), f32)],
+        in_specs=any_specs(8),
+        out_specs=any_specs(12),
         scratch_shapes=[
+            pltpu.VMEM(o.shape, bf16),
+            pltpu.VMEM(x.shape, bf16),
+            pltpu.VMEM(x.shape, bf16),
+            pltpu.VMEM(x.shape, bf16),
             pltpu.VMEM(wb.shape, bf16),
             pltpu.VMEM(wd.shape, bf16),
+            pltpu.VMEM(par.shape, f32),
+            pltpu.VMEM(bup.shape, f32),
             pltpu.VMEM((16, 4, 16, 128), bf16),
             pltpu.VMEM((16, 4, 16, 128), bf16),
             pltpu.VMEM((rows, 2048), f32),
+            *[pltpu.VMEM(shape, kind) for shape, kind in saved],
+            pltpu.VMEM((1, 2048), f32),
+            dma((8,)),
+            dma((10,)),
             dma((2, 16)),
             dma((2, 16)),
             dma((2,)),
-            dma((2,)),
         ],
         compiler_params=pltpu.CompilerParams(
-            collective_id=2, has_side_effects=True, vmem_limit_bytes=50 << 20
+            collective_id=2, has_side_effects=True, vmem_limit_bytes=VMEM_BYTES
         ),
         name="middle",
-    )(o, x, y, g, wb, wd, par, bup)
-
-
-def finish_kernel(
-    n, nb, dq_ref, dkv_ref, x_ref, dz1_ref, x1_ref, dur_ref, h_ref, dfr_ref, omix_ref, dar_ref, gv_ref, wa_ref,
-    gx_ref, gq_ref, gk_ref, gv_out, go_ref, gu_ref, gd_ref, gvec_ref,
-    pa, ta, da, na, la, pb, tb, db, nb_, lb, pd, td, dd, nd, ld, pv, tv, dv, nv, lv,
-    twin_buf, dkv_send, dkv_recv, dq_recv, dqkv, rs_send, rs_recv, ex_send, ex_recv, ex_local, tw_send, tw_recv,
-):
+    )(o, x, y, g, wb, wd, par, bup)[:11]
+
+
+def finish_kernel(n, nb, *refs):
+    ins = refs[:12]
+    outs = refs[12:20]
+    (
+        dq, dkv, x, dz1, x1, dur, hid, dfr, omix, dar, gvec, wa,
+        pa, ta, da, na, la, pb, tb, db, nb_, lb, pd, td, dd, nd, ld, tv, dv, nv, lv,
+        twin_buf, dkv_send, dkv_recv, dq_recv, dqkv, gx, gq, gk, gv, go, gu, gd, gs,
+        in_sem, out_sem, rs_send, rs_recv, ex_send, ex_recv, ex_local, tw_send, tw_recv,
+    ) = refs[20:]
     s = Spot(nb)
+    order = (1, 10, 8, 9, 4, 5, 6, 7, 0, 2, 3, 11)
+    local = (dq, dkv, x, dz1, x1, dur, hid, dfr, omix, dar, gvec, wa)
+    loads = copies([(ins[k], local[k]) for k in order], in_sem)
     greet_all(n, nb, s.me)
-    swap = remote(dkv_ref.at[:, :, 1 - s.c], twin_buf, tw_send, tw_recv, s.h, s.z * 2 + 1 - s.c)
+    swap = remote(ins[1].at[:, :, 1 - s.c], twin_buf, tw_send, tw_recv, s.h, s.z * 2 + 1 - s.c)
     swap.start()
     jobs = [
         Scatter(s, *bufs, rs_send.at[k], rs_recv.at[k])
         for k, bufs in enumerate(
-            ((pb, tb, db, nb_, lb), (pd, td, dd, nd, ld), (pv, tv, dv, nv, lv), (pa, ta, da, na, la))
+            ((pb, tb, db, nb_, lb), (pd, td, dd, nd, ld), (gvec, tv, dv, nv, lv), (pa, ta, da, na, la))
         )
     ]
-    pv[...] = gv_ref[...]
+    wait_all(loads[:6])
     jobs[2].begin()
-    pb[:, :, 0:512] = dot_0(omix_ref[...], dar_ref[...]).astype(bf16).reshape(n, 16, 512)
+    pb[:, :, 0:512] = dot_0(omix[...], dar[...]).astype(bf16).reshape(n, 16, 512)
     for t in range(4):
         cols = slice(512 * t, 512 * t + 512)
-        pb[:, :, 512 + 512 * t:1024 + 512 * t] = (
-            dot_0(x1_ref[...], dur_ref[:, cols]).astype(bf16).reshape(n, 16, 512)
-        )
+        pb[:, :, 512 + 512 * t:1024 + 512 * t] = dot_0(x1[...], dur[:, cols]).astype(bf16).reshape(n, 16, 512)
     jobs[0].begin()
+    wait_all(loads[6:])
     for t in range(4):
         cols = slice(512 * t, 512 * t + 512)
-        pd[8 * t:8 * t + 8] = dot_0(h_ref[:, cols], dfr_ref[...]).astype(bf16).reshape(8, 64, 512)
+        pd[8 * t:8 * t + 8] = dot_0(hid[:, cols], dfr[...]).astype(bf16).reshape(8, 64, 512)
     jobs[1].begin()
     swap.wait()
 
     def add(g):
-        dkv_send[g] = (dkv_ref[:, g, s.c] + twin_buf[:, g]).astype(bf16)
+        dkv_send[g] = (dkv[:, g, s.c] + twin_buf[:, g]).astype(bf16)
 
     each(16, add)
     kv_ex = Exchange(
         s, lambda p: dkv_send.at[p], lambda g: dkv_recv.at[g], ex_send.at[0], ex_recv.at[0], ex_local.at[0]
     )
-    q_ex = Exchange(s, lambda p: dq_ref.at[:, p], lambda g: dq_recv.at[g], ex_send.at[1], ex_recv.at[1], ex_local.at[1])
+    q_ex = Exchange(s, lambda p: dq.at[:, p], lambda g: dq_recv.at[g], ex_send.at[1], ex_recv.at[1], ex_local.at[1])
     kv_ex.begin()
     q_ex.begin()
     for job in jobs[:3]:
@@ -1152,25 +1295,29 @@
             dqkv[128 * m + 64:128 * m + 128, 1024 + 128 * t:1152 + 128 * t] = second
     for t in range(3):
         cols = slice(512 * t, 512 * t + 512)
-        pa[:, :, cols] = dot_0(x_ref[...], dqkv[:, cols]).astype(bf16).reshape(n, 16, 512)
+        pa[:, :, cols] = dot_0(x[...], dqkv[:, cols]).astype(bf16).reshape(n, 16, 512)
     jobs[3].begin()
-    gx_ref[...] = dz1_ref[...] + dot_t(dqkv[...], wa_ref[...].reshape(512, 1536))
+    gx[...] = dz1[...] + dot_t(dqkv[...], wa[...].reshape(512, 1536))
+    stores = copies([(gx, outs[0])], out_sem)
     total = jobs[0].total()
-    go_ref[...] = total[:, 0:512]
-    gu_ref[...] = total[:, 512:2560]
-    gd_ref[...] = jobs[1].total()
-    gvec_ref[...] = jobs[2].total()
+    go[...] = total[:, 0:512]
+    gu[...] = total[:, 512:2560]
+    gd[...] = jobs[1].total()
+    gs[...] = jobs[2].total()
+    stores += copies(zip((go, gu, gd, gs), outs[4:8]), out_sem.at[pl.ds(1, 4)])
     jobs[3].first()
     jobs[3].second()
     jobs[3].third()
     total = jobs[3].total()
-    gq_ref[...] = total[:, 1024:1536]
+    gq[...] = total[:, 1024:1536]
     for t in range(4):
         first, second = weave(total[:, 256 * t:256 * t + 128], total[:, 256 * t + 128:256 * t + 256])
-        gk_ref[:, 128 * t:128 * t + 128] = first
-        gv_out[:, 128 * t:128 * t + 128] = second
+        gk[:, 128 * t:128 * t + 128] = first
+        gv[:, 128 * t:128 * t + 128] = second
+    stores += copies(zip((gq, gk, gv), outs[1:4]), out_sem.at[pl.ds(5, 3)])
     for job in jobs:
         job.sent()
+    wait_all(stores)
 
 
 def finish(n, nb, dq, dkv, x, dz1, x1, dur, hid, dfr, omix, dar, gvec, wa):
@@ -1187,27 +1334,29 @@
             pltpu.VMEM((nz, depth, width), kind),
         ]
 
-    def wide(height, width):
-        return jax.ShapeDtypeStruct((height, width), f32)
-
+    args = (dq, dkv, x, dz1, x1, dur, hid, dfr, omix, dar, gvec, wa)
+    shapes = ((rows, 512), (16, 512), (16, 512), (16, 512), (16, 512), (16, 2048), (64, 512), (16, 128))
     return pl.pallas_call(
         functools.partial(finish_kernel, n, nb),
-        out_shape=(
-            wide(rows, 512), wide(16, 512), wide(16, 512), wide(16, 512), wide(16, 512), wide(16, 2048),
-            wide(64, 512), wide(8, 256),
-        ),
-        in_specs=vmem_specs(12),
-        out_specs=vmem_specs(8),
+        out_shape=[jax.ShapeDtypeStruct(shape, f32) for shape in shapes],
+        in_specs=any_specs(12),
+        out_specs=any_specs(8),
         scratch_shapes=[
+            *[pltpu.VMEM(arg.shape, arg.dtype) for arg in args],
             *buffers(16, 1536, bf16),
             *buffers(16, 2560, bf16),
             *buffers(64, 512, bf16),
-            *buffers(8, 256, f32),
+            *buffers(16, 128, f32)[1:2],
+            pltpu.VMEM((2, nz, 8, 128), f32),
+            *buffers(16, 128, f32)[3:],
             pltpu.VMEM((8, 16, 16, 128), f32),
             pltpu.VMEM((16, 8, 16, 128), bf16),
             pltpu.VMEM((16, 8, 16, 128), bf16),
             pltpu.VMEM((16, 4, 16, 128), bf16),
             pltpu.VMEM((rows, 1536), bf16),
+            *[pltpu.VMEM(shape, f32) for shape in shapes],
+            dma((12,)),
+            dma((8,)),
             dma((4, 9 * nz)),
             dma((4, 9 * nz)),
             dma((2, 16)),
@@ -1217,10 +1366,47 @@
             dma,
         ],
         compiler_params=pltpu.CompilerParams(
-            collective_id=3, has_side_effects=True, vmem_limit_bytes=58 << 20
+            collective_id=3, has_side_effects=True, vmem_limit_bytes=VMEM_BYTES
         ),
         name="finish",
-    )(dq, dkv, x, dz1, x1, dur, hid, dfr, omix, dar, gvec, wa)
+    )(*args)
+
+
+def deliver_kernel(count, *refs):
+    ins, outs = refs[:count], refs[count:2 * count + 7]
+    stage, lines, (in_sem, sems) = refs[2 * count + 7:3 * count + 7], refs[3 * count + 7:3 * count + 15], refs[-2:]
+    loads = copies(zip(ins, stage), in_sem)
+    jobs = []
+    for k in range(count - 1):
+        loads[k].wait()
+        jobs += copies([(stage[k], outs[k])], sems.at[pl.ds(k, 1)])
+    loads[-1].wait()
+    vec = stage[-1]
+    lines[0][...] = vec[0:1, 0:64].reshape(64)
+    for k in range(1, 8):
+        lines[k][...] = vec[k:k + 1, 0:16].reshape(16)
+    jobs += copies(zip(lines, outs[count - 1:]), sems.at[pl.ds(count - 1, 8)])
+    wait_all(jobs)
+
+
+def deliver(arrays, vec):
+    count = len(arrays) + 1
+    lines = [(64,)] + [(16,)] * 7
+    return pl.pallas_call(
+        functools.partial(deliver_kernel, count),
+        out_shape=[jax.ShapeDtypeStruct(a.shape, a.dtype) for a in arrays]
+        + [jax.ShapeDtypeStruct(shape, f32) for shape in lines],
+        in_specs=any_specs(count),
+        out_specs=any_specs(count + 7),
+        scratch_shapes=[
+            *[pltpu.VMEM(a.shape, a.dtype) for a in (*arrays, vec)],
+            *[pltpu.VMEM(shape, f32) for shape in lines],
+            pltpu.SemaphoreType.DMA((count,)),
+            pltpu.SemaphoreType.DMA((count + 7,)),
+        ],
+        compiler_params=pltpu.CompilerParams(vmem_limit_bytes=VMEM_BYTES),
+        name="deliver",
+    )(*arrays, vec)
 
 
 def by_pairs(
@@ -1232,38 +1418,22 @@
     x = stream.reshape(256, 512)
     y = accumulator.reshape(256, 512)
     g = upstream.reshape(256, 512)
-    small = (b_down, gain_attn, bias_attn, gain_ffn, bias_ffn, gain_final, bias_final)
-    row = jnp.concatenate([b_up.astype(f32), *(v.astype(f32) for v in small), jnp.zeros((80,), f32)])
-    seg_row = segment_ids.astype(f32).reshape(256)
-    vec = jnp.concatenate([row[None], seg_row[None], jnp.zeros((6, 256), f32)], axis=0)
-    q, kv, wa, wb, wd, vecs = project(n, nb, x, w_query, w_key, w_value, w_out, w_up, w_down, vec)
-    bup = vecs[:, 0, 0:64].reshape(1, 2048)
-    par = jnp.pad(vecs[:, 0, 64:176].reshape(n, 7, 16).transpose(1, 0, 2).reshape(7, 512), ((0, 1), (0, 0)))
-    me = lax.axis_index("head") * nb + lax.axis_index("blk")
-    pair = me // 2
-    seg = vecs[:, 1].reshape(n, 2, 8, 16).astype(jnp.int32)
-    seg = lax.dynamic_index_in_dim(seg, pair // 8, 1, False)
-    seg_k = seg.transpose(1, 0, 2).reshape(8, 16 * n)
-    seg_q = lax.dynamic_index_in_dim(seg.reshape(n // 2, 2, 8, 16), lax.rem(me, 2), 1, False)
-    seg_q = seg_q.transpose(1, 0, 2).reshape(8, 8 * n)
-    bounds = jnp.stack([seg_k[:, 0], seg_k[:, -1]])
-    o, of, lse, kv2 = attn_fwd(bounds, q.reshape(4, 256, 128), kv.reshape(4096, 128), seg_q, seg_k)
-    do, out, dacc, dz1, x1, dur, hid, dfr, omix, dar, pg, bg = middle(
+    smalls = (b_up, b_down, gain_attn, bias_attn, gain_ffn, bias_ffn, gain_final, bias_final)
+    q, kv, wa, wb, wd, par, bup, seg_k, seg_q = project(
+        n, nb, x, w_query, w_key, w_value, w_out, w_up, w_down, segment_ids.reshape(2, 128), smalls
+    )
+    o, of, lse, kv2 = attn_fwd(q.reshape(4, 256, 128), kv.reshape(4096, 128), seg_q, seg_k)
+    do, out, dacc, dz1, x1, dur, hid, dfr, omix, dar, gvec = middle(
         n, nb, o.reshape(4, 16, 16, 128), x, y, g, wb, wd, par, bup
     )
-    gvec = jnp.concatenate(
-        [bg.reshape(n, 64), pg[0:7].reshape(7, n, 16).transpose(1, 0, 2).reshape(n, 112), jnp.zeros((n, 80), f32)], axis=1
-    )
-    gvec = jnp.pad(gvec[:, None], ((0, 0), (0, 7), (0, 0)))
-    dq, dkv = attn_bwd(bounds, q.reshape(4, 256, 128), do.reshape(4, 256, 128), of, lse, kv2, seg_q)
+    dq, dkv, out, dacc = attn_bwd(q.reshape(4, 256, 128), do.reshape(4, 256, 128), of, lse, kv2, seg_q, seg_k, out, dacc)
     gx, gq, gk, gv, go, gu, gd, gs = finish(
         n, nb, dq.reshape(4, 16, 16, 128), dkv.reshape(8, 16, 2, 16, 128), x, dz1, x1, dur, hid, dfr, omix, dar, gvec, wa
     )
-    gs = gs[0]
-    smalls = [gs[64 + 16 * k:80 + 16 * k] for k in range(7)]
+    gx, gq, gk, gv, go, gu, gd, gbu, *small_grads = deliver((gx, gq, gk, gv, go, gu, gd), gs)
     return (
         out.reshape(stream.shape), gx.reshape(stream.shape), dacc.reshape(stream.shape),
-        gq, gk, gv, go, gu, gs[0:64], gd, *smalls,
+        gq, gk, gv, go, gu, gbu, gd, *small_grads,
     )
 
 

time: 229 us -> 190 us (0.83); the launches traced: 227 us -> 190 us
  local copies, waits for them, and re-layouts: 35.4 us -> 0 us
    unnamed x67 -> x0, local copies, waits for them, and re-layouts: 23.7 us -> none
    concatenate x3 -> x0, local copies, waits for them, and re-layouts: 5.58 us -> none  [the longest x1 5.43 us: by_pairs(): jnp.concatenate([b_up.astype(f32), *(v.astype(f32) for v in small), jnp.z...]
    slice x6 -> x0, local copies, waits for them, and re-layouts: 3.01 us -> none  [the longest x1 1.43 us: by_pairs(): smalls = [gs[64 + 16 * k:80 + 16 * k] for k in range(7)]]
    pallas_call x4 -> x5, Pallas kernels: 134 us -> 135 us  [the longest x1 57.7 us: finish(): pl.pallas_call(functools.partial(finish_kernel, n, nb), out_shape=[jax.Sh...]
where the time goes in v2:
time: 190 us
  Pallas kernels  189 us (99%)
    pallas_call x1, Pallas kernels, finish(): pl.pallas_call(functools.partial(finish_kernel, n, nb), out_shape=[jax.Sh...  57.7 us
    pallas_call x1, Pallas kernels, project(): pl.pallas_call(functools.partial(project_kernel, n, nb), out_shape=(jax.S...  54.2 us
    pallas_call x1, Pallas kernels, middle(): pl.pallas_call(functools.partial(middle_kernel, n, nb), out_shape=[jax.Sh...  31 us
    pallas_call x1, Pallas kernels, attn_bwd(): pl.pallas_call(attn_bwd_kernel, out_shape=[jax.ShapeDtypeStruct(shape, ki...  23.3 us
    pallas_call x1, Pallas kernels, attn_fwd(): pl.pallas_call(attn_fwd_kernel, out_shape=[jax.ShapeDtypeStruct(shape, ki...  21.1 us

profile of v2, /device:TPU:0, one launch (start us, length us, event | category | flops | bytes accessed | tf_op | source)
XLA Modules:
  0.0 190.3 jit_solution(1622527249360924297)
XLA Ops:
  0.7 54.2 %project.1 = (bf16[4,16,16,128]{3,2,1,0:T(8,128)(2,1)}, bf16[8,16,2,16,128]{4,3,2,1,0:T(8,128)(2,1)}, bf16[32,16,1536]{2,1,0:T(8,128)(2,1)}, bf16[32,16,2560]{2,...) custom-call(bf16[256,512]{1,0:T(8,128)(2,1)} %bitcast.19, ...), custom_call_target="tpu_custom_call" | custom-call | tf_op jit(solution)/shard_map/project/pallas_call | solution.py:1019
  54.8 21.1 %attn_fwd.1 = (bf16[4,256,128]{2,1,0:T(8,128)(2,1)}, f32[4,256,128]{2,1,0:T(8,128)}, f32[8,256]{1,0:T(8,128)}, bf16[4096,256]{1,0:T(8,128)(2,1)}) custom-call(bf16[4,256,128]{2,1,0:T(8,128)(2,1)} %bitcast.24, bf16[4096,128]{1,0:T(8,128)(2,1)} %bitcast.23, s32[8,256]{1,0:T(8,128)} %get-tuple-element.70.seg_q_hbm, s32[8,512]{1,0:T(8,128)} %get-tuple-element.71.seg_k_hbm), custom_call_target="tpu_custom_call" | custom-call | tf_op jit(solution)/shard_map/attn_fwd/pallas_call | solution.py:442
  75.9 31.0 %middle.1 = (bf16[4,16,16,128]{3,2,1,0:T(8,128)(2,1)}, bf16[256,512]{1,0:T(8,128)(2,1)}, f32[256,512]{1,0:T(8,128)}, f32[256,512]{1,0:T(8,128)}, bf16[256,512]{1...) custom-call(bf16[4,16,16,128]{3,2,1,0:T(8,128)(2,1)} %bitcast.29, ...), custom_call_target="tpu_custom_call" | custom-call | tf_op jit(solution)/shard_map/middle/pallas_call | solution.py:1198
  107.0 23.3 %attn_bwd.1 = (bf16[4,256,128]{2,1,0:T(8,128)(2,1)}, f32[4096,128]{1,0:T(8,128)}, bf16[256,512]{1,0:T(8,128)(2,1)}, f32[256,512]{1,0:T(8,128)}) custom-call(bf16[4,256,128]{2,1,0:T(8,128)(2,1)} %bitcast.25, bf16[4,256,128]{2,1,0:T(8,128)(2,1)} %bitcast.30, f32[4,256,128]{2,1,0:T(8,128)} %get-tuple-element.78.of_hbm, f32[8,256]{1,0:T(8,128)} %get-tuple-element.79.lse_hbm, ...), custom_call_target="tpu_custom_call" | custom-call | tf_op jit(solution)/shard_map/attn_bwd/pallas_call | solution.py:524
  130.2 57.7 %finish.1 = (f32[256,512]{1,0:T(8,128)}, f32[16,512]{1,0:T(8,128)}, f32[16,512]{1,0:T(8,128)}, f32[16,512]{1,0:T(8,128)}, f32[16,512]{1,0:T(8,128)}, /*index=5*/...) custom-call(bf16[4,16,16,128]{3,2,1,0:T(8,128)(2,1)} %bitcast.28, f32[8,16,2,16,128]{4,3,2,1,0:T(8,128)} %bitcast.22, ...), custom_call_target="tpu_custom_call" | custom-call | tf_op jit(solution)/shard_map/finish/pallas_call | solution.py:1339
  187.9 2.2 %deliver.1 = (f32[256,512]{1,0:T(8,128)}, f32[16,512]{1,0:T(8,128)}, f32[16,512]{1,0:T(8,128)}, f32[16,512]{1,0:T(8,128)}, f32[16,512]{1,0:T(8,128)}, /*index=5*...) custom-call(f32[256,512]{1,0:T(8,128)} %get-tuple-element.95.refs_0_, ...), custom_call_target="tpu_custom_call" | custom-call | tf_op jit(solution)/shard_map/deliver/pallas_call | solution.py:1395

commit v3 on v2

--- a/solution.py
+++ b/solution.py
@@ -374,9 +374,23 @@
         wide = pltpu.roll(wide, 64, 1)
     return jnp.where(lanes(wide.shape) < 64, wide, 0.0).astype(bf16)
 
+def key_steps(bounds, low, high):
+    chunks, keys = bounds.shape
+    first = sum(jnp.where(bounds[t, keys - 1] < low, 1, 0) for t in range(chunks))
+    last = sum(jnp.where(bounds[t, 0] <= high, 1, 0) for t in range(chunks))
+    pairs = (last - first + 1) // 2
+    start = jnp.minimum(first, chunks - 2 * pairs)
+    return start, pairs // 2, lax.rem(pairs, 2)
+
+
+def walk(step, fours, twos, carry):
+    carry = lax.fori_loop(0, fours, lambda t, c: step(4, 4 * t, c), carry)
+    return lax.fori_loop(0, twos, lambda t, c: step(2, 4 * fours, c), carry)
+
+
 def attn_fwd_kernel(
-    q_hbm, kv_hbm, seg_q_hbm, seg_k_hbm, o_hbm, of_hbm, lse_hbm, kv2_hbm,
-    q_ref, kv_ref, seg_q_ref, seg_k_ref, bounds, o_ref, of_ref, lse_ref, kv2_ref, vo_ref, in_sem, out_sem,
+    q_hbm, kv_hbm, seg_q_hbm, seg_k_hbm, o_hbm, of_hbm, lse_hbm, kv2_hbm, kvt_hbm,
+    q_ref, kv_ref, seg_q_ref, seg_k_ref, bounds, o_ref, of_ref, lse_ref, kv2_ref, kvt_ref, vo_ref, in_sem, out_sem,
 ):
     loads = copies(
         [(seg_q_hbm, seg_q_ref), (seg_k_hbm, seg_k_ref), (seg_k_hbm, bounds), (kv_hbm, kv_ref), (q_hbm, q_ref)], in_sem
@@ -388,14 +402,16 @@
     def prepare(t, c):
         rows = pl.ds(pl.multiple_of(t * keys, keys), keys)
         kv = kv_ref[rows, :]
-        wide = jnp.broadcast_to(seg_k_ref[pl.ds(t, 1), :], (128, keys)).T
+        marks = jnp.where(seg_k_ref[pl.ds(t, 1), :] == rows_of((128, keys)), 0.0, FAR)
+        kvt_ref[0:128, rows] = kv.T
+        kvt_ref[128:256, rows] = marks.astype(bf16)
         kv2_ref[rows, 0:128] = kv
-        kv2_ref[rows, 128:256] = jnp.where(wide == lanes(wide.shape), 0.0, FAR).astype(bf16)
+        kv2_ref[rows, 128:256] = marks.T.astype(bf16)
         vo_ref[rows, :] = jnp.where(lanes(kv.shape) < 64, 1.0, kv.astype(f32)).astype(bf16)
         return c
 
     lax.fori_loop(0, chunks, prepare, 0)
-    stores = copies([(kv2_ref, kv2_hbm)], out_sem)
+    stores = copies([(kv2_ref, kv2_hbm), (kvt_ref, kvt_hbm)], out_sem)
 
     def tile(j, c):
         q_tile = q_ref[j]
@@ -406,21 +422,19 @@
             left = half_lanes(q_tile, half)
             left = jnp.concatenate([left, query_marks(seg_q_ref[pl.ds(i, 1), :])], axis=1)
             low, high = bounds[i, 0], bounds[i, keys - 1]
-            first = lax.fori_loop(0, chunks, lambda t, n: n + jnp.where(bounds[t, keys - 1] < low, 1, 0), 0)
-            last = lax.fori_loop(0, chunks, lambda t, n: n + jnp.where(bounds[t, 0] <= high, 1, 0), 0)
-
-            def step(t, carry):
+            start, fours, twos = key_steps(bounds, low, high)
+
+            def step(width, t, carry):
                 top, acc = carry
-                at = pl.ds(pl.multiple_of(t * keys, keys), keys)
-                s = dot_t(left, kv2_ref[at, :])
+                at = pl.ds(pl.multiple_of((start + t) * keys, keys), width * keys)
+                s = dot_n(left, kvt_ref[:, at])
                 new = jnp.maximum(top, jnp.max(s, axis=1, keepdims=True))
                 p = jnp.exp2((s - new) * log_scale)
                 acc = acc * jnp.exp2((top - new) * log_scale) + dot_n(p.astype(bf16), vo_ref[at, :])
                 return new, acc
 
-            top, acc = lax.fori_loop(
-                first, last, step, (jnp.full((rows, 1), FAR, f32), jnp.zeros((rows, 128), f32))
-            )
+            carry = (jnp.full((rows, 1), FAR, f32), jnp.zeros((rows, 128), f32))
+            top, acc = walk(step, fours, twos, carry)
             total = pltpu.roll(acc, 64, 1)
             outs.append(acc / total)
             lse = jnp.broadcast_to(top * log_scale, acc.shape) + jnp.log2(acc)
@@ -431,26 +445,28 @@
         return c
 
     lax.fori_loop(0, chunks // 2, tile, 0)
-    stores += copies([(o_ref, o_hbm), (of_ref, of_hbm), (lse_ref, lse_hbm)], out_sem.at[pl.ds(1, 3)])
+    stores += copies([(o_ref, o_hbm), (of_ref, of_hbm), (lse_ref, lse_hbm)], out_sem.at[pl.ds(2, 3)])
     wait_all(stores)
 
 
 def attn_fwd(q, kv, seg_q, seg_k):
     chunks, keys = seg_k.shape
     dma = pltpu.SemaphoreType.DMA
-    shapes = ((q.shape, bf16), (q.shape, f32), (seg_q.shape, f32), ((chunks * keys, 256), bf16))
+    shapes = (
+        (q.shape, bf16), (q.shape, f32), (seg_q.shape, f32), ((chunks * keys, 256), bf16), ((256, chunks * keys), bf16)
+    )
     return pl.pallas_call(
         attn_fwd_kernel,
         out_shape=[jax.ShapeDtypeStruct(shape, kind) for shape, kind in shapes],
         in_specs=any_specs(4),
-        out_specs=any_specs(4),
+        out_specs=any_specs(5),
         scratch_shapes=[
             *[pltpu.VMEM(a.shape, a.dtype) for a in (q, kv, seg_q, seg_k)],
             pltpu.SMEM(seg_k.shape, jnp.int32),
             *[pltpu.VMEM(shape, kind) for shape, kind in shapes],
             pltpu.VMEM((chunks * keys, 128), bf16),
             dma((5,)),
-            dma((4,)),
+            dma((5,)),
         ],
         compiler_params=pltpu.CompilerParams(vmem_limit_bytes=VMEM_BYTES),
         name="attn_fwd",
@@ -458,14 +474,14 @@
 
 
 def attn_bwd_kernel(
-    q_hbm, do_hbm, of_hbm, lse_hbm, kv2_hbm, seg_q_hbm, seg_k_hbm, pass1, pass2, dq_hbm, dkv_hbm, out1, out2,
-    q_ref, do_ref, of_ref, lse_ref, kv2_ref, seg_q_ref, bounds, dq_ref, dkv_ref, hold1, hold2, in_sem, out_sem,
+    q_hbm, do_hbm, of_hbm, lse_hbm, kv2_hbm, kvt_hbm, seg_q_hbm, seg_k_hbm, pass1, pass2, dq_hbm, dkv_hbm, out1, out2,
+    q_ref, do_ref, of_ref, lse_ref, kv2_ref, kvt_ref, seg_q_ref, bounds, dq_ref, dkv_ref, hold1, hold2, in_sem, out_sem,
 ):
     loads = copies(
         [
             (q_hbm, q_ref), (do_hbm, do_ref), (of_hbm, of_ref), (lse_hbm, lse_ref), (kv2_hbm, kv2_ref),
             (seg_q_hbm, seg_q_ref), (seg_k_hbm, bounds),
-            (pass1, hold1), (pass2, hold2),
+            (pass1, hold1), (pass2, hold2), (kvt_hbm, kvt_ref),
         ],
         in_sem,
     )
@@ -492,21 +508,19 @@
             lse = lse_ref[pl.ds(i, 1), :]
             both = jnp.concatenate([left, grad], axis=0)
             marks = query_marks(seg_q_ref[pl.ds(i, 1), :])
-            right = jnp.concatenate([both, jnp.concatenate([marks, jnp.zeros_like(marks)], axis=0)], axis=1)
+            right = jnp.concatenate([both, jnp.concatenate([marks, jnp.zeros_like(marks)], axis=0)], axis=1).T
             low, high = bounds[i, 0], bounds[i, keys - 1]
-            first = lax.fori_loop(0, chunks, lambda t, n: n + jnp.where(bounds[t, keys - 1] < low, 1, 0), 0)
-            last = lax.fori_loop(0, chunks, lambda t, n: n + jnp.where(bounds[t, 0] <= high, 1, 0), 0)
-
-            def step(t, dq):
-                at = pl.ds(pl.multiple_of(t * keys, keys), keys)
-                kv2 = kv2_ref[at, :]
-                sdp = dot_t(kv2, right)
+            start, fours, twos = key_steps(bounds, low, high)
+
+            def step(width, t, dq):
+                at = pl.ds(pl.multiple_of((start + t) * keys, keys), width * keys)
+                sdp = dot_n(kv2_ref[at, :], right)
                 p = jnp.exp2(sdp[:, :rows] * log_scale - lse)
                 ds = (p * (sdp[:, rows:] - delta)).astype(bf16)
                 dkv_ref[at, :] += dot_n(jnp.concatenate([ds, p.astype(bf16)], axis=1), both)
-                return dq + dot_0(ds, kv2[:, 0:128])
-
-            dqs.append(lax.fori_loop(first, last, step, jnp.zeros((rows, 128), f32)))
+                return dq + dot_n(kvt_ref[0:128, at], ds)
+
+            dqs.append(walk(step, fours, twos, jnp.zeros((128, rows), f32)).T)
         dq = jnp.where(lanes(dqs[0].shape) < 64, dqs[0], pltpu.roll(dqs[1], 64, 1))
         dq_ref[j] = (dq * DH ** (-0.5)).astype(bf16)
         return c
@@ -518,26 +532,26 @@
     wait_all(stores)
 
 
-def attn_bwd(q, do, of, lse, kv2, seg_q, seg_k, pass1, pass2):
+def attn_bwd(q, do, of, lse, kv2, kvt, seg_q, seg_k, pass1, pass2):
     dma = pltpu.SemaphoreType.DMA
     shapes = ((q.shape, bf16), ((kv2.shape[0], 128), f32))
     return pl.pallas_call(
         attn_bwd_kernel,
         out_shape=[jax.ShapeDtypeStruct(shape, kind) for shape, kind in shapes]
         + [jax.ShapeDtypeStruct(a.shape, a.dtype) for a in (pass1, pass2)],
-        in_specs=any_specs(9),
+        in_specs=any_specs(10),
         out_specs=any_specs(4),
         scratch_shapes=[
-            *[pltpu.VMEM(a.shape, a.dtype) for a in (q, do, of, lse, kv2, seg_q)],
+            *[pltpu.VMEM(a.shape, a.dtype) for a in (q, do, of, lse, kv2, kvt, seg_q)],
             pltpu.SMEM(seg_k.shape, jnp.int32),
             *[pltpu.VMEM(shape, kind) for shape, kind in shapes],
             *[pltpu.VMEM(a.shape, a.dtype) for a in (pass1, pass2)],
-            dma((9,)),
+            dma((10,)),
             dma((4,)),
         ],
         compiler_params=pltpu.CompilerParams(vmem_limit_bytes=VMEM_BYTES),
         name="attn_bwd",
-    )(q, do, of, lse, kv2, seg_q, seg_k, pass1, pass2)
+    )(q, do, of, lse, kv2, kvt, seg_q, seg_k, pass1, pass2)
 
 
 class Spot:
@@ -1422,11 +1436,13 @@
     q, kv, wa, wb, wd, par, bup, seg_k, seg_q = project(
         n, nb, x, w_query, w_key, w_value, w_out, w_up, w_down, segment_ids.reshape(2, 128), smalls
     )
-    o, of, lse, kv2 = attn_fwd(q.reshape(4, 256, 128), kv.reshape(4096, 128), seg_q, seg_k)
+    o, of, lse, kv2, kvt = attn_fwd(q.reshape(4, 256, 128), kv.reshape(4096, 128), seg_q, seg_k)
     do, out, dacc, dz1, x1, dur, hid, dfr, omix, dar, gvec = middle(
         n, nb, o.reshape(4, 16, 16, 128), x, y, g, wb, wd, par, bup
     )
-    dq, dkv, out, dacc = attn_bwd(q.reshape(4, 256, 128), do.reshape(4, 256, 128), of, lse, kv2, seg_q, seg_k, out, dacc)
+    dq, dkv, out, dacc = attn_bwd(
+        q.reshape(4, 256, 128), do.reshape(4, 256, 128), of, lse, kv2, kvt, seg_q, seg_k, out, dacc
+    )
     gx, gq, gk, gv, go, gu, gd, gs = finish(
         n, nb, dq.reshape(4, 16, 16, 128), dkv.reshape(8, 16, 2, 16, 128), x, dz1, x1, dur, hid, dfr, omix, dar, gvec, wa
     )

time: 190 us -> 178 us (0.937)
  Pallas kernels: 189 us -> 177 us
    pallas_call x1, Pallas kernels: 21.1 us -> 14.2 us  [attn_fwd(): pl.pallas_call(attn_fwd_kernel, out_shape=[jax.ShapeDtypeStruct(shape, ki...]
    pallas_call x1, Pallas kernels: 23.3 us -> 19.5 us  [attn_bwd(): pl.pallas_call(attn_bwd_kernel, out_shape=[jax.ShapeDtypeStruct(shape, ki...]
where the time goes in v3:
time: 178 us; the launch traced here: 177 us
  Pallas kernels  177 us (99%)
    pallas_call x1, Pallas kernels, finish(): pl.pallas_call(functools.partial(finish_kernel, n, nb), out_shape=[jax.Sh...  56.7 us
    pallas_call x1, Pallas kernels, project(): pl.pallas_call(functools.partial(project_kernel, n, nb), out_shape=(jax.S...  54.2 us
    pallas_call x1, Pallas kernels, middle(): pl.pallas_call(functools.partial(middle_kernel, n, nb), out_shape=[jax.Sh...  29.8 us
    pallas_call x1, Pallas kernels, attn_bwd(): pl.pallas_call(attn_bwd_kernel, out_shape=[jax.ShapeDtypeStruct(shape, ki...  19.5 us
    pallas_call x1, Pallas kernels, attn_fwd(): pl.pallas_call(attn_fwd_kernel, out_shape=[jax.ShapeDtypeStruct(shape, ki...  14.2 us

profile of v3, /device:TPU:0, one launch (start us, length us, event | category | flops | bytes accessed | tf_op | source)
XLA Modules:
  0.0 177.4 jit_solution(5685086772126272824)
XLA Ops:
  0.7 54.2 %project.1 = (bf16[4,16,16,128]{3,2,1,0:T(8,128)(2,1)}, bf16[8,16,2,16,128]{4,3,2,1,0:T(8,128)(2,1)}, bf16[32,16,1536]{2,1,0:T(8,128)(2,1)}, bf16[32,16,2560]{2,...) custom-call(bf16[256,512]{1,0:T(8,128)(2,1)} %bitcast.19, ...), custom_call_target="tpu_custom_call" | custom-call | tf_op jit(solution)/shard_map/project/pallas_call | solution.py:1033
  54.8 14.2 %attn_fwd.1 = (bf16[4,256,128]{2,1,0:T(8,128)(2,1)}, f32[4,256,128]{2,1,0:T(8,128)}, f32[8,256]{1,0:T(8,128)}, bf16[4096,256]{1,0:T(8,128)(2,1)}, bf16[256,4096]{1,0:T(8,128)(2,1)}) custom-call(bf16[4,256,128]{2,1,0:T(8,128)(2,1)} %bitcast.24, bf16[4096,128]{1,0:T(8,128)(2,1)} %bitcast.23, s32[8,256]{1,0:T(8,128)} %get-tuple-element.71.seg_q_hbm, ...), custom_call_target="tpu_custom_call" | custom-call | tf_op jit(solution)/shard_map/attn_fwd/pallas_call | solution.py:458
  69.1 29.8 %middle.1 = (bf16[4,16,16,128]{3,2,1,0:T(8,128)(2,1)}, bf16[256,512]{1,0:T(8,128)(2,1)}, f32[256,512]{1,0:T(8,128)}, f32[256,512]{1,0:T(8,128)}, bf16[256,512]{1...) custom-call(bf16[4,16,16,128]{3,2,1,0:T(8,128)(2,1)} %bitcast.30, ...), custom_call_target="tpu_custom_call" | custom-call | tf_op jit(solution)/shard_map/middle/pallas_call | solution.py:1212
  98.8 19.5 %attn_bwd.1 = (bf16[4,256,128]{2,1,0:T(8,128)(2,1)}, f32[4096,128]{1,0:T(8,128)}, bf16[256,512]{1,0:T(8,128)(2,1)}, f32[256,512]{1,0:T(8,128)}) custom-call(bf16[4,256,128]{2,1,0:T(8,128)(2,1)} %bitcast.25, bf16[4,256,128]{2,1,0:T(8,128)(2,1)} %bitcast.29, f32[4,256,128]{2,1,0:T(8,128)} %get-tuple-element.79.of_hbm, f32[8,256]{1,0:T(8,128)} %get-tuple-element.80.lse_hbm, ...), custom_call_target="tpu_custom_call" | custom-call | tf_op jit(solution)/shard_map/attn_bwd/pallas_call | solution.py:538
  118.3 56.7 %finish.1 = (f32[256,512]{1,0:T(8,128)}, f32[16,512]{1,0:T(8,128)}, f32[16,512]{1,0:T(8,128)}, f32[16,512]{1,0:T(8,128)}, f32[16,512]{1,0:T(8,128)}, /*index=5*/...) custom-call(bf16[4,16,16,128]{3,2,1,0:T(8,128)(2,1)} %bitcast.28, f32[8,16,2,16,128]{4,3,2,1,0:T(8,128)} %bitcast.22, ...), custom_call_target="tpu_custom_call" | custom-call | tf_op jit(solution)/shard_map/finish/pallas_call | solution.py:1353
  175.1 2.2 %deliver.1 = (f32[256,512]{1,0:T(8,128)}, f32[16,512]{1,0:T(8,128)}, f32[16,512]{1,0:T(8,128)}, f32[16,512]{1,0:T(8,128)}, f32[16,512]{1,0:T(8,128)}, /*index=5*...) custom-call(f32[256,512]{1,0:T(8,128)} %get-tuple-element.97.refs_0_, ...), custom_call_target="tpu_custom_call" | custom-call | tf_op jit(solution)/shard_map/deliver/pallas_call | solution.py:1409

commit v4 on v3

--- a/solution.py
+++ b/solution.py
@@ -469,13 +469,14 @@
             dma((5,)),
         ],
         compiler_params=pltpu.CompilerParams(vmem_limit_bytes=VMEM_BYTES),
+        cost_estimate=pl.CostEstimate(flops=10**10, bytes_accessed=10**7, transcendentals=10**7),
         name="attn_fwd",
     )(q, kv, seg_q, seg_k)
 
 
 def attn_bwd_kernel(
     q_hbm, do_hbm, of_hbm, lse_hbm, kv2_hbm, kvt_hbm, seg_q_hbm, seg_k_hbm, pass1, pass2, dq_hbm, dkv_hbm, out1, out2,
-    q_ref, do_ref, of_ref, lse_ref, kv2_ref, kvt_ref, seg_q_ref, bounds, dq_ref, dkv_ref, hold1, hold2, in_sem, out_sem,
+    q_ref, do_ref, of_ref, lse_ref, kv2_ref, kvt_ref, seg_q_ref, bounds, dq_ref, dkv_low, dkv_ref, hold1, hold2, in_sem, out_sem,
 ):
     loads = copies(
         [
@@ -527,14 +528,14 @@
 
     lax.fori_loop(0, chunks // 2, tile, 0)
     dkv = dkv_ref[...]
-    dkv_ref[...] = jnp.where(lanes(dkv.shape) < 64, dkv * DH ** (-0.5), dkv)
-    stores += copies([(dq_ref, dq_hbm), (dkv_ref, dkv_hbm)], out_sem.at[pl.ds(2, 2)])
+    dkv_low[...] = jnp.where(lanes(dkv.shape) < 64, dkv * DH ** (-0.5), dkv).astype(bf16)
+    stores += copies([(dq_ref, dq_hbm), (dkv_low, dkv_hbm)], out_sem.at[pl.ds(2, 2)])
     wait_all(stores)
 
 
 def attn_bwd(q, do, of, lse, kv2, kvt, seg_q, seg_k, pass1, pass2):
     dma = pltpu.SemaphoreType.DMA
-    shapes = ((q.shape, bf16), ((kv2.shape[0], 128), f32))
+    shapes = ((q.shape, bf16), ((kv2.shape[0], 128), bf16))
     return pl.pallas_call(
         attn_bwd_kernel,
         out_shape=[jax.ShapeDtypeStruct(shape, kind) for shape, kind in shapes]
@@ -545,6 +546,7 @@
             *[pltpu.VMEM(a.shape, a.dtype) for a in (q, do, of, lse, kv2, kvt, seg_q)],
             pltpu.SMEM(seg_k.shape, jnp.int32),
             *[pltpu.VMEM(shape, kind) for shape, kind in shapes],
+            pltpu.VMEM((kv2.shape[0], 128), f32),
             *[pltpu.VMEM(a.shape, a.dtype) for a in (pass1, pass2)],
             dma((10,)),
             dma((4,)),
@@ -611,9 +613,10 @@
 
 class Gather:
     def __init__(self, spot, shard, full, send, recv, local):
-        self.s, self.shard, self.full, self.local = spot, shard, full, local
+        self.s, self.full, self.local = spot, full, local
+        self.shard = shard if callable(shard) else lambda z: shard
         self.send, self.recv = send, recv
-        self.cut = halves(shard.shape)
+        self.cut = halves(full.shape[1:])
 
     def copy(self, src, dst, k, h, z, c, recv_k=None):
         recv_k = k if recv_k is None else recv_k
@@ -621,7 +624,7 @@
 
     def to_z(self, z):
         s = self.s
-        return self.copy(self.shard, self.full.at[s.me], z, s.h, z, s.c, s.z)
+        return self.copy(self.shard(z), self.full.at[s.me], z, s.h, z, s.c, s.z)
 
     def from_z(self, z):
         s = self.s
@@ -631,7 +634,7 @@
     def near(self, w, z, own=False):
         s = self.s
         slot = self.full.at[s.index(s.h, z, s.c)]
-        return self.copy(self.shard if own else slot, slot, (1 + w) * s.nz + z, s.near[w], s.z, s.c)
+        return self.copy(self.shard(s.z) if own else slot, slot, (1 + w) * s.nz + z, s.near[w], s.z, s.c)
 
     def from_near(self, w, z):
         s = self.s
@@ -654,7 +657,7 @@
     def twin(self, h, z, own=False):
         s = self.s
         slot = self.full.at[s.index(h, z, s.c)]
-        return self.copy(self.shard if own else slot, slot, 5 * s.nz + h * s.nz + z, s.h, s.z, 1 - s.c)
+        return self.copy(self.shard(s.z) if own else slot, slot, 5 * s.nz + h * s.nz + z, s.h, s.z, 1 - s.c)
 
     def from_twin(self, h, z):
         s = self.s
@@ -663,9 +666,12 @@
 
     def begin(self):
         s = self.s
-        self.own = pltpu.make_async_copy(self.shard, self.full.at[s.me], self.local)
+        each(s.nz, lambda k: self.to_z(s.ahead(k)).start(), 1)
+
+    def begin_near(self):
+        s = self.s
+        self.own = pltpu.make_async_copy(self.shard(s.z), self.full.at[s.me], self.local)
         self.own.start()
-        each(s.nz, lambda k: self.to_z(s.ahead(k)).start(), 1)
         self.near(0, s.z, True).start()
         self.near(1, s.z, True).start()
         self.twin(s.h, s.z, True).start()
@@ -817,6 +823,12 @@
 
         each(s.nz, go, 1)
 
+    def columns(self):
+        s = self.s
+        self.l[s.z] = self.joined(s.z).astype(self.l.dtype)
+        each(s.nz, lambda k: self.from_line(s.ahead(k)).wait_recv(), 1)
+        return [self.l[w].astype(f32) + self.l[w + 2].astype(f32) for w in range(2)]
+
     def total(self):
         s = self.s
         value = self.joined(s.z)
@@ -871,6 +883,25 @@
     def sent(self):
         self.own().wait()
         each(16, lambda i: self.copy(i).wait_send(), 1)
+
+
+class Plane:
+    def __init__(self, spot, send, recv):
+        self.s, self.send, self.recv = spot, send, recv
+
+    def to(self, k):
+        return lax.rem(self.s.h + k, 4)
+
+    def frm(self, k):
+        return lax.rem(self.s.h + 4 - k, 4)
+
+    def copy(self, src, dst, j, at_send, at_recv):
+        s = self.s
+        return remote(src, dst, self.send.at[at_send], self.recv.at[at_recv], j, s.z * 2 + s.c)
+
+
+def pair_of(g):
+    return lax.rem(g, 4) * 4 + g // 4
 
 
 def weave(left, right):
@@ -918,77 +949,184 @@
     )
 
 
+class Line:
+    def __init__(self, spot, shard, full, send, recv, local):
+        self.s, self.shard, self.full, self.send, self.recv = spot, shard, full, send, recv
+        self.own = pltpu.make_async_copy(shard, full.at[spot.z], local)
+
+    def copy(self, way, t):
+        s = self.s
+        k = 2 * t + (way + 1) // 2
+        src = self.full.at[s.z - way * t] if t else self.shard
+        dst = self.full.at[s.z - way * t]
+        return remote(src, dst, self.send.at[k], self.recv.at[k], s.h, (s.z + way) * 2 + s.c)
+
+    def inside(self, z):
+        return (z >= 0) & (z < self.s.nz)
+
+    def sends(self, t, act):
+        for way in (1, -1):
+            z = self.s.z
+
+            @pl.when(self.inside(z + way) & self.inside(z - way * t))
+            def _():
+                act(self.copy(way, t))
+
+    def arrive(self, t):
+        for way in (1, -1):
+            s = self.s
+
+            @pl.when(self.inside(s.z - way * (t + 1)))
+            def _():
+                slot = self.full.at[s.z - way * (t + 1)]
+                k = 2 * t + (way + 1) // 2
+                remote(slot, slot, self.send.at[k], self.recv.at[k], s.h, (s.z - way) * 2 + s.c).wait_recv()
+
+    def begin(self):
+        self.own.start()
+        self.sends(0, lambda copy: copy.start())
+
+    def onward(self, t):
+        self.arrive(t)
+        if t + 1 < self.s.nz - 1:
+            self.sends(t + 1, lambda copy: copy.start())
+
+    def sent(self):
+        self.own.wait()
+        for t in range(self.s.nz - 1):
+            self.sends(t, lambda copy: copy.wait_send())
+
+
 def project_kernel(n, nb, *refs):
     x_hbm, wq_hbm, wk_hbm, wv_hbm, wo_hbm, wu_hbm, wd_hbm, seg_hbm = refs[:8]
     smalls = refs[8:16]
-    q_out, kv_out, wa_out, wb_out, wd_out, par_out, bup_out, segk_out, segq_out = refs[16:25]
+    q_out, kv_out, x_out, wa_out, fz_out, par_out, bup_out, segk_out, segq_out = refs[16:25]
     (
-        x, wq, wk, wv, wo, wu, wd, seg, *small, bup_small, vec, vecs, sa, sb, wa, kv_send, q_send, par, bup, segk, segq,
-        in_sem, out_sem, ag_send, ag_recv, ag_local, ex_send, ex_recv, ex_local, tw_send, tw_recv,
+        x, wq, wk, wv, wo, wu, wd, seg, *small, bup_small, vec, sa, sb, wa, x_all, kv_send, q_send,
+        par, bup, segk, segq,
+        in_sem, out_sem, w_send, w_recv, w_local, f_send, f_recv, f_local,
+        x_send, x_recv, x_local, ex_send, ex_recv, ex_local, tw_send, tw_recv,
     ) = refs[25:]
     s = Spot(nb)
     loads = copies(
         [(wq_hbm, wq), (wk_hbm, wk), (wv_hbm, wv), (seg_hbm, seg), (smalls[0], bup_small)]
         + [(smalls[k], small[k - 1]) for k in range(1, 8)]
-        + [(wo_hbm, wo), (wu_hbm, wu), (wd_hbm, wd), (x_hbm, x)],
+        + [(x_hbm, x), (wo_hbm, wo), (wu_hbm, wu), (wd_hbm, wd)],
         in_sem,
     )
     greet_all(n, nb, s.me)
-    wait_all(loads[:12])
-    for t in range(4):
-        tile = slice(128 * t, 128 * t + 128)
-        first, second = weave(wk[:, tile], wv[:, tile])
-        sa[:, 256 * t:256 * t + 128] = first
-        sa[:, 256 * t + 128:256 * t + 256] = second
-    sa[:, 1024:1536] = wq[...]
+
+    def pass_x(z, slot):
+        return remote(x.at[z // 2], x_all.at[slot], x_send.at[z], x_recv.at[slot], s.h, z * 2 + s.c)
+
+    wait_all(loads[:13])
     vec[...] = jnp.zeros_like(vec)
     vec[0:1, 0:64] = bup_small[...].astype(f32).reshape(1, 64)
     for k in range(7):
         vec[k + 1:k + 2, 0:16] = small[k][...].astype(f32).reshape(1, 16)
     vec[8:10, :] = seg[...].astype(f32)
-    jobs = [
-        Gather(s, shard, full, ag_send.at[k], ag_recv.at[k], ag_local.at[k])
-        for k, (shard, full) in enumerate(((sa, wa), (vec, vecs), (sb, wb_out), (wd, wd_out)))
-    ]
-    for job in jobs[:2]:
-        job.begin()
-    wait_all(loads[12:])
+    for t in range(4):
+        tile, at = slice(128 * t, 128 * t + 128), 256 * (t % 2)
+        first, second = weave(wk[:, tile], wv[:, tile])
+        sa[t // 2, :, at:at + 128] = first
+        sa[t // 2, :, at + 128:at + 256] = second
+    for w in range(2):
+        sa[w, :, 512:768] = wq[:, 256 * w:256 * w + 256]
+        sa[w, :, 768:896] = vec[...].astype(bf16)
+
+    def w_line(z, slot):
+        return remote(
+            sa.at[lax.rem(z, 2)], wa.at[s.h, slot, s.c], w_send.at[z], w_recv.at[slot], s.h, z * 2 + s.c
+        )
+
+    def w_plane(j, h):
+        slot = wa.at[h, :, s.c]
+        return remote(slot, slot, w_send.at[4 + j], w_recv.at[4 + h], j, s.z * 2 + s.c)
+
+    def w_twin(h, c):
+        slot = wa.at[h, :, c]
+        return remote(slot, slot, w_send.at[8 + h], w_recv.at[8 + h], s.h, s.z * 2 + 1 - s.c)
+
+    each(s.nz, lambda k: w_line(s.ahead(k), s.z).start(), 1)
+    own_w = pltpu.make_async_copy(sa.at[lax.rem(s.z, 2)], wa.at[s.h, s.z, s.c], w_local)
+    own_w.start()
+    each(s.nz, lambda k: pass_x(s.ahead(k), s.z).start(), 1)
+    own_x = pltpu.make_async_copy(x.at[s.z // 2], x_all.at[s.z], x_local)
+    own_x.start()
+    wait_all(loads[13:])
     sb[:, 0:512] = wo[...]
     sb[:, 512:2560] = wu[...]
-    for job in jobs[:2]:
-        job.spread()
-    for job in jobs[:2]:
-        job.cross()
-    for job in jobs[:2]:
-        job.last()
-    for job in jobs[2:]:
-        job.begin()
-    for job in jobs[:2]:
-        job.arrive()
+    for t in range(4):
+        sb[:, 2560 + 512 * t:3072 + 512 * t] = wd[16 * t:16 * t + 16, :]
+    line = Line(s, sb, fz_out, f_send, f_recv, f_local)
+    line.begin()
+    own_w.wait()
+    each(s.nz, lambda k: w_line(s.ahead(k), s.ahead(k)).wait_recv(), 1)
+    each(4, lambda i: w_plane(lax.rem(s.h + i, 4), s.h).start(), 1)
+    w_twin(s.h, s.c).start()
+
+    def w_arrive(i):
+        h = lax.rem(s.h + 4 - i, 4)
+        w_plane(h, h).wait_recv()
+        w_twin(h, s.c).start()
+
+    each(4, w_arrive, 1)
+    each(4, lambda h: w_twin(h, 1 - s.c).wait_recv())
     outs = copies([(wa, wa_out)], out_sem)
-    qkv = dot_n(x[...], wa[...].reshape(512, 1536)).astype(bf16)
-    for m in range(2):
-        rows = slice(128 * m, 128 * m + 128)
-        for h in range(8):
-            kv_send[8 * m + h] = qkv[rows, 128 * h:128 * h + 128].reshape(8, 16, 128)
-        for t in range(4):
-            tile = qkv[rows, 1024 + 128 * t:1152 + 128 * t]
+    own_x.wait()
+    plane = [Plane(s, ex_send.at[k], ex_recv.at[k]) for k in range(2)]
+    kinds = ((kv_send, lambda g: kv_out.at[:, g, s.c]), (q_send, lambda g: q_out.at[:, g]))
+
+    def block(w, j, z):
+        src, dst = kinds[w]
+        return plane[w].copy(src.at[j, z], dst(s.h * 4 + z), j, j * 4 + z, s.h * 4 + z)
+
+    def from_block(w, j, z):
+        src, dst = kinds[w]
+        slot = dst(j * 4 + z)
+        return plane[w].copy(slot, slot, j, j * 4 + z, j * 4 + z)
+
+    def own_block(w, z):
+        src, dst = kinds[w]
+        return pltpu.make_async_copy(src.at[s.h, z], dst(s.h * 4 + z), ex_local.at[w, z])
+
+    def twin(src, j, z, c):
+        slot = kv_out.at[:, j * 4 + z, c]
+        k = j * 4 + z
+        return remote(slot if src is None else src, slot, tw_send.at[k], tw_recv.at[k], s.h, s.z * 2 + 1 - s.c)
+
+    def project_rows(k):
+        z = s.ahead(k)
+        qkv = dot_n(x_all[z], wa[:, :, :, :, 0:768].reshape(512, 768)).astype(bf16)
+        for j in range(4):
+            kv_send[j, z] = qkv[:, 128 * j:128 * j + 128].reshape(8, 16, 128)
+        for t in range(2):
+            tile = qkv[:, 512 + 128 * t:640 + 128 * t]
             first, second = weave(tile[0:64], tile[64:128])
-            q_send[8 * m + 2 * t] = first.reshape(4, 16, 128)
-            q_send[8 * m + 2 * t + 1] = second.reshape(4, 16, 128)
-    kv_ex = Exchange(
-        s, lambda p: kv_send.at[p], lambda g: kv_out.at[:, g, s.c], ex_send.at[0], ex_recv.at[0], ex_local.at[0]
-    )
-    q_ex = Exchange(s, lambda p: q_send.at[p], lambda g: q_out.at[:, g], ex_send.at[1], ex_recv.at[1], ex_local.at[1])
-    kv_ex.begin()
-    q_ex.begin()
-    for job in jobs[2:]:
-        job.spread()
+            q_send[2 * t, z] = first.reshape(4, 16, 128)
+            q_send[2 * t + 1, z] = second.reshape(4, 16, 128)
+        for w in range(2):
+            each(4, lambda i: block(w, plane[w].to(i), z).start(), 1)
+            own_block(w, z).start()
+        twin(kv_send.at[s.h, z], s.h, z, s.c).start()
+
+    project_rows(0)
+
+    def project_next(k):
+        z = s.ahead(k)
+        pass_x(z, z).wait_recv()
+        project_rows(k)
+
+    each(s.nz, project_next, 1)
+    line.onward(0)
+    line.onward(1)
+    vecs = wa[:, :, :, :, 768:896].reshape(n, 16, 128).astype(f32)
+    outs += copies([(x_all, x_out)], out_sem.at[pl.ds(5, 1)])
     bup[...] = spread_row(vecs[:, 0, :], 2048, 64)
     for k in range(7):
         par[k:k + 1, :] = spread_row(vecs[:, k + 1, :], 512, 16)
     par[7:8, :] = jnp.zeros((1, 512), f32)
-    ids = jnp.where(kv_ex.g < 8, vecs[:, 8, :], vecs[:, 9, :]).astype(bf16)
+    ids = jnp.where(s.z < 2, vecs[:, 8, :], vecs[:, 9, :]).astype(bf16)
     for i in range(8):
         pick = (rows_of((128, 512)) == 16 * i + lax.rem(lanes((128, 512)), 16)).astype(f32).astype(bf16)
         wide = dot_n(ids, pick)
@@ -999,31 +1137,29 @@
         own = (source // 2 == lanes((n, 256)) // 16) & (lax.rem(source, 2) == s.c)
         segq[i:i + 1, :] = column_sum(jnp.where(own, wide[:, 0:256], 0.0)).astype(jnp.int32)
     outs += copies([(par, par_out), (bup, bup_out), (segk, segk_out), (segq, segq_out)], out_sem.at[pl.ds(1, 4)])
-    for job in jobs[2:]:
-        job.cross()
-
-    def twin(g, c):
-        slot = kv_out.at[:, g, c]
-        return remote(slot, slot, tw_send.at[g], tw_recv.at[g], s.h, s.z * 2 + 1 - s.c)
-
-    kv_ex.own().wait()
-    twin(kv_ex.g, s.c).start()
-
     def forward(i):
-        kv_ex.arrive(i)
-        twin(lax.rem(kv_ex.g + 16 - i, 16), s.c).start()
-
-    each(16, forward, 1)
-    for job in jobs[2:]:
-        job.last()
-    for job in jobs[2:]:
-        job.arrive()
-    each(16, lambda g: twin(g, 1 - s.c).wait_recv())
-    each(16, lambda g: twin(g, s.c).wait_send())
-    each(16, lambda i: kv_ex.copy(i).wait_send(), 1)
-    q_ex.end()
-    for job in jobs:
-        job.sent()
+        j = plane[0].frm(i)
+
+        def go(k):
+            z = s.ahead(k)
+            from_block(0, j, z).wait_recv()
+            twin(None, j, z, s.c).start()
+
+        each(s.nz, go)
+
+    each(4, forward, 1)
+    line.onward(2)
+    each(4, lambda i: each(s.nz, lambda z: from_block(1, plane[1].frm(i), z).wait_recv()), 1)
+    each(4, lambda j: each(s.nz, lambda z: twin(None, j, z, 1 - s.c).wait_recv()))
+    each(4, lambda j: each(s.nz, lambda z: twin(None, j, z, s.c).wait_send()))
+    for w in range(2):
+        each(s.nz, lambda z: own_block(w, z).wait())
+        each(4, lambda i: each(s.nz, lambda z: block(w, plane[w].to(i), z).wait_send()), 1)
+    each(s.nz, lambda k: pass_x(s.ahead(k), s.z).wait_send(), 1)
+    each(s.nz, lambda k: w_line(s.ahead(k), s.z).wait_send(), 1)
+    each(4, lambda i: w_plane(lax.rem(s.h + i, 4), s.h).wait_send(), 1)
+    each(4, lambda h: w_twin(h, s.c).wait_send())
+    line.sent()
     wait_all(outs)
 
 
@@ -1035,9 +1171,9 @@
         out_shape=(
             jax.ShapeDtypeStruct((4, 16, 16, 128), bf16),
             jax.ShapeDtypeStruct((8, 16, 2, 16, 128), bf16),
-            jax.ShapeDtypeStruct((n, 16, 1536), bf16),
-            jax.ShapeDtypeStruct((n, 16, 2560), bf16),
-            jax.ShapeDtypeStruct((n, 64, 512), bf16),
+            jax.ShapeDtypeStruct((nz, 128, 512), bf16),
+            jax.ShapeDtypeStruct((4, nz, 2, 16, 896), bf16),
+            jax.ShapeDtypeStruct((nz, 16, 4608), bf16),
             jax.ShapeDtypeStruct((8, 512), f32),
             jax.ShapeDtypeStruct((1, 2048), f32),
             jax.ShapeDtypeStruct((8, 512), jnp.int32),
@@ -1057,26 +1193,32 @@
             *[pltpu.VMEM((16,), bf16)] * 7,
             pltpu.VMEM((64,), bf16),
             pltpu.VMEM((16, 128), f32),
-            pltpu.VMEM((n, 16, 128), f32),
-            pltpu.VMEM((16, 1536), bf16),
-            pltpu.VMEM((16, 2560), bf16),
-            pltpu.VMEM((n, 16, 1536), bf16),
-            pltpu.VMEM((16, 8, 16, 128), bf16),
-            pltpu.VMEM((16, 4, 16, 128), bf16),
+            pltpu.VMEM((2, 16, 896), bf16),
+            pltpu.VMEM((16, 4608), bf16),
+            pltpu.VMEM((4, nz, 2, 16, 896), bf16),
+            pltpu.VMEM((nz, 128, 512), bf16),
+            pltpu.VMEM((4, nz, 8, 16, 128), bf16),
+            pltpu.VMEM((4, nz, 4, 16, 128), bf16),
             pltpu.VMEM((8, 512), f32),
             pltpu.VMEM((1, 2048), f32),
             pltpu.VMEM((8, 512), jnp.int32),
             pltpu.VMEM((8, 256), jnp.int32),
             dma((16,)),
-            dma((5,)),
-            dma((4, 9 * nz)),
-            dma((4, 9 * nz)),
-            dma((4,)),
-            dma((2, 16)),
-            dma((2, 16)),
-            dma((2,)),
-            dma((16,)),
-            dma((16,)),
+            dma((6,)),
+            dma((12,)),
+            dma((12,)),
+            dma,
+            dma((2 * nz,)),
+            dma((2 * nz,)),
+            dma,
+            dma((nz,)),
+            dma((nz,)),
+            dma,
+            dma((2, 4 * nz)),
+            dma((2, 4 * nz)),
+            dma((2, nz)),
+            dma((4 * nz,)),
+            dma((4 * nz,)),
         ],
         compiler_params=pltpu.CompilerParams(
             collective_id=1, has_side_effects=True, vmem_limit_bytes=VMEM_BYTES
@@ -1106,27 +1248,49 @@
 
 
 def middle_kernel(n, nb, *refs):
-    o_hbm, x_hbm, y_hbm, g_hbm, wb_hbm, wd_hbm, par_hbm, bup_hbm = refs[:8]
-    outs_hbm = refs[9:20]
-    do_out = refs[8]
+    o_hbm, x_hbm, y_hbm, g_hbm, fz_hbm, fx_hbm, fy_hbm, par_hbm, bup_hbm = refs[:9]
+    outs_hbm = refs[10:20]
+    do_out = refs[9]
     (
         o_in, x, y, g_in, wb, wd, par, bup, o_recv, do_send, slope,
         out, dacc_ref, dz1_ref, x1_ref, dur_ref, hid_ref, dfr_ref, omix, dar_ref, gvec, bias_up,
-        in_sem, out_sem, ex_send, ex_recv, ex_local,
+        in_sem, out_sem, ex_send, ex_recv, ex_local, f_send, f_recv,
     ) = refs[20:]
     s = Spot(nb)
     loads = copies(
-        [(o_hbm, o_in), (x_hbm, x), (y_hbm, y), (g_hbm, g_in), (par_hbm, par), (bup_hbm, bup), (wb_hbm, wb), (wd_hbm, wd)],
+        [
+            (o_hbm, o_in), (x_hbm, x), (y_hbm, y), (g_hbm, g_in), (par_hbm, par), (bup_hbm, bup),
+            (fz_hbm, wb.at[s.h, :, s.c]), (fx_hbm, wb.at[s.near[0], :, s.c]), (fy_hbm, wb.at[s.near[1], :, s.c]),
+        ],
         in_sem,
     )
     greet_all(n, nb, s.me)
     loads[0].wait()
     o_ex = Exchange(
-        s, lambda p: o_in.at[:, p], lambda g: o_recv.at[g], ex_send.at[0], ex_recv.at[0], ex_local.at[0]
+        s, lambda g: o_in.at[:, g], lambda g: o_recv.at[pair_of(g)], ex_send.at[0], ex_recv.at[0], ex_local.at[0]
     )
     o_ex.begin()
+    cut = [pl.ds(0, 2304), pl.ds(2304, 2304)]
+    heads = (s.h, s.near[0], s.near[1], s.diag)
+
+    def onward(w, h, to):
+        src = (fx_hbm, fy_hbm)[w].at[:, :, cut[w]]
+        return remote(src, wb.at[h, :, s.c, :, cut[w]], f_send.at[4 + w], f_recv.at[4 + w], to, s.z * 2 + s.c)
+
+    def twin(k, c):
+        slot = wb.at[heads[k], :, c]
+        src = (fz_hbm, fx_hbm, fy_hbm, slot)[k]
+        return remote(src, slot, f_send.at[k], f_recv.at[k], s.h, s.z * 2 + 1 - s.c)
+
+    for w in range(2):
+        onward(w, s.near[w], s.near[1 - w]).start()
+    for k in range(3):
+        twin(k, s.c).start()
+    for w in range(2):
+        onward(w, s.diag, s.near[1 - w]).wait_recv()
+    twin(3, s.c).start()
+    o_ex.end()
     wait_all(loads[1:])
-    o_ex.end()
     for m in range(2):
         for t in range(4):
             first, second = weave(
@@ -1137,7 +1301,12 @@
     gain1, bias1 = par[1:2], par[2:3]
     gain2, bias2 = par[3:4], par[4:5]
     gain3, bias3 = par[5:6], par[6:7]
-    w_out = wb[:, :, 0:512].reshape(512, 512)
+    for k in range(4):
+        twin(k, 1 - s.c).wait_recv()
+    for t in range(4):
+        for r in range(4):
+            wd[t, :, :, r] = wb[t, :, :, :, 2560 + 512 * r:3072 + 512 * r]
+    w_out = wb[:, :, :, :, 0:512].reshape(512, 512)
     a = dot_n(omix[...], w_out)
     n1, r1 = row_norm(x[...].astype(f32) + a)
     x1 = n1 * gain1 + bias1
@@ -1146,12 +1315,12 @@
     feed = jnp.zeros_like(x1)
     for t in range(4):
         cols = slice(512 * t, 512 * t + 512)
-        u = dot_n(x1r, wb[:, :, 512 + 512 * t:1024 + 512 * t].reshape(512, 512)) + bup[:, cols]
+        u = dot_n(x1r, wb[:, :, :, :, 512 + 512 * t:1024 + 512 * t].reshape(512, 512)) + bup[:, cols]
         phi = 0.5 * (1.0 + lax.erf(u * (0.5**0.5)))
         hid = (u * phi).astype(bf16)
         slope[:, cols] = phi + u * jnp.exp(-0.5 * u * u) * ((2.0 * math.pi) ** -0.5)
         hid_ref[:, cols] = hid
-        feed = feed + dot_n(hid, wd[8 * t:8 * t + 8].reshape(512, 512))
+        feed = feed + dot_n(hid, wd[t].reshape(512, 512))
     feed = feed + par[0:1]
     n2, r2 = row_norm(x1 + feed)
     n3, r3 = row_norm(y[...].astype(f32) + a + feed)
@@ -1166,11 +1335,11 @@
     dx1 = dz2
     for t in range(4):
         cols = slice(512 * t, 512 * t + 512)
-        du = dot_t(dfr, wd[8 * t:8 * t + 8].reshape(512, 512)) * slope[:, cols]
+        du = dot_t(dfr, wd[t].reshape(512, 512)) * slope[:, cols]
         bias_up[:, cols] = column_sum(du)
         dur = du.astype(bf16)
         dur_ref[:, cols] = dur
-        dx1 = dx1 + dot_t(dur, wb[:, :, 512 + 512 * t:1024 + 512 * t].reshape(512, 512))
+        dx1 = dx1 + dot_t(dur, wb[:, :, :, :, 512 + 512 * t:1024 + 512 * t].reshape(512, 512))
     dz1 = row_norm_back(dx1, n1, r1, gain1)
     dz1_ref[...] = dz1
     dar = (dz1 + dacc).astype(bf16)
@@ -1183,7 +1352,7 @@
             do_send[8 * m + 2 * t] = first.reshape(4, 16, 128)
             do_send[8 * m + 2 * t + 1] = second.reshape(4, 16, 128)
     do_ex = Exchange(
-        s, lambda p: do_send.at[p], lambda g: do_out.at[:, g], ex_send.at[1], ex_recv.at[1], ex_local.at[1]
+        s, lambda g: do_send.at[pair_of(g)], lambda g: do_out.at[:, g], ex_send.at[1], ex_recv.at[1], ex_local.at[1]
     )
     do_ex.begin()
     stores = copies(
@@ -1199,10 +1368,14 @@
         gvec[:, k + 1, :] = gather_row(sums[k], n, 16)
     stores += copies([(gvec, outs_hbm[9])], out_sem.at[pl.ds(9, 1)])
     do_ex.end()
+    for w in range(2):
+        onward(w, s.near[w], s.near[1 - w]).wait_send()
+    for k in range(4):
+        twin(k, s.c).wait_send()
     wait_all(stores)
 
 
-def middle(n, nb, o, x, y, g, wb, wd, par, bup):
+def middle(n, nb, o, x, y, g, fz, fx, fy, par, bup):
     dma = pltpu.SemaphoreType.DMA
     rows = x.shape[0]
     saved = [
@@ -1212,17 +1385,16 @@
     return pl.pallas_call(
         functools.partial(middle_kernel, n, nb),
         out_shape=[jax.ShapeDtypeStruct((4, 16, 16, 128), bf16)]
-        + [jax.ShapeDtypeStruct(shape, kind) for shape, kind in saved]
-        + [jax.ShapeDtypeStruct((8, 128), f32)],
-        in_specs=any_specs(8),
-        out_specs=any_specs(12),
+        + [jax.ShapeDtypeStruct(shape, kind) for shape, kind in saved],
+        in_specs=any_specs(9),
+        out_specs=any_specs(11),
         scratch_shapes=[
             pltpu.VMEM(o.shape, bf16),
             pltpu.VMEM(x.shape, bf16),
             pltpu.VMEM(x.shape, bf16),
             pltpu.VMEM(x.shape, bf16),
-            pltpu.VMEM(wb.shape, bf16),
-            pltpu.VMEM(wd.shape, bf16),
+            pltpu.VMEM((4, nb // 2, 2, 16, 4608), bf16),
+            pltpu.VMEM((4, 4, 2, 4, 16, 512), bf16),
             pltpu.VMEM(par.shape, f32),
             pltpu.VMEM(bup.shape, f32),
             pltpu.VMEM((16, 4, 16, 128), bf16),
@@ -1230,31 +1402,33 @@
             pltpu.VMEM((rows, 2048), f32),
             *[pltpu.VMEM(shape, kind) for shape, kind in saved],
             pltpu.VMEM((1, 2048), f32),
-            dma((8,)),
+            dma((9,)),
             dma((10,)),
             dma((2, 16)),
             dma((2, 16)),
             dma((2,)),
+            dma((6,)),
+            dma((6,)),
         ],
         compiler_params=pltpu.CompilerParams(
             collective_id=2, has_side_effects=True, vmem_limit_bytes=VMEM_BYTES
         ),
         name="middle",
-    )(o, x, y, g, wb, wd, par, bup)[:11]
+    )(o, x, y, g, fz, fx, fy, par, bup)
 
 
 def finish_kernel(n, nb, *refs):
     ins = refs[:12]
     outs = refs[12:20]
     (
-        dq, dkv, x, dz1, x1, dur, hid, dfr, omix, dar, gvec, wa,
+        dq, dkv, xm, dz1, x1, dur, hid, dfr, omix, dar, gvec, wa,
         pa, ta, da, na, la, pb, tb, db, nb_, lb, pd, td, dd, nd, ld, tv, dv, nv, lv,
-        twin_buf, dkv_send, dkv_recv, dq_recv, dqkv, gx, gq, gk, gv, go, gu, gd, gs,
-        in_sem, out_sem, rs_send, rs_recv, ex_send, ex_recv, ex_local, tw_send, tw_recv,
+        twin_buf, dkv_send, dkv_recv, dq_recv, dqkv, dx_send, dx_recv, gx, gq, gk, gv, go, gu, gd, gs,
+        in_sem, out_sem, rs_send, rs_recv, ex_send, ex_recv, dx_ssem, dx_rsem, tw_send, tw_recv,
     ) = refs[20:]
     s = Spot(nb)
-    order = (1, 10, 8, 9, 4, 5, 6, 7, 0, 2, 3, 11)
-    local = (dq, dkv, x, dz1, x1, dur, hid, dfr, omix, dar, gvec, wa)
+    order = (1, 0, 10, 8, 9, 4, 5, 6, 7, 2, 11, 3)
+    local = (dq, dkv, xm, dz1, x1, dur, hid, dfr, omix, dar, gvec, wa)
     loads = copies([(ins[k], local[k]) for k in order], in_sem)
     greet_all(n, nb, s.me)
     swap = remote(ins[1].at[:, :, 1 - s.c], twin_buf, tw_send, tw_recv, s.h, s.z * 2 + 1 - s.c)
@@ -1265,53 +1439,78 @@
             ((pb, tb, db, nb_, lb), (pd, td, dd, nd, ld), (gvec, tv, dv, nv, lv), (pa, ta, da, na, la))
         )
     ]
-    wait_all(loads[:6])
+    swap.wait()
+    wait_all(loads[:2])
+
+    def add(g):
+        dkv_send[g] = (dkv[:, g, s.c].astype(f32) + twin_buf[:, g].astype(f32)).astype(bf16)
+
+    each(4 * s.nz, add)
+    plane = [Plane(s, ex_send.at[k], ex_recv.at[k]) for k in range(2)]
+
+    def block(w, j, slot):
+        group = pl.ds(j * s.nz, s.nz)
+        src, dst = ((dkv_send.at[group], dkv_recv.at[slot]), (dq.at[:, group], dq_recv.at[slot]))[w]
+        return plane[w].copy(src, dst, j, j, slot)
+
+    for w in range(2):
+        each(4, lambda i: block(w, plane[w].to(i), s.h).start(), 1)
+    wait_all(loads[2:8])
     jobs[2].begin()
     pb[:, :, 0:512] = dot_0(omix[...], dar[...]).astype(bf16).reshape(n, 16, 512)
     for t in range(4):
         cols = slice(512 * t, 512 * t + 512)
         pb[:, :, 512 + 512 * t:1024 + 512 * t] = dot_0(x1[...], dur[:, cols]).astype(bf16).reshape(n, 16, 512)
     jobs[0].begin()
-    wait_all(loads[6:])
+    wait_all(loads[8:])
     for t in range(4):
         cols = slice(512 * t, 512 * t + 512)
         pd[8 * t:8 * t + 8] = dot_0(hid[:, cols], dfr[...]).astype(bf16).reshape(8, 64, 512)
     jobs[1].begin()
-    swap.wait()
-
-    def add(g):
-        dkv_send[g] = (dkv[:, g, s.c] + twin_buf[:, g]).astype(bf16)
-
-    each(16, add)
-    kv_ex = Exchange(
-        s, lambda p: dkv_send.at[p], lambda g: dkv_recv.at[g], ex_send.at[0], ex_recv.at[0], ex_local.at[0]
-    )
-    q_ex = Exchange(s, lambda p: dq.at[:, p], lambda g: dq_recv.at[g], ex_send.at[1], ex_recv.at[1], ex_local.at[1])
-    kv_ex.begin()
-    q_ex.begin()
-    for job in jobs[:3]:
+
+    def own(z):
+        dkv_recv[s.h, z] = dkv_send[s.h * s.nz + z]
+        dq_recv[s.h, :, z] = dq[:, s.h * s.nz + z]
+
+    each(s.nz, own)
+    for job in jobs[:2]:
         job.first()
+    for w in range(2):
+        each(4, lambda i: block(w, plane[w].frm(i), plane[w].frm(i)).wait_recv(), 1)
+    for z in range(4):
+        rows = slice(128 * z, 128 * z + 128)
+        for j in range(4):
+            dqkv[rows, 128 * j:128 * j + 128] = dkv_recv[j, z].reshape(128, 128)
+        for t in range(2):
+            first, second = weave(
+                dq_recv[2 * t, :, z].reshape(64, 128), dq_recv[2 * t + 1, :, z].reshape(64, 128)
+            )
+            dqkv[128 * z:128 * z + 64, 512 + 128 * t:640 + 128 * t] = first
+            dqkv[128 * z + 64:128 * z + 128, 512 + 128 * t:640 + 128 * t] = second
+    weight = wa[:, :, :, :, 0:768].reshape(512, 768)
+    for z in range(4):
+        dx_send[z] = dot_t(dqkv[128 * z:128 * z + 128, :], weight).astype(bf16)
+
+    def back(z, slot):
+        return remote(dx_send.at[z], dx_recv.at[slot], dx_ssem.at[z], dx_rsem.at[slot], s.h, z * 2 + s.c)
+
+    each(s.nz, lambda k: back(s.ahead(k), s.z).start(), 1)
+    dx_recv[s.z] = dx_send[s.z]
+    tokens = xm[...].reshape(512, 512)
+    pa[...] = dot_0(tokens, dqkv[...]).astype(bf16).reshape(n, 16, 768)
+    jobs[3].begin()
+    jobs[2].first()
     for job in jobs[:3]:
         job.second()
+    jobs[3].first()
     for job in jobs[:3]:
         job.third()
-    kv_ex.end()
-    q_ex.end()
+    jobs[3].second()
+    jobs[3].third()
+    each(s.nz, lambda k: back(s.ahead(k), s.ahead(k)).wait_recv(), 1)
     for m in range(2):
         rows = slice(128 * m, 128 * m + 128)
-        for h in range(8):
-            dqkv[rows, 128 * h:128 * h + 128] = dkv_recv[8 * m + h].reshape(128, 128)
-        for t in range(4):
-            first, second = weave(
-                dq_recv[8 * m + 2 * t].reshape(64, 128), dq_recv[8 * m + 2 * t + 1].reshape(64, 128)
-            )
-            dqkv[128 * m:128 * m + 64, 1024 + 128 * t:1152 + 128 * t] = first
-            dqkv[128 * m + 64:128 * m + 128, 1024 + 128 * t:1152 + 128 * t] = second
-    for t in range(3):
-        cols = slice(512 * t, 512 * t + 512)
-        pa[:, :, cols] = dot_0(x[...], dqkv[:, cols]).astype(bf16).reshape(n, 16, 512)
-    jobs[3].begin()
-    gx[...] = dz1[...] + dot_t(dqkv[...], wa[...].reshape(512, 1536))
+        gx[rows, :] = dz1[rows, :] + (dx_recv[2 * m].astype(f32) + dx_recv[2 * m + 1].astype(f32))
     stores = copies([(gx, outs[0])], out_sem)
     total = jobs[0].total()
     go[...] = total[:, 0:512]
@@ -1319,25 +1518,26 @@
     gd[...] = jobs[1].total()
     gs[...] = jobs[2].total()
     stores += copies(zip((go, gu, gd, gs), outs[4:8]), out_sem.at[pl.ds(1, 4)])
-    jobs[3].first()
-    jobs[3].second()
-    jobs[3].third()
-    total = jobs[3].total()
-    gq[...] = total[:, 1024:1536]
-    for t in range(4):
-        first, second = weave(total[:, 256 * t:256 * t + 128], total[:, 256 * t + 128:256 * t + 256])
-        gk[:, 128 * t:128 * t + 128] = first
-        gv[:, 128 * t:128 * t + 128] = second
+    for w, part in enumerate(jobs[3].columns()):
+        gq[:, 256 * w:256 * w + 256] = part[:, 512:768]
+        for t in range(2):
+            first, second = weave(part[:, 256 * t:256 * t + 128], part[:, 256 * t + 128:256 * t + 256])
+            at = 256 * w + 128 * t
+            gk[:, at:at + 128] = first
+            gv[:, at:at + 128] = second
     stores += copies(zip((gq, gk, gv), outs[1:4]), out_sem.at[pl.ds(5, 3)])
+    for w in range(2):
+        each(4, lambda i: block(w, plane[w].to(i), s.h).wait_send(), 1)
+    each(s.nz, lambda k: back(s.ahead(k), s.z).wait_send(), 1)
     for job in jobs:
         job.sent()
     wait_all(stores)
 
 
-def finish(n, nb, dq, dkv, x, dz1, x1, dur, hid, dfr, omix, dar, gvec, wa):
+def finish(n, nb, dq, dkv, xm, dz1, x1, dur, hid, dfr, omix, dar, gvec, wa):
     dma = pltpu.SemaphoreType.DMA
     nz = nb // 2
-    rows = x.shape[0]
+    rows = dz1.shape[0]
 
     def buffers(depth, width, kind):
         return [
@@ -1348,7 +1548,7 @@
             pltpu.VMEM((nz, depth, width), kind),
         ]
 
-    args = (dq, dkv, x, dz1, x1, dur, hid, dfr, omix, dar, gvec, wa)
+    args = (dq, dkv, xm, dz1, x1, dur, hid, dfr, omix, dar, gvec, wa)
     shapes = ((rows, 512), (16, 512), (16, 512), (16, 512), (16, 512), (16, 2048), (64, 512), (16, 128))
     return pl.pallas_call(
         functools.partial(finish_kernel, n, nb),
@@ -1357,25 +1557,28 @@
         out_specs=any_specs(8),
         scratch_shapes=[
             *[pltpu.VMEM(arg.shape, arg.dtype) for arg in args],
-            *buffers(16, 1536, bf16),
+            *buffers(16, 768, bf16),
             *buffers(16, 2560, bf16),
             *buffers(64, 512, bf16),
             *buffers(16, 128, f32)[1:2],
             pltpu.VMEM((2, nz, 8, 128), f32),
             *buffers(16, 128, f32)[3:],
-            pltpu.VMEM((8, 16, 16, 128), f32),
+            pltpu.VMEM((8, 16, 16, 128), bf16),
             pltpu.VMEM((16, 8, 16, 128), bf16),
-            pltpu.VMEM((16, 8, 16, 128), bf16),
-            pltpu.VMEM((16, 4, 16, 128), bf16),
-            pltpu.VMEM((rows, 1536), bf16),
+            pltpu.VMEM((4, nz, 8, 16, 128), bf16),
+            pltpu.VMEM((4, 4, nz, 16, 128), bf16),
+            pltpu.VMEM((512, 768), bf16),
+            pltpu.VMEM((nz, 128, 512), bf16),
+            pltpu.VMEM((nz, 128, 512), bf16),
             *[pltpu.VMEM(shape, f32) for shape in shapes],
             dma((12,)),
             dma((8,)),
             dma((4, 9 * nz)),
             dma((4, 9 * nz)),
-            dma((2, 16)),
-            dma((2, 16)),
-            dma((2,)),
+            dma((2, 4)),
+            dma((2, 4)),
+            dma((nz,)),
+            dma((nz,)),
             dma,
             dma,
         ],
@@ -1433,18 +1636,19 @@
     y = accumulator.reshape(256, 512)
     g = upstream.reshape(256, 512)
     smalls = (b_up, b_down, gain_attn, bias_attn, gain_ffn, bias_ffn, gain_final, bias_final)
-    q, kv, wa, wb, wd, par, bup, seg_k, seg_q = project(
-        n, nb, x, w_query, w_key, w_value, w_out, w_up, w_down, segment_ids.reshape(2, 128), smalls
-    )
+    q, kv, xm, wa, fz, par, bup, seg_k, seg_q = project(
+        n, nb, stream.reshape(2, 128, 512), w_query, w_key, w_value, w_out, w_up, w_down, segment_ids.reshape(2, 128), smalls
+    )
+    fx, fy = (lax.ppermute(fz, "head", [(h, h ^ w) for h in range(4)]) for w in (1, 2))
     o, of, lse, kv2, kvt = attn_fwd(q.reshape(4, 256, 128), kv.reshape(4096, 128), seg_q, seg_k)
     do, out, dacc, dz1, x1, dur, hid, dfr, omix, dar, gvec = middle(
-        n, nb, o.reshape(4, 16, 16, 128), x, y, g, wb, wd, par, bup
+        n, nb, o.reshape(4, 16, 16, 128), x, y, g, fz, fx, fy, par, bup
     )
     dq, dkv, out, dacc = attn_bwd(
         q.reshape(4, 256, 128), do.reshape(4, 256, 128), of, lse, kv2, kvt, seg_q, seg_k, out, dacc
     )
     gx, gq, gk, gv, go, gu, gd, gs = finish(
-        n, nb, dq.reshape(4, 16, 16, 128), dkv.reshape(8, 16, 2, 16, 128), x, dz1, x1, dur, hid, dfr, omix, dar, gvec, wa
+        n, nb, dq.reshape(4, 16, 16, 128), dkv.reshape(8, 16, 2, 16, 128), xm, dz1, x1, dur, hid, dfr, omix, dar, gvec, wa
     )
     gx, gq, gk, gv, go, gu, gd, gbu, *small_grads = deliver((gx, gq, gk, gv, go, gu, gd), gs)
     return (

time: 178 us -> 158 us (0.89)
  Pallas kernels: 177 us -> 154 us
    pallas_call x1, Pallas kernels: 54.2 us -> 37.5 us  [project(): pl.pallas_call(functools.partial(project_kernel, n, nb), out_shape=(jax.S...]
    pallas_call x1, Pallas kernels: 56.7 us -> 50.1 us  [finish(): pl.pallas_call(functools.partial(finish_kernel, n, nb), out_shape=[jax.Sh...]
  transfers between devices with their start and end apart: 0 -> 2, of which waited for: 0 -> 0; matrix products, arithmetic and copies ran while one was open for 0% -> 0% of each run, Pallas kernels for 0% -> 9%
where the time goes in v4:
time: 158 us
  Pallas kernels  154 us (97%)
  starting transfers between devices  1.76 us (1%)
    pallas_call x1, Pallas kernels, finish(): pl.pallas_call(functools.partial(finish_kernel, n, nb), out_shape=[jax.Sh...  50.1 us
    pallas_call x1, Pallas kernels, project(): pl.pallas_call(functools.partial(project_kernel, n, nb), out_shape=(jax.S...  37.5 us
    pallas_call x1, Pallas kernels, middle(): pl.pallas_call(functools.partial(middle_kernel, n, nb), out_shape=[jax.Sh...  31.1 us
    pallas_call x1, Pallas kernels, attn_bwd(): pl.pallas_call(attn_bwd_kernel, out_shape=[jax.ShapeDtypeStruct(shape, ki...  19.1 us
    pallas_call x1, Pallas kernels, attn_fwd(): pl.pallas_call(attn_fwd_kernel, out_shape=[jax.ShapeDtypeStruct(shape, ki...  14.2 us
  transfers between devices with their start and end apart: 2, of which 0 were waited for; matrix products, arithmetic and copies ran while one was open for 0% of the time, Pallas kernels for 9%

profile of v4, /device:TPU:0, one launch (start us, length us, event | category | flops | bytes accessed | tf_op | source)
XLA Modules:
  0.0 157.9 jit_solution(2096384414568753639)
XLA Ops:
  0.7 37.5 %project.1 = (bf16[4,16,16,128]{3,2,1,0:T(8,128)(2,1)}, bf16[8,16,2,16,128]{4,3,2,1,0:T(8,128)(2,1)}, bf16[4,128,512]{2,1,0:T(8,128)(2,1)}, bf16[4,4,2,16,896]{4...) custom-call(bf16[2,128,512]{2,1,0:T(8,128)(2,1)} %bitcast.21, ...), custom_call_target="tpu_custom_call" | custom-call | tf_op jit(solution)/shard_map/project/pallas_call | solution.py:1169
  38.2 1.0 collective-permute-start.1
  39.2 0.8 collective-permute-start
  39.9 14.2 %attn_fwd.1 = (bf16[4,256,128]{2,1,0:T(8,128)(2,1)}, f32[4,256,128]{2,1,0:T(8,128)}, f32[8,256]{1,0:T(8,128)}, bf16[4096,256]{1,0:T(8,128)(2,1)}, bf16[256,4096]{1,0:T(8,128)(2,1)}) custom-call(bf16[4,256,128]{2,1,0:T(8,128)(2,1)} %bitcast.23, bf16[4096,128]{1,0:T(8,128)(2,1)} %bitcast.31, s32[8,256]{1,0:T(8,128)} %get-tuple-element.71.seg_q_hbm, ...), custom_call_target="tpu_custom_call" | custom-call | flops 10000000000 | bytes 10000000 | tf_op jit(solution)/shard_map/attn_fwd/pallas_call | solution.py:458
  54.2 0.0 collective-permute-done.1.refs_6_
  54.2 0.0 copy-start
  54.2 0.0 collective-permute-done.refs_5_
  54.2 0.0 copy-start.1
  54.2 0.8 copy-done
  55.0 0.2 copy-done.1
  55.3 31.1 %middle.1 = (bf16[4,16,16,128]{3,2,1,0:T(8,128)(2,1)}, bf16[256,512]{1,0:T(8,128)(2,1)}, f32[256,512]{1,0:T(8,128)}, f32[256,512]{1,0:T(8,128)}, bf16[256,512]{1...) custom-call(bf16[4,16,16,128]{3,2,1,0:T(8,128)(2,1)} %bitcast.29, ...), custom_call_target="tpu_custom_call" | custom-call | tf_op jit(solution)/shard_map/middle/pallas_call | solution.py:1385
  86.3 19.1 %attn_bwd.1 = (bf16[4,256,128]{2,1,0:T(8,128)(2,1)}, bf16[4096,128]{1,0:T(8,128)(2,1)}, bf16[256,512]{1,0:T(8,128)(2,1)}, f32[256,512]{1,0:T(8,128)}) custom-call(bf16[4,256,128]{2,1,0:T(8,128)(2,1)} %bitcast.24, bf16[4,256,128]{2,1,0:T(8,128)(2,1)} %bitcast.26, f32[4,256,128]{2,1,0:T(8,128)} %get-tuple-element.78.of_hbm, ...), custom_call_target="tpu_custom_call" | custom-call | tf_op jit(solution)/shard_map/attn_bwd/pallas_call | solution.py:539
  105.5 50.1 %finish.1 = (f32[256,512]{1,0:T(8,128)}, f32[16,512]{1,0:T(8,128)}, f32[16,512]{1,0:T(8,128)}, f32[16,512]{1,0:T(8,128)}, f32[16,512]{1,0:T(8,128)}, /*index=5*/...) custom-call(bf16[4,16,16,128]{3,2,1,0:T(8,128)(2,1)} %bitcast.25, bf16[8,16,2,16,128]{4,3,2,1,0:T(8,128)(2,1)} %bitcast.20, ...), custom_call_target="tpu_custom_call" | custom-call | tf_op jit(solution)/shard_map/finish/pallas_call | solution.py:1553
  155.6 2.2 %deliver.1 = (f32[256,512]{1,0:T(8,128)}, f32[16,512]{1,0:T(8,128)}, f32[16,512]{1,0:T(8,128)}, f32[16,512]{1,0:T(8,128)}, f32[16,512]{1,0:T(8,128)}, /*index=5*...) custom-call(f32[256,512]{1,0:T(8,128)} %get-tuple-element.97.refs_0_, ...), custom_call_target="tpu_custom_call" | custom-call | tf_op jit(solution)/shard_map/deliver/pallas_call | solution.py:1612
Async XLA Ops:
  38.2 16.0 %collective-permute-start.1 = (bf16[4,16,4608]{2,1,0:T(8,128)(2,1)}, bf16[4,16,4608]{2,1,0:T(8,128)(2,1)S(1)}, u32[]{:S(2)}, u32[]{:S(2)}) collective-permute-start(bf16[4,16,4608]{2,1,0:T(8,128)(2,1)} %get-tuple-element.74.refs_4_), channel_id=1, source_target_pairs={{0,16},{8,24},{16,0},{24,8},{1,17},{9,25},{17,1},{25,9},{2,18},{10... | collective-permute-start | bytes 1769480 | tf_op jit(solution)/shard_map/ppermute | solution.py:1642
  39.2 15.0 %collective-permute-start = (bf16[4,16,4608]{2,1,0:T(8,128)(2,1)}, bf16[4,16,4608]{2,1,0:T(8,128)(2,1)S(1)}, u32[]{:S(2)}, u32[]{:S(2)}) collective-permute-start(bf16[4,16,4608]{2,1,0:T(8,128)(2,1)} %get-tuple-element.74.refs_4_), channel_id=1, source_target_pairs={{0,8},{8,0},{16,24},{24,16},{1,9},{9,1},{17,25},{25,17},{2,10},{10... | collective-permute-start | bytes 1769480 | tf_op jit(solution)/shard_map/ppermute | solution.py:1642
  54.2 0.9 copy-start
  54.2 1.1 copy-start.1

commit v5 on v4

--- a/solution.py
+++ b/solution.py
@@ -591,17 +591,29 @@
     lax.fori_loop(start, count, run, 0)
 
 
-def greet_all(n, nb, me):
-    barrier = pltpu.get_barrier_semaphore()
-
+def hail(h, b):
+    pl.semaphore_signal(
+        pltpu.get_barrier_semaphore(), inc=1, device_id={"head": h, "blk": b}, device_id_type=MESH
+    )
+
+
+def greet_near(s):
+    for k in range(1, s.nz):
+        hail(s.h, s.ahead(k) * 2 + s.c)
+    for i in range(1, 4):
+        hail(lax.rem(s.h + i, 4), s.z * 2 + s.c)
+    hail(s.h, s.z * 2 + 1 - s.c)
+    pl.semaphore_wait(pltpu.get_barrier_semaphore(), s.nz + 3)
+
+
+def greet_core(s):
     def signal(i):
-        t = lax.rem(me + i, n)
-        pl.semaphore_signal(
-            barrier, inc=1, device_id={"head": t // nb, "blk": lax.rem(t, nb)}, device_id_type=MESH
-        )
-
-    each(n, signal, 1)
-    pl.semaphore_wait(barrier, n - 1)
+        t = lax.rem(s.me + 2 * i, 4 * s.nb)
+        hail(t // s.nb, lax.rem(t, s.nb))
+
+    each(2 * s.nb, signal, 1)
+    hail(s.h, s.z * 2 + 1 - s.c)
+    pl.semaphore_wait(pltpu.get_barrier_semaphore(), 2 * s.nb)
 
 
 def halves(shape):
@@ -741,7 +753,7 @@
         return remote(src, dst, self.send.at[k], self.recv.at[recv_k], h, z * 2 + c)
 
     def mine(self, h, z):
-        return self.s.index(h, z, self.s.c)
+        return h * self.s.nz + z if self.t is None else self.s.index(h, z, self.s.c)
 
     def to_twin(self, h, z):
         s = self.s
@@ -772,6 +784,8 @@
         each(4, lambda h: each(self.s.nz, lambda z: self.to_twin(h, z).start()))
 
     def pair(self, h, z):
+        if self.t is None:
+            return self.part[self.mine(h, z)].astype(f32)
         self.to_twin(h, z).wait_recv()
         return self.part[self.mine(h, z)].astype(f32) + self.t[h, z].astype(f32)
 
@@ -783,7 +797,8 @@
 
         def go(k):
             z = s.ahead(k)
-            self.keep(s.diag, z, self.pair(s.diag, z))
+            if self.t is not None:
+                self.keep(s.diag, z, self.pair(s.diag, z))
             for w in range(2):
                 self.to_diag(w, z).start()
 
@@ -844,7 +859,8 @@
         s = self.s
 
         def go(z):
-            each(4, lambda h: self.to_twin(h, z).wait_send())
+            if self.t is not None:
+                each(4, lambda h: self.to_twin(h, z).wait_send())
             for w in range(2):
                 self.to_diag(w, z).wait_send()
                 self.to_near(w, z).wait_send()
@@ -1014,7 +1030,7 @@
         + [(x_hbm, x), (wo_hbm, wo), (wu_hbm, wu), (wd_hbm, wd)],
         in_sem,
     )
-    greet_all(n, nb, s.me)
+    greet_near(s)
 
     def pass_x(z, slot):
         return remote(x.at[z // 2], x_all.at[slot], x_send.at[z], x_recv.at[slot], s.h, z * 2 + s.c)
@@ -1243,19 +1259,29 @@
     )
 
 
+def normal(u):
+    bell = jnp.exp(-0.5 * u * u)
+    t = 1.0 / (1.0 + (0.3275911 * 0.5**0.5) * jnp.abs(u))
+    poly = 0.5 * 1.061405429
+    for factor in (-1.453152027, 1.421413741, -0.284496736, 0.254829592):
+        poly = poly * t + 0.5 * factor
+    tail = poly * t * bell
+    return jnp.where(u < 0, tail, 1.0 - tail), bell * ((2.0 * math.pi) ** -0.5)
+
+
 def column_sum(v):
     return jnp.sum(v, axis=0, keepdims=True)
 
 
 def middle_kernel(n, nb, *refs):
     o_hbm, x_hbm, y_hbm, g_hbm, fz_hbm, fx_hbm, fy_hbm, par_hbm, bup_hbm = refs[:9]
-    outs_hbm = refs[10:20]
+    outs_hbm = refs[10:16]
     do_out = refs[9]
     (
         o_in, x, y, g_in, wb, wd, par, bup, o_recv, do_send, slope,
-        out, dacc_ref, dz1_ref, x1_ref, dur_ref, hid_ref, dfr_ref, omix, dar_ref, gvec, bias_up,
-        in_sem, out_sem, ex_send, ex_recv, ex_local, f_send, f_recv,
-    ) = refs[20:]
+        out, dacc_ref, dz1_ref, gvec, sum_b, sum_d, bias_up, omix, hid_ref, dur_ref, po, pu, pd, to, tu, td,
+        in_sem, out_sem, ex_send, ex_recv, ex_local, f_send, f_recv, p_send, p_recv,
+    ) = refs[16:]
     s = Spot(nb)
     loads = copies(
         [
@@ -1264,7 +1290,7 @@
         ],
         in_sem,
     )
-    greet_all(n, nb, s.me)
+    greet_core(s)
     loads[0].wait()
     o_ex = Exchange(
         s, lambda g: o_in.at[:, g], lambda g: o_recv.at[pair_of(g)], ex_send.at[0], ex_recv.at[0], ex_local.at[0]
@@ -1311,14 +1337,13 @@
     n1, r1 = row_norm(x[...].astype(f32) + a)
     x1 = n1 * gain1 + bias1
     x1r = x1.astype(bf16)
-    x1_ref[...] = x1r
     feed = jnp.zeros_like(x1)
     for t in range(4):
         cols = slice(512 * t, 512 * t + 512)
         u = dot_n(x1r, wb[:, :, :, :, 512 + 512 * t:1024 + 512 * t].reshape(512, 512)) + bup[:, cols]
-        phi = 0.5 * (1.0 + lax.erf(u * (0.5**0.5)))
+        phi, density = normal(u)
         hid = (u * phi).astype(bf16)
-        slope[:, cols] = phi + u * jnp.exp(-0.5 * u * u) * ((2.0 * math.pi) ** -0.5)
+        slope[:, cols] = phi + u * density
         hid_ref[:, cols] = hid
         feed = feed + dot_n(hid, wd[t].reshape(512, 512))
     feed = feed + par[0:1]
@@ -1331,7 +1356,13 @@
     dz2 = row_norm_back(g, n2, r2, gain2)
     df = dz2 + dacc
     dfr = df.astype(bf16)
-    dfr_ref[...] = dfr
+    swaps = [
+        remote(part.at[:, :, 1 - s.c], there, p_send.at[k], p_recv.at[k], s.h, s.z * 2 + 1 - s.c)
+        for k, (part, there) in enumerate(((pd, td), (pu, tu), (po, to)))
+    ]
+    for t in range(4):
+        pd[t] = dot_0(hid_ref[:, 512 * t:512 * t + 512], dfr).astype(bf16).reshape(nb // 2, 2, 64, 512)
+    swaps[0].start()
     dx1 = dz2
     for t in range(4):
         cols = slice(512 * t, 512 * t + 512)
@@ -1343,7 +1374,6 @@
     dz1 = row_norm_back(dx1, n1, r1, gain1)
     dz1_ref[...] = dz1
     dar = (dz1 + dacc).astype(bf16)
-    dar_ref[...] = dar
     do = dot_t(dar, w_out).astype(bf16)
     for m in range(2):
         for t in range(4):
@@ -1355,9 +1385,13 @@
         s, lambda g: do_send.at[pair_of(g)], lambda g: do_out.at[:, g], ex_send.at[1], ex_recv.at[1], ex_local.at[1]
     )
     do_ex.begin()
-    stores = copies(
-        zip((out, dacc_ref, dz1_ref, x1_ref, dur_ref, hid_ref, dfr_ref, omix, dar_ref), outs_hbm[:9]), out_sem
-    )
+    stores = copies(zip((out, dacc_ref, dz1_ref), outs_hbm[:3]), out_sem)
+    for t in range(4):
+        cols = slice(512 * t, 512 * t + 512)
+        pu[:, :, :, :, cols] = dot_0(x1r, dur_ref[:, cols]).astype(bf16).reshape(4, nb // 2, 2, 16, 512)
+    swaps[1].start()
+    po[...] = dot_0(omix[...], dar).astype(bf16).reshape(po.shape)
+    swaps[2].start()
     sum_g = column_sum(g)
     sums = (
         column_sum(df), column_sum(dx1 * n1), column_sum(dx1), column_sum(g * n2), sum_g, column_sum(g * n3), sum_g
@@ -1366,7 +1400,18 @@
     gvec[:, 0, :] = gather_row(bias_up[...], n, 64)
     for k in range(7):
         gvec[:, k + 1, :] = gather_row(sums[k], n, 16)
-    stores += copies([(gvec, outs_hbm[9])], out_sem.at[pl.ds(9, 1)])
+    stores += copies([(gvec, outs_hbm[3])], out_sem.at[pl.ds(3, 1)])
+    for swap in swaps:
+        swap.wait()
+
+    def join(part, there):
+        value = part[:, :, s.c].astype(f32) + there[...].astype(f32)
+        return value.astype(bf16).reshape(-1, *value.shape[2:])
+
+    sum_d[...] = join(pd, td)
+    sum_b[:, :, 512:2560] = join(pu, tu)
+    sum_b[:, :, 0:512] = join(po, to)
+    stores += copies(zip((sum_b, sum_d), outs_hbm[4:6]), out_sem.at[pl.ds(4, 2)])
     do_ex.end()
     for w in range(2):
         onward(w, s.near[w], s.near[1 - w]).wait_send()
@@ -1378,16 +1423,17 @@
 def middle(n, nb, o, x, y, g, fz, fx, fy, par, bup):
     dma = pltpu.SemaphoreType.DMA
     rows = x.shape[0]
+    nz = nb // 2
     saved = [
-        ((rows, 512), bf16), ((rows, 512), f32), ((rows, 512), f32), ((rows, 512), bf16), ((rows, 2048), bf16),
-        ((rows, 2048), bf16), ((rows, 512), bf16), ((rows, 512), bf16), ((rows, 512), bf16), ((n, 16, 128), f32),
+        ((rows, 512), bf16), ((rows, 512), f32), ((rows, 512), f32), ((n, 16, 128), f32),
+        ((4 * nz, 16, 2560), bf16), ((4 * nz, 64, 512), bf16),
     ]
     return pl.pallas_call(
         functools.partial(middle_kernel, n, nb),
         out_shape=[jax.ShapeDtypeStruct((4, 16, 16, 128), bf16)]
         + [jax.ShapeDtypeStruct(shape, kind) for shape, kind in saved],
         in_specs=any_specs(9),
-        out_specs=any_specs(11),
+        out_specs=any_specs(7),
         scratch_shapes=[
             pltpu.VMEM(o.shape, bf16),
             pltpu.VMEM(x.shape, bf16),
@@ -1402,13 +1448,20 @@
             pltpu.VMEM((rows, 2048), f32),
             *[pltpu.VMEM(shape, kind) for shape, kind in saved],
             pltpu.VMEM((1, 2048), f32),
+            pltpu.VMEM((rows, 512), bf16),
+            pltpu.VMEM((rows, 2048), bf16),
+            pltpu.VMEM((rows, 2048), bf16),
+            *[pltpu.VMEM((4, nz, 2, *tail), bf16) for tail in ((16, 512), (16, 2048), (64, 512))],
+            *[pltpu.VMEM((4, nz, *tail), bf16) for tail in ((16, 512), (16, 2048), (64, 512))],
             dma((9,)),
-            dma((10,)),
+            dma((6,)),
             dma((2, 16)),
             dma((2, 16)),
             dma((2,)),
             dma((6,)),
             dma((6,)),
+            dma((3,)),
+            dma((3,)),
         ],
         compiler_params=pltpu.CompilerParams(
             collective_id=2, has_side_effects=True, vmem_limit_bytes=VMEM_BYTES
@@ -1418,29 +1471,30 @@
 
 
 def finish_kernel(n, nb, *refs):
-    ins = refs[:12]
-    outs = refs[12:20]
+    ins = refs[:8]
+    outs = refs[8:16]
     (
-        dq, dkv, xm, dz1, x1, dur, hid, dfr, omix, dar, gvec, wa,
-        pa, ta, da, na, la, pb, tb, db, nb_, lb, pd, td, dd, nd, ld, tv, dv, nv, lv,
+        dq, dkv, xm, dz1, pb, pd, gvec, wa,
+        pa, ta, da, na, la, db, nb_, lb, dd, nd, ld, tv, dv, nv, lv,
         twin_buf, dkv_send, dkv_recv, dq_recv, dqkv, dx_send, dx_recv, gx, gq, gk, gv, go, gu, gd, gs,
         in_sem, out_sem, rs_send, rs_recv, ex_send, ex_recv, dx_ssem, dx_rsem, tw_send, tw_recv,
-    ) = refs[20:]
+    ) = refs[16:]
     s = Spot(nb)
-    order = (1, 0, 10, 8, 9, 4, 5, 6, 7, 2, 11, 3)
-    local = (dq, dkv, xm, dz1, x1, dur, hid, dfr, omix, dar, gvec, wa)
+    order = (1, 0, 4, 5, 6, 7, 2, 3)
+    local = (dq, dkv, xm, dz1, pb, pd, gvec, wa)
     loads = copies([(ins[k], local[k]) for k in order], in_sem)
-    greet_all(n, nb, s.me)
+    greet_near(s)
     swap = remote(ins[1].at[:, :, 1 - s.c], twin_buf, tw_send, tw_recv, s.h, s.z * 2 + 1 - s.c)
     swap.start()
     jobs = [
         Scatter(s, *bufs, rs_send.at[k], rs_recv.at[k])
         for k, bufs in enumerate(
-            ((pb, tb, db, nb_, lb), (pd, td, dd, nd, ld), (gvec, tv, dv, nv, lv), (pa, ta, da, na, la))
+            ((pb, None, db, nb_, lb), (pd, None, dd, nd, ld), (gvec, tv, dv, nv, lv), (pa, ta, da, na, la))
         )
     ]
+    wait_all(loads[:5])
+    jobs[2].begin()
     swap.wait()
-    wait_all(loads[:2])
 
     def add(g):
         dkv_send[g] = (dkv[:, g, s.c].astype(f32) + twin_buf[:, g].astype(f32)).astype(bf16)
@@ -1448,56 +1502,47 @@
     each(4 * s.nz, add)
     plane = [Plane(s, ex_send.at[k], ex_recv.at[k]) for k in range(2)]
 
-    def block(w, j, slot):
-        group = pl.ds(j * s.nz, s.nz)
-        src, dst = ((dkv_send.at[group], dkv_recv.at[slot]), (dq.at[:, group], dq_recv.at[slot]))[w]
-        return plane[w].copy(src, dst, j, j, slot)
-
-    for w in range(2):
-        each(4, lambda i: block(w, plane[w].to(i), s.h).start(), 1)
-    wait_all(loads[2:8])
-    jobs[2].begin()
-    pb[:, :, 0:512] = dot_0(omix[...], dar[...]).astype(bf16).reshape(n, 16, 512)
-    for t in range(4):
-        cols = slice(512 * t, 512 * t + 512)
-        pb[:, :, 512 + 512 * t:1024 + 512 * t] = dot_0(x1[...], dur[:, cols]).astype(bf16).reshape(n, 16, 512)
-    jobs[0].begin()
-    wait_all(loads[8:])
-    for t in range(4):
-        cols = slice(512 * t, 512 * t + 512)
-        pd[8 * t:8 * t + 8] = dot_0(hid[:, cols], dfr[...]).astype(bf16).reshape(8, 64, 512)
-    jobs[1].begin()
-
-    def own(z):
+    def block(w, j, z, slot):
+        g = j * s.nz + z
+        src, dst = ((dkv_send.at[g], dkv_recv.at[slot, z]), (dq.at[:, g], dq_recv.at[slot, z]))[w]
+        return plane[w].copy(src, dst, j, g, slot * s.nz + z)
+
+    def pass_on(k):
+        z = s.ahead(k)
+        for w in range(2):
+            each(4, lambda i: block(w, plane[w].to(i), z, s.h).start(), 1)
         dkv_recv[s.h, z] = dkv_send[s.h * s.nz + z]
-        dq_recv[s.h, :, z] = dq[:, s.h * s.nz + z]
-
-    each(s.nz, own)
+        dq_recv[s.h, z] = dq[:, s.h * s.nz + z]
+
+    each(s.nz + 1, pass_on, 1)
     for job in jobs[:2]:
         job.first()
-    for w in range(2):
-        each(4, lambda i: block(w, plane[w].frm(i), plane[w].frm(i)).wait_recv(), 1)
-    for z in range(4):
-        rows = slice(128 * z, 128 * z + 128)
-        for j in range(4):
-            dqkv[rows, 128 * j:128 * j + 128] = dkv_recv[j, z].reshape(128, 128)
-        for t in range(2):
-            first, second = weave(
-                dq_recv[2 * t, :, z].reshape(64, 128), dq_recv[2 * t + 1, :, z].reshape(64, 128)
-            )
-            dqkv[128 * z:128 * z + 64, 512 + 128 * t:640 + 128 * t] = first
-            dqkv[128 * z + 64:128 * z + 128, 512 + 128 * t:640 + 128 * t] = second
-    weight = wa[:, :, :, :, 0:768].reshape(512, 768)
-    for z in range(4):
-        dx_send[z] = dot_t(dqkv[128 * z:128 * z + 128, :], weight).astype(bf16)
+    wait_all(loads[5:])
 
     def back(z, slot):
         return remote(dx_send.at[z], dx_recv.at[slot], dx_ssem.at[z], dx_rsem.at[slot], s.h, z * 2 + s.c)
 
-    each(s.nz, lambda k: back(s.ahead(k), s.z).start(), 1)
+    def take(k):
+        z = s.ahead(k)
+        for w in range(2):
+            each(4, lambda i: block(w, plane[w].frm(i), z, plane[w].frm(i)).wait_recv(), 1)
+        for j in range(4):
+            dqkv[z, :, 128 * j:128 * j + 128] = dkv_recv[j, z].reshape(128, 128)
+        for t in range(2):
+            first, second = weave(dq_recv[2 * t, z].reshape(64, 128), dq_recv[2 * t + 1, z].reshape(64, 128))
+            dqkv[z, 0:64, 512 + 128 * t:640 + 128 * t] = first
+            dqkv[z, 64:128, 512 + 128 * t:640 + 128 * t] = second
+        dx_send[z] = dot_t(dqkv[z], wa[:, :, :, :, 0:768].reshape(512, 768)).astype(bf16)
+
+    def take_and_send(k):
+        take(k)
+        back(s.ahead(k), s.z).start()
+
+    each(s.nz, take_and_send, 1)
+    take(s.nz)
     dx_recv[s.z] = dx_send[s.z]
     tokens = xm[...].reshape(512, 512)
-    pa[...] = dot_0(tokens, dqkv[...]).astype(bf16).reshape(n, 16, 768)
+    pa[...] = dot_0(tokens, dqkv[...].reshape(512, 768)).astype(bf16).reshape(n, 16, 768)
     jobs[3].begin()
     jobs[2].first()
     for job in jobs[:3]:
@@ -1527,14 +1572,14 @@
             gv[:, at:at + 128] = second
     stores += copies(zip((gq, gk, gv), outs[1:4]), out_sem.at[pl.ds(5, 3)])
     for w in range(2):
-        each(4, lambda i: block(w, plane[w].to(i), s.h).wait_send(), 1)
+        each(4, lambda i: each(s.nz, lambda z: block(w, plane[w].to(i), z, s.h).wait_send()), 1)
     each(s.nz, lambda k: back(s.ahead(k), s.z).wait_send(), 1)
     for job in jobs:
         job.sent()
     wait_all(stores)
 
 
-def finish(n, nb, dq, dkv, xm, dz1, x1, dur, hid, dfr, omix, dar, gvec, wa):
+def finish(n, nb, dq, dkv, xm, dz1, pb, pd, gvec, wa):
     dma = pltpu.SemaphoreType.DMA
     nz = nb // 2
     rows = dz1.shape[0]
@@ -1548,35 +1593,35 @@
             pltpu.VMEM((nz, depth, width), kind),
         ]
 
-    args = (dq, dkv, xm, dz1, x1, dur, hid, dfr, omix, dar, gvec, wa)
+    args = (dq, dkv, xm, dz1, pb, pd, gvec, wa)
     shapes = ((rows, 512), (16, 512), (16, 512), (16, 512), (16, 512), (16, 2048), (64, 512), (16, 128))
     return pl.pallas_call(
         functools.partial(finish_kernel, n, nb),
         out_shape=[jax.ShapeDtypeStruct(shape, f32) for shape in shapes],
-        in_specs=any_specs(12),
+        in_specs=any_specs(8),
         out_specs=any_specs(8),
         scratch_shapes=[
             *[pltpu.VMEM(arg.shape, arg.dtype) for arg in args],
             *buffers(16, 768, bf16),
-            *buffers(16, 2560, bf16),
-            *buffers(64, 512, bf16),
+            *buffers(16, 2560, bf16)[2:],
+            *buffers(64, 512, bf16)[2:],
             *buffers(16, 128, f32)[1:2],
             pltpu.VMEM((2, nz, 8, 128), f32),
             *buffers(16, 128, f32)[3:],
             pltpu.VMEM((8, 16, 16, 128), bf16),
             pltpu.VMEM((16, 8, 16, 128), bf16),
             pltpu.VMEM((4, nz, 8, 16, 128), bf16),
-            pltpu.VMEM((4, 4, nz, 16, 128), bf16),
-            pltpu.VMEM((512, 768), bf16),
+            pltpu.VMEM((4, nz, 4, 16, 128), bf16),
+            pltpu.VMEM((nz, 128, 768), bf16),
             pltpu.VMEM((nz, 128, 512), bf16),
             pltpu.VMEM((nz, 128, 512), bf16),
             *[pltpu.VMEM(shape, f32) for shape in shapes],
-            dma((12,)),
+            dma((8,)),
             dma((8,)),
             dma((4, 9 * nz)),
             dma((4, 9 * nz)),
-            dma((2, 4)),
-            dma((2, 4)),
+            dma((2, 4 * nz)),
+            dma((2, 4 * nz)),
             dma((nz,)),
             dma((nz,)),
             dma,
@@ -1641,14 +1686,14 @@
     )
     fx, fy = (lax.ppermute(fz, "head", [(h, h ^ w) for h in range(4)]) for w in (1, 2))
     o, of, lse, kv2, kvt = attn_fwd(q.reshape(4, 256, 128), kv.reshape(4096, 128), seg_q, seg_k)
-    do, out, dacc, dz1, x1, dur, hid, dfr, omix, dar, gvec = middle(
+    do, out, dacc, dz1, gvec, pb, pd = middle(
         n, nb, o.reshape(4, 16, 16, 128), x, y, g, fz, fx, fy, par, bup
     )
     dq, dkv, out, dacc = attn_bwd(
         q.reshape(4, 256, 128), do.reshape(4, 256, 128), of, lse, kv2, kvt, seg_q, seg_k, out, dacc
     )
     gx, gq, gk, gv, go, gu, gd, gs = finish(
-        n, nb, dq.reshape(4, 16, 16, 128), dkv.reshape(8, 16, 2, 16, 128), xm, dz1, x1, dur, hid, dfr, omix, dar, gvec, wa
+        n, nb, dq.reshape(4, 16, 16, 128), dkv.reshape(8, 16, 2, 16, 128), xm, dz1, pb, pd, gvec, wa
     )
     gx, gq, gk, gv, go, gu, gd, gbu, *small_grads = deliver((gx, gq, gk, gv, go, gu, gd), gs)
     return (

time: 158 us -> 151 us (0.956)
  Pallas kernels: 154 us -> 147 us
    pallas_call x1, Pallas kernels: 37.5 us -> 34.8 us  [project(): pl.pallas_call(functools.partial(project_kernel, n, nb), out_shape=(jax.S...]
    pallas_call x1, Pallas kernels: 50.1 us -> 48.1 us  [finish(): pl.pallas_call(functools.partial(finish_kernel, n, nb), out_shape=[jax.Sh...]
    pallas_call x1, Pallas kernels: 31.1 us -> 29.2 us  [middle(): pl.pallas_call(functools.partial(middle_kernel, n, nb), out_shape=[jax.Sh...]
where the time goes in v5:
time: 151 us
  Pallas kernels  147 us (97%)
  starting transfers between devices  2.73 us (2%)
    pallas_call x1, Pallas kernels, finish(): pl.pallas_call(functools.partial(finish_kernel, n, nb), out_shape=[jax.Sh...  48.1 us
    pallas_call x1, Pallas kernels, project(): pl.pallas_call(functools.partial(project_kernel, n, nb), out_shape=(jax.S...  34.8 us
    pallas_call x1, Pallas kernels, middle(): pl.pallas_call(functools.partial(middle_kernel, n, nb), out_shape=[jax.Sh...  29.2 us
    pallas_call x1, Pallas kernels, attn_bwd(): pl.pallas_call(attn_bwd_kernel, out_shape=[jax.ShapeDtypeStruct(shape, ki...  18.4 us
    pallas_call x1, Pallas kernels, attn_fwd(): pl.pallas_call(attn_fwd_kernel, out_shape=[jax.ShapeDtypeStruct(shape, ki...  13.9 us
  transfers between devices with their start and end apart: 2, of which 0 were waited for; matrix products, arithmetic and copies ran while one was open for 0% of the time, Pallas kernels for 9%

profile of v5, /device:TPU:0, one launch (start us, length us, event | category | flops | bytes accessed | tf_op | source)
XLA Modules:
  0.0 151.3 jit_solution(4260096393510336798)
XLA Ops:
  0.7 34.8 %project.1 = (bf16[4,16,16,128]{3,2,1,0:T(8,128)(2,1)}, bf16[8,16,2,16,128]{4,3,2,1,0:T(8,128)(2,1)}, bf16[4,128,512]{2,1,0:T(8,128)(2,1)}, bf16[4,4,2,16,896]{4...) custom-call(bf16[2,128,512]{2,1,0:T(8,128)(2,1)} %bitcast.21, ...), custom_call_target="tpu_custom_call" | custom-call | tf_op jit(solution)/shard_map/project/pallas_call | solution.py:1185
  35.4 1.2 collective-permute-start.1
  36.7 1.5 collective-permute-start
  38.2 13.9 %attn_fwd.1 = (bf16[4,256,128]{2,1,0:T(8,128)(2,1)}, f32[4,256,128]{2,1,0:T(8,128)}, f32[8,256]{1,0:T(8,128)}, bf16[4096,256]{1,0:T(8,128)(2,1)}, bf16[256,4096]{1,0:T(8,128)(2,1)}) custom-call(bf16[4,256,128]{2,1,0:T(8,128)(2,1)} %bitcast.23, bf16[4096,128]{1,0:T(8,128)(2,1)} %bitcast.31, s32[8,256]{1,0:T(8,128)} %get-tuple-element.67.seg_q_hbm, ...), custom_call_target="tpu_custom_call" | custom-call | flops 10000000000 | bytes 10000000 | tf_op jit(solution)/shard_map/attn_fwd/pallas_call | solution.py:458
  52.1 0.0 collective-permute-done.1.refs_6_
  52.1 0.0 copy-start
  52.1 0.0 collective-permute-done.refs_5_
  52.1 0.0 copy-start.1
  52.1 0.8 copy-done
  52.9 0.3 copy-done.1
  53.2 29.2 %middle.1 = (bf16[4,16,16,128]{3,2,1,0:T(8,128)(2,1)}, bf16[256,512]{1,0:T(8,128)(2,1)}, f32[256,512]{1,0:T(8,128)}, f32[256,512]{1,0:T(8,128)}, f32[32,16,128]{...) custom-call(bf16[4,16,16,128]{3,2,1,0:T(8,128)(2,1)} %bitcast.29, bf16[256,512]{1,0:T(8,128)(2,1)} %bitcast.22, ...), custom_call_target="tpu_custom_call" | custom-call | tf_op jit(solution)/shard_map/middle/pallas_call | solution.py:1431
  82.4 18.4 %attn_bwd.1 = (bf16[4,256,128]{2,1,0:T(8,128)(2,1)}, bf16[4096,128]{1,0:T(8,128)(2,1)}, bf16[256,512]{1,0:T(8,128)(2,1)}, f32[256,512]{1,0:T(8,128)}) custom-call(bf16[4,256,128]{2,1,0:T(8,128)(2,1)} %bitcast.24, bf16[4,256,128]{2,1,0:T(8,128)(2,1)} %bitcast.26, f32[4,256,128]{2,1,0:T(8,128)} %get-tuple-element.74.of_hbm, ...), custom_call_target="tpu_custom_call" | custom-call | tf_op jit(solution)/shard_map/attn_bwd/pallas_call | solution.py:539
  100.9 48.1 %finish.1 = (f32[256,512]{1,0:T(8,128)}, f32[16,512]{1,0:T(8,128)}, f32[16,512]{1,0:T(8,128)}, f32[16,512]{1,0:T(8,128)}, f32[16,512]{1,0:T(8,128)}, /*index=5*/...) custom-call(bf16[4,16,16,128]{3,2,1,0:T(8,128)(2,1)} %bitcast.25, bf16[8,16,2,16,128]{4,3,2,1,0:T(8,128)(2,1)} %bitcast.20, ...), custom_call_target="tpu_custom_call" | custom-call | tf_op jit(solution)/shard_map/finish/pallas_call | solution.py:1598
  149.0 2.2 %deliver.1 = (f32[256,512]{1,0:T(8,128)}, f32[16,512]{1,0:T(8,128)}, f32[16,512]{1,0:T(8,128)}, f32[16,512]{1,0:T(8,128)}, f32[16,512]{1,0:T(8,128)}, /*index=5*...) custom-call(f32[256,512]{1,0:T(8,128)} %get-tuple-element.89.refs_0_, ...), custom_call_target="tpu_custom_call" | custom-call | tf_op jit(solution)/shard_map/deliver/pallas_call | solution.py:1657
Async XLA Ops:
  35.4 16.7 %collective-permute-start.1 = (bf16[4,16,4608]{2,1,0:T(8,128)(2,1)}, bf16[4,16,4608]{2,1,0:T(8,128)(2,1)S(1)}, u32[]{:S(2)}, u32[]{:S(2)}) collective-permute-start(bf16[4,16,4608]{2,1,0:T(8,128)(2,1)} %get-tuple-element.70.refs_4_), channel_id=1, source_target_pairs={{0,16},{8,24},{16,0},{24,8},{1,17},{9,25},{17,1},{25,9},{2,18},{10... | collective-permute-start | bytes 1769480 | tf_op jit(solution)/shard_map/ppermute | solution.py:1687
  36.7 15.4 %collective-permute-start = (bf16[4,16,4608]{2,1,0:T(8,128)(2,1)}, bf16[4,16,4608]{2,1,0:T(8,128)(2,1)S(1)}, u32[]{:S(2)}, u32[]{:S(2)}) collective-permute-start(bf16[4,16,4608]{2,1,0:T(8,128)(2,1)} %get-tuple-element.70.refs_4_), channel_id=1, source_target_pairs={{0,8},{8,0},{16,24},{24,16},{1,9},{9,1},{17,25},{25,17},{2,10},{10... | collective-permute-start | bytes 1769480 | tf_op jit(solution)/shard_map/ppermute | solution.py:1687
  52.1 0.8 copy-start
  52.1 1.1 copy-start.1

commit v6 on v5

--- a/solution.py
+++ b/solution.py
@@ -552,6 +552,7 @@
             dma((4,)),
         ],
         compiler_params=pltpu.CompilerParams(vmem_limit_bytes=VMEM_BYTES),
+        cost_estimate=pl.CostEstimate(flops=10**10, bytes_accessed=10**7, transcendentals=10**7),
         name="attn_bwd",
     )(q, do, of, lse, kv2, kvt, seg_q, seg_k, pass1, pass2)
 
@@ -616,137 +617,10 @@
     pl.semaphore_wait(pltpu.get_barrier_semaphore(), 2 * s.nb)
 
 
-def halves(shape):
-    rows, width = shape
-    if width > 128:
-        return [(slice(None), slice(w * width // 2, (w + 1) * width // 2)) for w in range(2)]
-    return [(slice(w * rows // 2, (w + 1) * rows // 2), slice(None)) for w in range(2)]
-
-
-class Gather:
-    def __init__(self, spot, shard, full, send, recv, local):
-        self.s, self.full, self.local = spot, full, local
-        self.shard = shard if callable(shard) else lambda z: shard
-        self.send, self.recv = send, recv
-        self.cut = halves(full.shape[1:])
-
-    def copy(self, src, dst, k, h, z, c, recv_k=None):
-        recv_k = k if recv_k is None else recv_k
-        return remote(src, dst, self.send.at[k], self.recv.at[recv_k], h, z * 2 + c)
-
-    def to_z(self, z):
-        s = self.s
-        return self.copy(self.shard(z), self.full.at[s.me], z, s.h, z, s.c, s.z)
-
-    def from_z(self, z):
-        s = self.s
-        slot = self.full.at[s.index(s.h, z, s.c)]
-        return self.copy(slot, slot, z, s.h, z, s.c)
-
-    def near(self, w, z, own=False):
-        s = self.s
-        slot = self.full.at[s.index(s.h, z, s.c)]
-        return self.copy(self.shard(s.z) if own else slot, slot, (1 + w) * s.nz + z, s.near[w], s.z, s.c)
-
-    def from_near(self, w, z):
-        s = self.s
-        slot = self.full.at[s.index(s.near[w], z, s.c)]
-        return self.copy(slot, slot, (1 + w) * s.nz + z, s.near[w], s.z, s.c)
-
-    def lanes(self, slot, w):
-        return slot.at[self.cut[w]]
-
-    def onward(self, w, z):
-        s = self.s
-        slot = self.lanes(self.full.at[s.index(s.near[w], z, s.c)], w)
-        return self.copy(slot, slot, (3 + w) * s.nz + z, s.near[1 - w], s.z, s.c)
-
-    def from_onward(self, w, z):
-        s = self.s
-        slot = self.lanes(self.full.at[s.index(s.diag, z, s.c)], w)
-        return self.copy(slot, slot, (3 + w) * s.nz + z, s.near[1 - w], s.z, s.c)
-
-    def twin(self, h, z, own=False):
-        s = self.s
-        slot = self.full.at[s.index(h, z, s.c)]
-        return self.copy(self.shard(s.z) if own else slot, slot, 5 * s.nz + h * s.nz + z, s.h, s.z, 1 - s.c)
-
-    def from_twin(self, h, z):
-        s = self.s
-        slot = self.full.at[s.index(h, z, 1 - s.c)]
-        return self.copy(slot, slot, 5 * s.nz + h * s.nz + z, s.h, s.z, 1 - s.c)
-
-    def begin(self):
-        s = self.s
-        each(s.nz, lambda k: self.to_z(s.ahead(k)).start(), 1)
-
-    def begin_near(self):
-        s = self.s
-        self.own = pltpu.make_async_copy(self.shard(s.z), self.full.at[s.me], self.local)
-        self.own.start()
-        self.near(0, s.z, True).start()
-        self.near(1, s.z, True).start()
-        self.twin(s.h, s.z, True).start()
-
-    def spread(self):
-        s = self.s
-
-        def go(k):
-            z = s.ahead(k)
-            self.from_z(z).wait_recv()
-            self.near(0, z).start()
-            self.near(1, z).start()
-            self.twin(s.h, z).start()
-
-        each(s.nz, go, 1)
-
-    def cross(self):
-        s = self.s
-
-        def go(k):
-            z = s.ahead(k)
-            for w in range(2):
-                self.from_near(w, z).wait_recv()
-                self.onward(w, z).start()
-                self.twin(s.near[w], z).start()
-
-        each(s.nz, go)
-
-    def last(self):
-        s = self.s
-
-        def go(k):
-            z = s.ahead(k)
-            for w in range(2):
-                self.from_onward(w, z).wait_recv()
-            self.twin(s.diag, z).start()
-
-        each(s.nz, go)
-
-    def arrive(self):
-        s = self.s
-        each(4, lambda h: each(s.nz, lambda z: self.from_twin(h, z).wait_recv()))
-        self.own.wait()
-
-    def sent(self):
-        s = self.s
-        each(s.nz, lambda k: self.to_z(s.ahead(k)).wait_send(), 1)
-
-        def go(z):
-            for w in range(2):
-                self.near(w, z).wait_send()
-                self.onward(w, z).wait_send()
-            each(4, lambda h: self.twin(h, z).wait_send())
-
-        each(s.nz, go)
-
-
 class Scatter:
     def __init__(self, spot, part, twin, diag, near, line, send, recv):
         self.s, self.part, self.t, self.d, self.n, self.l = spot, part, twin, diag, near, line
         self.send, self.recv = send, recv
-        self.cut = halves(part.shape[1:])
-        self.axis = 1 if self.cut[0][0] == slice(None) else 0
 
     def copy(self, src, dst, k, h, z, c, recv_k=None):
         recv_k = k if recv_k is None else recv_k
@@ -760,10 +634,10 @@
         src = self.part.at[s.index(h, z, 1 - s.c)]
         return self.copy(src, self.t.at[h, z], h * s.nz + z, s.h, s.z, 1 - s.c)
 
-    def to_diag(self, w, z):
+    def to_diag(self, z):
         s = self.s
-        src = self.part.at[self.mine(s.diag, z)].at[self.cut[w]]
-        return self.copy(src, self.d.at[w, z], (4 + w) * s.nz + z, s.near[w], s.z, s.c)
+        src = self.part.at[self.mine(s.diag, z)]
+        return self.copy(src, self.d.at[z], 4 * s.nz + z, s.diag, s.z, s.c)
 
     def to_near(self, w, z):
         s = self.s
@@ -792,37 +666,26 @@
     def keep(self, h, z, value):
         self.part[self.mine(h, z)] = value.astype(self.part.dtype)
 
-    def first(self):
-        s = self.s
-
-        def go(k):
-            z = s.ahead(k)
-            if self.t is not None:
-                self.keep(s.diag, z, self.pair(s.diag, z))
-            for w in range(2):
-                self.to_diag(w, z).start()
-
-        each(s.nz + 1, go, 1)
-
     def second(self):
         s = self.s
 
         def go(k):
             z = s.ahead(k)
             for w in range(2):
-                value = self.pair(s.near[w], z)
-                self.to_diag(1 - w, z).wait_recv()
-                other = self.d[1 - w, z].astype(f32)
-                pieces = [value[cut] for cut in self.cut]
-                pieces[1 - w] = pieces[1 - w] + other
-                value = jnp.concatenate(pieces, axis=self.axis)
-                self.keep(s.near[w], z, value)
+                if self.t is not None:
+                    self.keep(s.near[w], z, self.pair(s.near[w], z))
                 self.to_near(w, z).start()
+            if self.t is not None:
+                self.keep(s.diag, z, self.pair(s.diag, z))
+                self.to_diag(z).start()
 
         each(s.nz + 1, go, 1)
 
     def joined(self, z):
         value = self.pair(self.s.h, z)
+        if self.t is not None:
+            self.to_diag(z).wait_recv()
+        value = value + self.d[z].astype(f32)
         for w in range(2):
             self.to_near(w, z).wait_recv()
             value = value + self.n[w, z].astype(f32)
@@ -861,8 +724,8 @@
         def go(z):
             if self.t is not None:
                 each(4, lambda h: self.to_twin(h, z).wait_send())
+                self.to_diag(z).wait_send()
             for w in range(2):
-                self.to_diag(w, z).wait_send()
                 self.to_near(w, z).wait_send()
 
         each(s.nz, go)
@@ -1275,13 +1138,13 @@
 
 def middle_kernel(n, nb, *refs):
     o_hbm, x_hbm, y_hbm, g_hbm, fz_hbm, fx_hbm, fy_hbm, par_hbm, bup_hbm = refs[:9]
-    outs_hbm = refs[10:16]
+    outs_hbm = refs[10:17]
     do_out = refs[9]
     (
         o_in, x, y, g_in, wb, wd, par, bup, o_recv, do_send, slope,
-        out, dacc_ref, dz1_ref, gvec, sum_b, sum_d, bias_up, omix, hid_ref, dur_ref, po, pu, pd, to, tu, td,
+        out, dacc_ref, dz1_ref, gvec, sum_b, sum_d, far, bias_up, omix, hid_ref, dur_ref, po, pu, pd, to, tu, td,
         in_sem, out_sem, ex_send, ex_recv, ex_local, f_send, f_recv, p_send, p_recv,
-    ) = refs[16:]
+    ) = refs[17:]
     s = Spot(nb)
     loads = copies(
         [
@@ -1412,6 +1275,11 @@
     sum_b[:, :, 512:2560] = join(pu, tu)
     sum_b[:, :, 0:512] = join(po, to)
     stores += copies(zip((sum_b, sum_d), outs_hbm[4:6]), out_sem.at[pl.ds(4, 2)])
+    group = pl.ds(s.diag * s.nz, s.nz)
+    far[:, :, 0:2560] = sum_b[group]
+    for r in range(4):
+        far[:, :, 2560 + 512 * r:3072 + 512 * r] = sum_d[group, 16 * r:16 * r + 16, :]
+    stores += copies([(far, outs_hbm[6])], out_sem.at[pl.ds(6, 1)])
     do_ex.end()
     for w in range(2):
         onward(w, s.near[w], s.near[1 - w]).wait_send()
@@ -1431,9 +1299,10 @@
     return pl.pallas_call(
         functools.partial(middle_kernel, n, nb),
         out_shape=[jax.ShapeDtypeStruct((4, 16, 16, 128), bf16)]
-        + [jax.ShapeDtypeStruct(shape, kind) for shape, kind in saved],
+        + [jax.ShapeDtypeStruct(shape, kind) for shape, kind in saved]
+        + [jax.ShapeDtypeStruct((nz, 16, 4608), bf16)],
         in_specs=any_specs(9),
-        out_specs=any_specs(7),
+        out_specs=any_specs(8),
         scratch_shapes=[
             pltpu.VMEM(o.shape, bf16),
             pltpu.VMEM(x.shape, bf16),
@@ -1447,6 +1316,7 @@
             pltpu.VMEM((16, 4, 16, 128), bf16),
             pltpu.VMEM((rows, 2048), f32),
             *[pltpu.VMEM(shape, kind) for shape, kind in saved],
+            pltpu.VMEM((nz, 16, 4608), bf16),
             pltpu.VMEM((1, 2048), f32),
             pltpu.VMEM((rows, 512), bf16),
             pltpu.VMEM((rows, 2048), bf16),
@@ -1454,7 +1324,7 @@
             *[pltpu.VMEM((4, nz, 2, *tail), bf16) for tail in ((16, 512), (16, 2048), (64, 512))],
             *[pltpu.VMEM((4, nz, *tail), bf16) for tail in ((16, 512), (16, 2048), (64, 512))],
             dma((9,)),
-            dma((6,)),
+            dma((7,)),
             dma((2, 16)),
             dma((2, 16)),
             dma((2,)),
@@ -1471,18 +1341,23 @@
 
 
 def finish_kernel(n, nb, *refs):
-    ins = refs[:8]
-    outs = refs[8:16]
+    ins, far = refs[:8], refs[8]
+    outs = refs[9:17]
     (
         dq, dkv, xm, dz1, pb, pd, gvec, wa,
         pa, ta, da, na, la, db, nb_, lb, dd, nd, ld, tv, dv, nv, lv,
         twin_buf, dkv_send, dkv_recv, dq_recv, dqkv, dx_send, dx_recv, gx, gq, gk, gv, go, gu, gd, gs,
-        in_sem, out_sem, rs_send, rs_recv, ex_send, ex_recv, dx_ssem, dx_rsem, tw_send, tw_recv,
-    ) = refs[16:]
+        in_sem, far_sem, out_sem, rs_send, rs_recv, ex_send, ex_recv, dx_ssem, dx_rsem, tw_send, tw_recv,
+    ) = refs[17:]
     s = Spot(nb)
     order = (1, 0, 4, 5, 6, 7, 2, 3)
     local = (dq, dkv, xm, dz1, pb, pd, gvec, wa)
     loads = copies([(ins[k], local[k]) for k in order], in_sem)
+    corners = copies(
+        [(far.at[:, :, pl.ds(0, 2560)], db)]
+        + [(far.at[:, :, pl.ds(2560 + 512 * r, 512)], dd.at[:, pl.ds(16 * r, 16)]) for r in range(4)],
+        far_sem,
+    )
     greet_near(s)
     swap = remote(ins[1].at[:, :, 1 - s.c], twin_buf, tw_send, tw_recv, s.h, s.z * 2 + 1 - s.c)
     swap.start()
@@ -1515,9 +1390,8 @@
         dq_recv[s.h, z] = dq[:, s.h * s.nz + z]
 
     each(s.nz + 1, pass_on, 1)
-    for job in jobs[:2]:
-        job.first()
     wait_all(loads[5:])
+    wait_all(corners)
 
     def back(z, slot):
         return remote(dx_send.at[z], dx_recv.at[slot], dx_ssem.at[z], dx_rsem.at[slot], s.h, z * 2 + s.c)
@@ -1539,19 +1413,17 @@
         back(s.ahead(k), s.z).start()
 
     each(s.nz, take_and_send, 1)
+    for job in jobs[:2]:
+        job.second()
     take(s.nz)
     dx_recv[s.z] = dx_send[s.z]
     tokens = xm[...].reshape(512, 512)
     pa[...] = dot_0(tokens, dqkv[...].reshape(512, 768)).astype(bf16).reshape(n, 16, 768)
     jobs[3].begin()
-    jobs[2].first()
-    for job in jobs[:3]:
-        job.second()
-    jobs[3].first()
-    for job in jobs[:3]:
+    jobs[2].second()
+    jobs[3].second()
+    for job in jobs:
         job.third()
-    jobs[3].second()
-    jobs[3].third()
     each(s.nz, lambda k: back(s.ahead(k), s.ahead(k)).wait_recv(), 1)
     for m in range(2):
         rows = slice(128 * m, 128 * m + 128)
@@ -1579,7 +1451,7 @@
     wait_all(stores)
 
 
-def finish(n, nb, dq, dkv, xm, dz1, pb, pd, gvec, wa):
+def finish(n, nb, dq, dkv, xm, dz1, pb, pd, gvec, wa, far):
     dma = pltpu.SemaphoreType.DMA
     nz = nb // 2
     rows = dz1.shape[0]
@@ -1588,7 +1460,7 @@
         return [
             pltpu.VMEM((n, depth, width), kind),
             pltpu.VMEM((4, nz, depth, width), kind),
-            pltpu.VMEM((2, nz, depth, width // 2), kind),
+            pltpu.VMEM((nz, depth, width), kind),
             pltpu.VMEM((2, nz, depth, width), kind),
             pltpu.VMEM((nz, depth, width), kind),
         ]
@@ -1598,16 +1470,14 @@
     return pl.pallas_call(
         functools.partial(finish_kernel, n, nb),
         out_shape=[jax.ShapeDtypeStruct(shape, f32) for shape in shapes],
-        in_specs=any_specs(8),
+        in_specs=any_specs(9),
         out_specs=any_specs(8),
         scratch_shapes=[
             *[pltpu.VMEM(arg.shape, arg.dtype) for arg in args],
             *buffers(16, 768, bf16),
             *buffers(16, 2560, bf16)[2:],
             *buffers(64, 512, bf16)[2:],
-            *buffers(16, 128, f32)[1:2],
-            pltpu.VMEM((2, nz, 8, 128), f32),
-            *buffers(16, 128, f32)[3:],
+            *buffers(16, 128, f32)[1:],
             pltpu.VMEM((8, 16, 16, 128), bf16),
             pltpu.VMEM((16, 8, 16, 128), bf16),
             pltpu.VMEM((4, nz, 8, 16, 128), bf16),
@@ -1617,6 +1487,7 @@
             pltpu.VMEM((nz, 128, 512), bf16),
             *[pltpu.VMEM(shape, f32) for shape in shapes],
             dma((8,)),
+            dma((5,)),
             dma((8,)),
             dma((4, 9 * nz)),
             dma((4, 9 * nz)),
@@ -1631,7 +1502,7 @@
             collective_id=3, has_side_effects=True, vmem_limit_bytes=VMEM_BYTES
         ),
         name="finish",
-    )(*args)
+    )(*args, far)
 
 
 def deliver_kernel(count, *refs):
@@ -1686,14 +1557,15 @@
     )
     fx, fy = (lax.ppermute(fz, "head", [(h, h ^ w) for h in range(4)]) for w in (1, 2))
     o, of, lse, kv2, kvt = attn_fwd(q.reshape(4, 256, 128), kv.reshape(4096, 128), seg_q, seg_k)
-    do, out, dacc, dz1, gvec, pb, pd = middle(
+    do, out, dacc, dz1, gvec, pb, pd, far = middle(
         n, nb, o.reshape(4, 16, 16, 128), x, y, g, fz, fx, fy, par, bup
     )
+    far = lax.ppermute(far, "head", [(h, 3 - h) for h in range(4)])
     dq, dkv, out, dacc = attn_bwd(
         q.reshape(4, 256, 128), do.reshape(4, 256, 128), of, lse, kv2, kvt, seg_q, seg_k, out, dacc
     )
     gx, gq, gk, gv, go, gu, gd, gs = finish(
-        n, nb, dq.reshape(4, 16, 16, 128), dkv.reshape(8, 16, 2, 16, 128), xm, dz1, pb, pd, gvec, wa
+        n, nb, dq.reshape(4, 16, 16, 128), dkv.reshape(8, 16, 2, 16, 128), xm, dz1, pb, pd, gvec, wa, far
     )
     gx, gq, gk, gv, go, gu, gd, gbu, *small_grads = deliver((gx, gq, gk, gv, go, gu, gd), gs)
     return (

time: 151 us -> 150 us (level)
  Pallas kernels: 147 us -> 142 us
  starting transfers between devices: 2.73 us -> 4.41 us
    pallas_call x1, Pallas kernels: 48.1 us -> 41.9 us  [finish(): pl.pallas_call(functools.partial(finish_kernel, n, nb), out_shape=[jax.Sh...]
    ppermute x0 -> x1, starting transfers between devices: none -> 1.68 us  [by_pairs(): far = lax.ppermute(far, 'head', [(h, 3 - h) for h in range(4)])]
  transfers between devices with their start and end apart: 2 -> 3, of which waited for: 0 -> 0; matrix products, arithmetic and copies ran while one was open for 0% -> 0% of each run, Pallas kernels for 9% -> 22%
where the time goes in v6:
time: 150 us; the launch traced here: 149 us
  Pallas kernels  142 us (95%)
  starting transfers between devices  4.41 us (3%)
  local copies, waits for them, and re-layouts  1.87 us (1%)
    pallas_call x1, Pallas kernels, finish(): pl.pallas_call(functools.partial(finish_kernel, n, nb), out_shape=[jax.Sh...  41.9 us
    pallas_call x1, Pallas kernels, project(): pl.pallas_call(functools.partial(project_kernel, n, nb), out_shape=(jax.S...  34.8 us
    pallas_call x1, Pallas kernels, middle(): pl.pallas_call(functools.partial(middle_kernel, n, nb), out_shape=[jax.Sh...  30 us
    pallas_call x1, Pallas kernels, attn_bwd(): pl.pallas_call(attn_bwd_kernel, out_shape=[jax.ShapeDtypeStruct(shape, ki...  19.2 us
    pallas_call x1, Pallas kernels, attn_fwd(): pl.pallas_call(attn_fwd_kernel, out_shape=[jax.ShapeDtypeStruct(shape, ki...  14.2 us
  transfers between devices with their start and end apart: 3, of which 0 were waited for; matrix products, arithmetic and copies ran while one was open for 0% of the time, Pallas kernels for 22%

profile of v6, /device:TPU:0, one launch (start us, length us, event | category | flops | bytes accessed | tf_op | source)
XLA Modules:
  0.0 149.5 jit_solution(14485904378080375967)
XLA Ops:
  0.7 34.8 %project.1 = (bf16[4,16,16,128]{3,2,1,0:T(8,128)(2,1)}, bf16[8,16,2,16,128]{4,3,2,1,0:T(8,128)(2,1)}, bf16[4,128,512]{2,1,0:T(8,128)(2,1)}, bf16[4,4,2,16,896]{4...) custom-call(bf16[2,128,512]{2,1,0:T(8,128)(2,1)} %bitcast.21, ...), custom_call_target="tpu_custom_call" | custom-call | tf_op jit(solution)/shard_map/project/pallas_call | solution.py:1048
  35.4 1.2 collective-permute-start.1
  36.7 1.5 collective-permute-start
  38.2 14.2 %attn_fwd.1 = (bf16[4,256,128]{2,1,0:T(8,128)(2,1)}, f32[4,256,128]{2,1,0:T(8,128)}, f32[8,256]{1,0:T(8,128)}, bf16[4096,256]{1,0:T(8,128)(2,1)}, bf16[256,4096]{1,0:T(8,128)(2,1)}) custom-call(bf16[4,256,128]{2,1,0:T(8,128)(2,1)} %bitcast.30, bf16[4096,128]{1,0:T(8,128)(2,1)} %bitcast.28, s32[8,256]{1,0:T(8,128)} %get-tuple-element.68.seg_q_hbm, ...), custom_call_target="tpu_custom_call" | custom-call | flops 10000000000 | bytes 10000000 | tf_op jit(solution)/shard_map/attn_fwd/pallas_call | solution.py:458
  52.4 0.0 collective-permute-done.1.refs_6_
  52.4 0.0 copy-start.1
  52.4 0.0 collective-permute-done.refs_5_
  52.4 0.0 copy-start.2
  52.4 0.8 copy-done.1
  53.2 0.3 copy-done.2
  53.5 30.0 %middle.1 = (bf16[4,16,16,128]{3,2,1,0:T(8,128)(2,1)}, bf16[256,512]{1,0:T(8,128)(2,1)}, f32[256,512]{1,0:T(8,128)}, f32[256,512]{1,0:T(8,128)}, f32[32,16,128]{...) custom-call(bf16[4,16,16,128]{3,2,1,0:T(8,128)(2,1)} %bitcast.26, ...), custom_call_target="tpu_custom_call" | custom-call | tf_op jit(solution)/shard_map/middle/pallas_call | solution.py:1299
  83.5 1.7 %collective-permute-start.2 = (bf16[4,16,4608]{2,1,0:T(8,128)(2,1)}, bf16[4,16,4608]{2,1,0:T(8,128)(2,1)S(1)}, u32[]{:S(2)}, u32[]{:S(2)}) collective-permute-start(bf16[4,16,4608]{2,1,0:T(8,128)(2,1)} %get-tuple-element.90), channel_id=1, source_target_pairs={{0,24},{8,16},{16,8},{24,0},{1,25},{9,17},{17,9},{25,1},{2,26},{10... | collective-permute-start | bytes 1769480 | tf_op jit(solution)/shard_map/ppermute | solution.py:1563
  85.2 19.2 %attn_bwd.1 = (bf16[4,256,128]{2,1,0:T(8,128)(2,1)}, bf16[4096,128]{1,0:T(8,128)(2,1)}, bf16[256,512]{1,0:T(8,128)(2,1)}, f32[256,512]{1,0:T(8,128)}) custom-call(bf16[4,256,128]{2,1,0:T(8,128)(2,1)} %bitcast.31, bf16[4,256,128]{2,1,0:T(8,128)(2,1)} %bitcast.32, f32[4,256,128]{2,1,0:T(8,128)} %get-tuple-element.75.of_hbm, ...), custom_call_target="tpu_custom_call" | custom-call | flops 10000000000 | bytes 10000000 | tf_op jit(solution)/shard_map/attn_bwd/pallas_call | solution.py:539
  104.4 0.0 collective-permute-done.2.refs_8_
  104.4 0.0 copy-start
  104.4 0.8 copy-done
  105.3 41.9 %finish.1 = (f32[256,512]{1,0:T(8,128)}, f32[16,512]{1,0:T(8,128)}, f32[16,512]{1,0:T(8,128)}, f32[16,512]{1,0:T(8,128)}, f32[16,512]{1,0:T(8,128)}, /*index=5*/...) custom-call(bf16[4,16,16,128]{3,2,1,0:T(8,128)(2,1)} %bitcast.23, bf16[8,16,2,16,128]{4,3,2,1,0:T(8,128)(2,1)} %bitcast.20, ...), custom_call_target="tpu_custom_call" | custom-call | tf_op jit(solution)/shard_map/finish/pallas_call | solution.py:1470
  147.1 2.2 %deliver.1 = (f32[256,512]{1,0:T(8,128)}, f32[16,512]{1,0:T(8,128)}, f32[16,512]{1,0:T(8,128)}, f32[16,512]{1,0:T(8,128)}, f32[16,512]{1,0:T(8,128)}, /*index=5*...) custom-call(f32[256,512]{1,0:T(8,128)} %get-tuple-element.91.refs_0_, ...), custom_call_target="tpu_custom_call" | custom-call | tf_op jit(solution)/shard_map/deliver/pallas_call | solution.py:1528
Async XLA Ops:
  35.4 17.0 %collective-permute-start.1 = (bf16[4,16,4608]{2,1,0:T(8,128)(2,1)}, bf16[4,16,4608]{2,1,0:T(8,128)(2,1)S(1)}, u32[]{:S(2)}, u32[]{:S(2)}) collective-permute-start(bf16[4,16,4608]{2,1,0:T(8,128)(2,1)} %get-tuple-element.71.refs_4_), channel_id=1, source_target_pairs={{0,16},{8,24},{16,0},{24,8},{1,17},{9,25},{17,1},{25,9},{2,18},{10... | collective-permute-start | bytes 1769480 | tf_op jit(solution)/shard_map/ppermute | solution.py:1558
  36.7 15.7 %collective-permute-start = (bf16[4,16,4608]{2,1,0:T(8,128)(2,1)}, bf16[4,16,4608]{2,1,0:T(8,128)(2,1)S(1)}, u32[]{:S(2)}, u32[]{:S(2)}) collective-permute-start(bf16[4,16,4608]{2,1,0:T(8,128)(2,1)} %get-tuple-element.71.refs_4_), channel_id=1, source_target_pairs={{0,8},{8,0},{16,24},{24,16},{1,9},{9,1},{17,25},{25,17},{2,10},{10... | collective-permute-start | bytes 1769480 | tf_op jit(solution)/shard_map/ppermute | solution.py:1558
  52.4 0.8 copy-start.1
  52.4 1.0 copy-start.2
  83.5 20.9 %collective-permute-start.2 = (bf16[4,16,4608]{2,1,0:T(8,128)(2,1)}, bf16[4,16,4608]{2,1,0:T(8,128)(2,1)S(1)}, u32[]{:S(2)}, u32[]{:S(2)}) collective-permute-start(bf16[4,16,4608]{2,1,0:T(8,128)(2,1)} %get-tuple-element.90), channel_id=1, source_target_pairs={{0,24},{8,16},{16,8},{24,0},{1,25},{9,17},{17,9},{25,1},{2,26},{10... | collective-permute-start | bytes 1769480 | tf_op jit(solution)/shard_map/ppermute | solution.py:1563
  104.4 0.8 copy-start

commit v7 on v6

--- a/solution.py
+++ b/solution.py
@@ -929,7 +929,6 @@
     each(s.nz, lambda k: w_line(s.ahead(k), s.z).start(), 1)
     own_w = pltpu.make_async_copy(sa.at[lax.rem(s.z, 2)], wa.at[s.h, s.z, s.c], w_local)
     own_w.start()
-    each(s.nz, lambda k: pass_x(s.ahead(k), s.z).start(), 1)
     own_x = pltpu.make_async_copy(x.at[s.z // 2], x_all.at[s.z], x_local)
     own_x.start()
     wait_all(loads[13:])
@@ -938,11 +937,13 @@
     for t in range(4):
         sb[:, 2560 + 512 * t:3072 + 512 * t] = wd[16 * t:16 * t + 16, :]
     line = Line(s, sb, fz_out, f_send, f_recv, f_local)
-    line.begin()
     own_w.wait()
     each(s.nz, lambda k: w_line(s.ahead(k), s.ahead(k)).wait_recv(), 1)
+    each(s.nz, lambda k: pass_x(s.ahead(k), s.z).start(), 1)
     each(4, lambda i: w_plane(lax.rem(s.h + i, 4), s.h).start(), 1)
     w_twin(s.h, s.c).start()
+
+    line.begin()
 
     def w_arrive(i):
         h = lax.rem(s.h + 4 - i, 4)

time: 150 us -> 148 us (0.987)
    pallas_call x1, Pallas kernels: 30 us -> 27 us  [middle(): pl.pallas_call(functools.partial(middle_kernel, n, nb), out_shape=[jax.Sh...]
  transfers between devices with their start and end apart: 3 -> 3, of which waited for: 0 -> 0; matrix products, arithmetic and copies ran while one was open for 0% -> 0% of each run, Pallas kernels for 22% -> 23%
where the time goes in v7:
time: 148 us; the launch traced here: 147 us
  Pallas kernels  141 us (95%)
  starting transfers between devices  3.8 us (3%)
  local copies, waits for them, and re-layouts  1.87 us (1%)
    pallas_call x1, Pallas kernels, finish(): pl.pallas_call(functools.partial(finish_kernel, n, nb), out_shape=[jax.Sh...  42.3 us
    pallas_call x1, Pallas kernels, project(): pl.pallas_call(functools.partial(project_kernel, n, nb), out_shape=(jax.S...  35.8 us
    pallas_call x1, Pallas kernels, middle(): pl.pallas_call(functools.partial(middle_kernel, n, nb), out_shape=[jax.Sh...  27 us
    pallas_call x1, Pallas kernels, attn_bwd(): pl.pallas_call(attn_bwd_kernel, out_shape=[jax.ShapeDtypeStruct(shape, ki...  19.2 us
    pallas_call x1, Pallas kernels, attn_fwd(): pl.pallas_call(attn_fwd_kernel, out_shape=[jax.ShapeDtypeStruct(shape, ki...  14.2 us
  transfers between devices with their start and end apart: 3, of which 0 were waited for; matrix products, arithmetic and copies ran while one was open for 0% of the time, Pallas kernels for 23%

profile of v7, /device:TPU:0, one launch (start us, length us, event | category | flops | bytes accessed | tf_op | source)
XLA Modules:
  0.0 147.3 jit_solution(5649596350504159392)
XLA Ops:
  0.7 35.8 %project.1 = (bf16[4,16,16,128]{3,2,1,0:T(8,128)(2,1)}, bf16[8,16,2,16,128]{4,3,2,1,0:T(8,128)(2,1)}, bf16[4,128,512]{2,1,0:T(8,128)(2,1)}, bf16[4,4,2,16,896]{4...) custom-call(bf16[2,128,512]{2,1,0:T(8,128)(2,1)} %bitcast.21, ...), custom_call_target="tpu_custom_call" | custom-call | tf_op jit(solution)/shard_map/project/pallas_call | solution.py:1049
  36.4 0.8 collective-permute-start.1
  37.2 1.5 %collective-permute-start = (bf16[4,16,4608]{2,1,0:T(8,128)(2,1)}, bf16[4,16,4608]{2,1,0:T(8,128)(2,1)S(1)}, u32[]{:S(2)}, u32[]{:S(2)}) collective-permute-start(bf16[4,16,4608]{2,1,0:T(8,128)(2,1)} %get-tuple-element.71.refs_4_), channel_id=1, source_target_pairs={{0,8},{8,0},{16,24},{24,16},{1,9},{9,1},{17,25},{25,17},{2,10},{10... | collective-permute-start | bytes 1769480 | tf_op jit(solution)/shard_map/ppermute | solution.py:1559
  38.7 14.2 %attn_fwd.1 = (bf16[4,256,128]{2,1,0:T(8,128)(2,1)}, f32[4,256,128]{2,1,0:T(8,128)}, f32[8,256]{1,0:T(8,128)}, bf16[4096,256]{1,0:T(8,128)(2,1)}, bf16[256,4096]{1,0:T(8,128)(2,1)}) custom-call(bf16[4,256,128]{2,1,0:T(8,128)(2,1)} %bitcast.30, bf16[4096,128]{1,0:T(8,128)(2,1)} %bitcast.28, s32[8,256]{1,0:T(8,128)} %get-tuple-element.68.seg_q_hbm, ...), custom_call_target="tpu_custom_call" | custom-call | flops 10000000000 | bytes 10000000 | tf_op jit(solution)/shard_map/attn_fwd/pallas_call | solution.py:458
  52.9 0.0 collective-permute-done.1.refs_6_
  52.9 0.0 copy-start.1
  52.9 0.0 collective-permute-done.refs_5_
  53.0 0.0 copy-start.2
  53.0 0.8 copy-done.1
  53.8 0.3 copy-done.2
  54.0 27.0 %middle.1 = (bf16[4,16,16,128]{3,2,1,0:T(8,128)(2,1)}, bf16[256,512]{1,0:T(8,128)(2,1)}, f32[256,512]{1,0:T(8,128)}, f32[256,512]{1,0:T(8,128)}, f32[32,16,128]{...) custom-call(bf16[4,16,16,128]{3,2,1,0:T(8,128)(2,1)} %bitcast.26, ...), custom_call_target="tpu_custom_call" | custom-call | tf_op jit(solution)/shard_map/middle/pallas_call | solution.py:1300
  81.0 1.5 %collective-permute-start.2 = (bf16[4,16,4608]{2,1,0:T(8,128)(2,1)}, bf16[4,16,4608]{2,1,0:T(8,128)(2,1)S(1)}, u32[]{:S(2)}, u32[]{:S(2)}) collective-permute-start(bf16[4,16,4608]{2,1,0:T(8,128)(2,1)} %get-tuple-element.90), channel_id=1, source_target_pairs={{0,24},{8,16},{16,8},{24,0},{1,25},{9,17},{17,9},{25,1},{2,26},{10... | collective-permute-start | bytes 1769480 | tf_op jit(solution)/shard_map/ppermute | solution.py:1564
  82.6 19.2 %attn_bwd.1 = (bf16[4,256,128]{2,1,0:T(8,128)(2,1)}, bf16[4096,128]{1,0:T(8,128)(2,1)}, bf16[256,512]{1,0:T(8,128)(2,1)}, f32[256,512]{1,0:T(8,128)}) custom-call(bf16[4,256,128]{2,1,0:T(8,128)(2,1)} %bitcast.31, bf16[4,256,128]{2,1,0:T(8,128)(2,1)} %bitcast.32, f32[4,256,128]{2,1,0:T(8,128)} %get-tuple-element.75.of_hbm, ...), custom_call_target="tpu_custom_call" | custom-call | flops 10000000000 | bytes 10000000 | tf_op jit(solution)/shard_map/attn_bwd/pallas_call | solution.py:539
  101.8 0.0 collective-permute-done.2.refs_8_
  101.8 0.0 copy-start
  101.8 0.8 copy-done
  102.7 42.3 %finish.1 = (f32[256,512]{1,0:T(8,128)}, f32[16,512]{1,0:T(8,128)}, f32[16,512]{1,0:T(8,128)}, f32[16,512]{1,0:T(8,128)}, f32[16,512]{1,0:T(8,128)}, /*index=5*/...) custom-call(bf16[4,16,16,128]{3,2,1,0:T(8,128)(2,1)} %bitcast.23, bf16[8,16,2,16,128]{4,3,2,1,0:T(8,128)(2,1)} %bitcast.20, ...), custom_call_target="tpu_custom_call" | custom-call | tf_op jit(solution)/shard_map/finish/pallas_call | solution.py:1471
  145.0 2.2 %deliver.1 = (f32[256,512]{1,0:T(8,128)}, f32[16,512]{1,0:T(8,128)}, f32[16,512]{1,0:T(8,128)}, f32[16,512]{1,0:T(8,128)}, f32[16,512]{1,0:T(8,128)}, /*index=5*...) custom-call(f32[256,512]{1,0:T(8,128)} %get-tuple-element.91.refs_0_, ...), custom_call_target="tpu_custom_call" | custom-call | tf_op jit(solution)/shard_map/deliver/pallas_call | solution.py:1529
Async XLA Ops:
  36.4 16.5 %collective-permute-start.1 = (bf16[4,16,4608]{2,1,0:T(8,128)(2,1)}, bf16[4,16,4608]{2,1,0:T(8,128)(2,1)S(1)}, u32[]{:S(2)}, u32[]{:S(2)}) collective-permute-start(bf16[4,16,4608]{2,1,0:T(8,128)(2,1)} %get-tuple-element.71.refs_4_), channel_id=1, source_target_pairs={{0,16},{8,24},{16,0},{24,8},{1,17},{9,25},{17,1},{25,9},{2,18},{10... | collective-permute-start | bytes 1769480 | tf_op jit(solution)/shard_map/ppermute | solution.py:1559
  37.2 15.8 %collective-permute-start = (bf16[4,16,4608]{2,1,0:T(8,128)(2,1)}, bf16[4,16,4608]{2,1,0:T(8,128)(2,1)S(1)}, u32[]{:S(2)}, u32[]{:S(2)}) collective-permute-start(bf16[4,16,4608]{2,1,0:T(8,128)(2,1)} %get-tuple-element.71.refs_4_), channel_id=1, source_target_pairs={{0,8},{8,0},{16,24},{24,16},{1,9},{9,1},{17,25},{25,17},{2,10},{10... | collective-permute-start | bytes 1769480 | tf_op jit(solution)/shard_map/ppermute | solution.py:1559
  52.9 0.8 copy-start.1
  53.0 1.0 copy-start.2
  81.0 20.8 %collective-permute-start.2 = (bf16[4,16,4608]{2,1,0:T(8,128)(2,1)}, bf16[4,16,4608]{2,1,0:T(8,128)(2,1)S(1)}, u32[]{:S(2)}, u32[]{:S(2)}) collective-permute-start(bf16[4,16,4608]{2,1,0:T(8,128)(2,1)} %get-tuple-element.90), channel_id=1, source_target_pairs={{0,24},{8,16},{16,8},{24,0},{1,25},{9,17},{17,9},{25,1},{2,26},{10... | collective-permute-start | bytes 1769480 | tf_op jit(solution)/shard_map/ppermute | solution.py:1564
  101.8 0.8 copy-start

commit v8 on v7

--- a/solution.py
+++ b/solution.py
@@ -943,14 +943,13 @@
     each(4, lambda i: w_plane(lax.rem(s.h + i, 4), s.h).start(), 1)
     w_twin(s.h, s.c).start()
 
-    line.begin()
-
     def w_arrive(i):
         h = lax.rem(s.h + 4 - i, 4)
         w_plane(h, h).wait_recv()
         w_twin(h, s.c).start()
 
     each(4, w_arrive, 1)
+    line.begin()
     each(4, lambda h: w_twin(h, 1 - s.c).wait_recv())
     outs = copies([(wa, wa_out)], out_sem)
     own_x.wait()

time: 148 us -> 147 us (level)
  transfers between devices with their start and end apart: 3 -> 3, of which waited for: 0 -> 0; matrix products, arithmetic and copies ran while one was open for 0% -> 0% of each run, Pallas kernels for 23% -> 22%
where the time goes in v8:
time: 147 us; the launch traced here: 146 us
  Pallas kernels  140 us (95%)
  starting transfers between devices  3.82 us (3%)
  local copies, waits for them, and re-layouts  1.87 us (1%)
    pallas_call x1, Pallas kernels, finish(): pl.pallas_call(functools.partial(finish_kernel, n, nb), out_shape=[jax.Sh...  42.5 us
    pallas_call x1, Pallas kernels, project(): pl.pallas_call(functools.partial(project_kernel, n, nb), out_shape=(jax.S...  35.8 us
    pallas_call x1, Pallas kernels, middle(): pl.pallas_call(functools.partial(middle_kernel, n, nb), out_shape=[jax.Sh...  27 us
    pallas_call x1, Pallas kernels, attn_bwd(): pl.pallas_call(attn_bwd_kernel, out_shape=[jax.ShapeDtypeStruct(shape, ki...  18.5 us
    pallas_call x1, Pallas kernels, attn_fwd(): pl.pallas_call(attn_fwd_kernel, out_shape=[jax.ShapeDtypeStruct(shape, ki...  13.9 us
  transfers between devices with their start and end apart: 3, of which 0 were waited for; matrix products, arithmetic and copies ran while one was open for 0% of the time, Pallas kernels for 22%

profile of v8, /device:TPU:0, one launch (start us, length us, event | category | flops | bytes accessed | tf_op | source)
XLA Modules:
  0.0 146.5 jit_solution(466462054108198797)
XLA Ops:
  0.7 35.8 %project.1 = (bf16[4,16,16,128]{3,2,1,0:T(8,128)(2,1)}, bf16[8,16,2,16,128]{4,3,2,1,0:T(8,128)(2,1)}, bf16[4,128,512]{2,1,0:T(8,128)(2,1)}, bf16[4,4,2,16,896]{4...) custom-call(bf16[2,128,512]{2,1,0:T(8,128)(2,1)} %bitcast.21, ...), custom_call_target="tpu_custom_call" | custom-call | tf_op jit(solution)/shard_map/project/pallas_call | solution.py:1048
  36.4 0.8 collective-permute-start.1
  37.2 1.5 %collective-permute-start = (bf16[4,16,4608]{2,1,0:T(8,128)(2,1)}, bf16[4,16,4608]{2,1,0:T(8,128)(2,1)S(1)}, u32[]{:S(2)}, u32[]{:S(2)}) collective-permute-start(bf16[4,16,4608]{2,1,0:T(8,128)(2,1)} %get-tuple-element.71.refs_4_), channel_id=1, source_target_pairs={{0,8},{8,0},{16,24},{24,16},{1,9},{9,1},{17,25},{25,17},{2,10},{10... | collective-permute-start | bytes 1769480 | tf_op jit(solution)/shard_map/ppermute | solution.py:1558
  38.7 13.9 %attn_fwd.1 = (bf16[4,256,128]{2,1,0:T(8,128)(2,1)}, f32[4,256,128]{2,1,0:T(8,128)}, f32[8,256]{1,0:T(8,128)}, bf16[4096,256]{1,0:T(8,128)(2,1)}, bf16[256,4096]{1,0:T(8,128)(2,1)}) custom-call(bf16[4,256,128]{2,1,0:T(8,128)(2,1)} %bitcast.30, bf16[4096,128]{1,0:T(8,128)(2,1)} %bitcast.28, s32[8,256]{1,0:T(8,128)} %get-tuple-element.68.seg_q_hbm, ...), custom_call_target="tpu_custom_call" | custom-call | flops 10000000000 | bytes 10000000 | tf_op jit(solution)/shard_map/attn_fwd/pallas_call | solution.py:458
  52.6 0.0 collective-permute-done.1.refs_6_
  52.6 0.0 copy-start.1
  52.6 0.0 collective-permute-done.refs_5_
  52.7 0.0 copy-start.2
  52.7 0.8 copy-done.1
  53.4 0.3 copy-done.2
  53.7 27.0 %middle.1 = (bf16[4,16,16,128]{3,2,1,0:T(8,128)(2,1)}, bf16[256,512]{1,0:T(8,128)(2,1)}, f32[256,512]{1,0:T(8,128)}, f32[256,512]{1,0:T(8,128)}, f32[32,16,128]{...) custom-call(bf16[4,16,16,128]{3,2,1,0:T(8,128)(2,1)} %bitcast.26, ...), custom_call_target="tpu_custom_call" | custom-call | tf_op jit(solution)/shard_map/middle/pallas_call | solution.py:1299
  80.7 1.6 %collective-permute-start.2 = (bf16[4,16,4608]{2,1,0:T(8,128)(2,1)}, bf16[4,16,4608]{2,1,0:T(8,128)(2,1)S(1)}, u32[]{:S(2)}, u32[]{:S(2)}) collective-permute-start(bf16[4,16,4608]{2,1,0:T(8,128)(2,1)} %get-tuple-element.90), channel_id=1, source_target_pairs={{0,24},{8,16},{16,8},{24,0},{1,25},{9,17},{17,9},{25,1},{2,26},{10... | collective-permute-start | bytes 1769480 | tf_op jit(solution)/shard_map/ppermute | solution.py:1563
  82.3 18.5 %attn_bwd.1 = (bf16[4,256,128]{2,1,0:T(8,128)(2,1)}, bf16[4096,128]{1,0:T(8,128)(2,1)}, bf16[256,512]{1,0:T(8,128)(2,1)}, f32[256,512]{1,0:T(8,128)}) custom-call(bf16[4,256,128]{2,1,0:T(8,128)(2,1)} %bitcast.31, bf16[4,256,128]{2,1,0:T(8,128)(2,1)} %bitcast.32, f32[4,256,128]{2,1,0:T(8,128)} %get-tuple-element.75.of_hbm, ...), custom_call_target="tpu_custom_call" | custom-call | flops 10000000000 | bytes 10000000 | tf_op jit(solution)/shard_map/attn_bwd/pallas_call | solution.py:539
  100.8 0.0 collective-permute-done.2.refs_8_
  100.8 0.0 copy-start
  100.8 0.8 copy-done
  101.6 42.5 %finish.1 = (f32[256,512]{1,0:T(8,128)}, f32[16,512]{1,0:T(8,128)}, f32[16,512]{1,0:T(8,128)}, f32[16,512]{1,0:T(8,128)}, f32[16,512]{1,0:T(8,128)}, /*index=5*/...) custom-call(bf16[4,16,16,128]{3,2,1,0:T(8,128)(2,1)} %bitcast.23, bf16[8,16,2,16,128]{4,3,2,1,0:T(8,128)(2,1)} %bitcast.20, ...), custom_call_target="tpu_custom_call" | custom-call | tf_op jit(solution)/shard_map/finish/pallas_call | solution.py:1470
  144.1 2.2 %deliver.1 = (f32[256,512]{1,0:T(8,128)}, f32[16,512]{1,0:T(8,128)}, f32[16,512]{1,0:T(8,128)}, f32[16,512]{1,0:T(8,128)}, f32[16,512]{1,0:T(8,128)}, /*index=5*...) custom-call(f32[256,512]{1,0:T(8,128)} %get-tuple-element.91.refs_0_, ...), custom_call_target="tpu_custom_call" | custom-call | tf_op jit(solution)/shard_map/deliver/pallas_call | solution.py:1528
Async XLA Ops:
  36.4 16.2 %collective-permute-start.1 = (bf16[4,16,4608]{2,1,0:T(8,128)(2,1)}, bf16[4,16,4608]{2,1,0:T(8,128)(2,1)S(1)}, u32[]{:S(2)}, u32[]{:S(2)}) collective-permute-start(bf16[4,16,4608]{2,1,0:T(8,128)(2,1)} %get-tuple-element.71.refs_4_), channel_id=1, source_target_pairs={{0,16},{8,24},{16,0},{24,8},{1,17},{9,25},{17,1},{25,9},{2,18},{10... | collective-permute-start | bytes 1769480 | tf_op jit(solution)/shard_map/ppermute | solution.py:1558
  37.2 15.4 %collective-permute-start = (bf16[4,16,4608]{2,1,0:T(8,128)(2,1)}, bf16[4,16,4608]{2,1,0:T(8,128)(2,1)S(1)}, u32[]{:S(2)}, u32[]{:S(2)}) collective-permute-start(bf16[4,16,4608]{2,1,0:T(8,128)(2,1)} %get-tuple-element.71.refs_4_), channel_id=1, source_target_pairs={{0,8},{8,0},{16,24},{24,16},{1,9},{9,1},{17,25},{25,17},{2,10},{10... | collective-permute-start | bytes 1769480 | tf_op jit(solution)/shard_map/ppermute | solution.py:1558
  52.6 0.8 copy-start.1
  52.7 1.0 copy-start.2
  80.7 20.1 %collective-permute-start.2 = (bf16[4,16,4608]{2,1,0:T(8,128)(2,1)}, bf16[4,16,4608]{2,1,0:T(8,128)(2,1)S(1)}, u32[]{:S(2)}, u32[]{:S(2)}) collective-permute-start(bf16[4,16,4608]{2,1,0:T(8,128)(2,1)} %get-tuple-element.90), channel_id=1, source_target_pairs={{0,24},{8,16},{16,8},{24,0},{1,25},{9,17},{17,9},{25,1},{2,26},{10... | collective-permute-start | bytes 1769480 | tf_op jit(solution)/shard_map/ppermute | solution.py:1563
  100.8 0.8 copy-start
